TPU v7x, 1024 devices: a whole 8x8x8 slice. The times are simulated.
1024 devices in a mesh: outer: 16 (over x, core), inner: 64 (over z, y).
Axes of the slice: x: 8, y: 8, z: 8, core: 2. Of those that a mesh axis runs over, the one named last changes fastest.
Arguments:
- code_tokens: bfloat16 [16384, 16, 768], P(('outer', 'inner')), may hold values from -24 to 24
- text_tokens: bfloat16 [16384, 16, 768], P(('outer', 'inner')), may hold values from -24 to 24
- code_weight: bfloat16 [768, 1024], replicated, may hold values from -0.21875 to 0.21875
- text_weight: bfloat16 [768, 1024], replicated, may hold values from -0.21875 to 0.21875
Outputs:
- pair_loss: float32 [16384], P(('outer', 'inner'))
- grad_code: bfloat16 [16384, 768], P(('outer', 'inner'))
- grad_text: bfloat16 [16384, 768], P(('outer', 'inner'))
All inputs are finite; a program needn't handle non-finite values.
Results may differ from a plain program's by a relative error of at most 0.025.
Values may be sent and summed in bfloat16 or wider, within the bound.
No kernel may reach another device: no remote copies, remote signals or barrier semaphores. Data moves between devices by JAX's collectives and lax.ppermute only.
A program may use at most 32 MiB of HBM per device.

v0:
```python
import jax
import jax.numpy as jnp
from jax import lax
from jax.sharding import PartitionSpec as P

score_scale = 0.1


def back_head(rows, weight):
    return lax.dot_general(
        rows, weight.astype(jnp.float32), (((1,), (1,)), ((), ())), precision=lax.Precision.HIGHEST
    )


def shards(code_tokens, text_tokens, code_weight, text_weight):
    code_rows = jnp.mean(code_tokens.astype(jnp.float32), axis=1).astype(jnp.bfloat16)
    text_rows = jnp.mean(text_tokens.astype(jnp.float32), axis=1).astype(jnp.bfloat16)
    pairs_here = code_rows.shape[0]
    outer_pos = lax.axis_index("outer")
    inner_pos = lax.axis_index("inner")
    n_outer = lax.axis_size("outer")
    n_inner = lax.axis_size("inner")
    own_code = jnp.dot(code_rows, code_weight, preferred_element_type=jnp.float32).astype(
        jnp.bfloat16
    )
    own_text = jnp.dot(text_rows, text_weight, preferred_element_type=jnp.float32).astype(
        jnp.bfloat16
    )
    code_group = lax.all_gather(own_code, "inner", axis=0, tiled=True)
    text_group = lax.all_gather(own_text, "outer", axis=0, tiled=True)
    scores = (
        lax.dot_general(
            code_group, text_group, (((1,), (1,)), ((), ())), preferred_element_type=jnp.float32
        )
        * score_scale
    )
    exps = jnp.exp(scores)
    row_part = jnp.sum(exps, axis=1)
    col_part = jnp.sum(exps, axis=0)
    row_grid = jnp.zeros((n_outer, n_inner * pairs_here), jnp.float32)
    row_grid = lax.dynamic_update_slice(row_grid, row_part[None, :], (outer_pos, jnp.int32(0)))
    col_grid = jnp.zeros((n_outer, n_inner, pairs_here), jnp.float32)
    col_grid = lax.dynamic_update_slice(
        col_grid, col_part.reshape(n_outer, 1, pairs_here), (jnp.int32(0), inner_pos, jnp.int32(0))
    )
    row_grid, col_grid = lax.psum((row_grid, col_grid), ("outer", "inner"))
    row_total = lax.dynamic_index_in_dim(row_grid, outer_pos, 0, keepdims=False)
    col_total = lax.dynamic_index_in_dim(col_grid, inner_pos, 1, keepdims=False).reshape(
        n_outer * pairs_here
    )
    mixing = (0.5 * (exps / row_total[:, None] + exps / col_total[None, :])).astype(jnp.bfloat16)
    own_row_total = lax.dynamic_slice_in_dim(row_total, inner_pos * pairs_here, pairs_here)
    own_col_total = lax.dynamic_slice_in_dim(col_total, outer_pos * pairs_here, pairs_here)
    own_scores = (
        jnp.sum(own_code.astype(jnp.float32) * own_text.astype(jnp.float32), axis=1) * score_scale
    )
    pair_loss = 0.5 * (jnp.log(own_row_total) + jnp.log(own_col_total)) - own_scores
    code_term = jnp.dot(mixing, text_group, preferred_element_type=jnp.float32)
    text_term = lax.dot_general(
        mixing, code_group, (((0,), (0,)), ((), ())), preferred_element_type=jnp.float32
    )
    code_sum = lax.psum_scatter(code_term, "inner", scatter_dimension=0, tiled=True)
    text_sum = lax.psum_scatter(
        text_term.astype(jnp.bfloat16), "outer", scatter_dimension=0, tiled=True
    ).astype(jnp.float32)
    grad_code = back_head(score_scale * (code_sum - own_text.astype(jnp.float32)), code_weight)
    grad_text = back_head(score_scale * (text_sum - own_code.astype(jnp.float32)), text_weight)
    return (pair_loss, grad_code.astype(jnp.bfloat16), grad_text.astype(jnp.bfloat16))


def solution(mesh):
    return jax.shard_map(
        shards,
        mesh=mesh,
        in_specs=(P(("outer", "inner"), None, None), P(("outer", "inner"), None, None), P(), P()),
        out_specs=(P(("outer", "inner")), P(("outer", "inner"), None), P(("outer", "inner"), None)),
        check_vma=False,
    )
```

profile of v0, /device:TPU:2, one launch (start us, length us, event | category | flops | bytes accessed | tf_op | source)
XLA Modules:
  0.0 731.4 jit_solution(15362485428325232192)
XLA Ops:
  7.2 0.0 copy-start
  7.2 0.0 all-gather.2.cloned.1.call-start
  7.2 1.3 convert_reduce_fusion.1
  8.5 2.3 convolution_convert_fusion.2
  10.8 0.0 all-gather.2.cloned.1.call-update
  10.9 0.0 all-reduce.3.cloned.1.call-start
  10.9 0.1 convert_reduce_fusion
  11.1 1.2 fusion.3
  12.3 28.7 %all_gather.7 = bf16[256,1024]{1,0:T(8,128)(2,1)S(1)} all-gather(bf16[16,1024]{1,0:T(8,128)(2,1)S(1)} %get-tuple-element.8), channel_id=1, replica_groups=mesh['outer'=16,'inner'=64] {'outer'}, dimensions={0}, use_global_device_ids=true | all-gather | bytes 557056 | tf_op jit(solution)/shard_map/all_gather | solution.py:30
  41.0 73.8 %all-gather.2.cloned.1.call-done = bf16[1024,1024]{1,0:T(8,128)(2,1)} async-done(((bf16[16,1024]{1,0:T(8,128)(2,1)}), bf16[1024,1024]{1,0:T(8,128)(2,1)}) %all-gather.2.cloned.1.call-update) | async-done | bytes 2097168 | tf_op jit(solution)/shard_map/all_gather | solution.py:29
  114.8 3.3 fusion.18
  118.1 0.1 reshape.19
  118.2 0.1 dynamic_update_slice.6
  118.4 0.1 dynamic_update_slice.7
  118.5 0.5 copy-done.5
  119.0 0.3 copy-done.2
  119.3 0.0 all-reduce.3.cloned.1.call-update
  119.3 0.0 reduce-scatter.5.cloned.1.call-start
  119.4 284.3 %all-reduce.3.cloned.1.call-done = (f32[16,64,16]{2,1,0:T(8,128)}, f32[16,1024]{1,0:T(8,128)}) async-done(((f32[16,64,16]{2,1,0:T(8,128)}, f32[16,1024]{1,0:T(8,128)}), (f32[16,64,16]{2,1,0:T(8,128)}, f32[16,1024]{1,0:T(8,128)})) %all-reduce.3.cloned.1.call-update) | async-done | bytes 131088 | tf_op jit(solution)/shard_map/psum | solution.py:46
  403.7 0.9 dynamic-slice_reduce_fusion
  404.6 0.1 reshape.20
  404.7 0.8 constant_dynamic-slice_fusion
  405.4 3.7 convolution_convert_fusion
  409.1 0.0 reduce-scatter.5.cloned.1.call-update
  409.1 0.0 reduce-scatter.3.cloned.1.call-start
  409.2 2.7 fusion.17
  411.8 0.0 reduce-scatter.3.cloned.1.call-update
  411.9 1.4 fusion.12
  413.3 46.4 %reduce-scatter.5.cloned.1.call-done = bf16[16,1024]{1,0:T(8,128)(2,1)} async-done(((bf16[256,1024]{1,0:T(8,128)(2,1)}), bf16[16,1024]{1,0:T(8,128)(2,1)}) %reduce-scatter.5.cloned.1.call-update) | async-done | bytes 32784 | tf_op jit(solution)/shard_map/reduce_scatter | solution.py:63
  459.8 2.7 convolution_convert_fusion.3
  462.4 259.7 %reduce-scatter.3.cloned.1.call-done = f32[16,1024]{1,0:T(8,128)} async-done(((f32[1024,1024]{1,0:T(8,128)}), f32[16,1024]{1,0:T(8,128)}) %reduce-scatter.3.cloned.1.call-update) | async-done | bytes 65552 | tf_op jit(solution)/shard_map/reduce_scatter | solution.py:62
  722.1 2.8 convolution_convert_fusion.4
  (13 shorter events, 0.1 us)
Async XLA Ops:
  7.2 3.9 copy-start
  7.2 3.7 copy-start.4
  7.2 107.6 %all-gather.2.cloned.1.call-start = ((), (), s32[]{:S(2)}) async-start(), calls=%async_computation.2 | async-start | bytes 2129920 | tf_op jit(solution)/shard_map/all_gather | solution.py:29
  10.9 392.8 %all-reduce.3.cloned.1.call-start = ((), (), s32[]{:S(2)}) async-start(), calls=%async_computation.5 | async-start | bytes 1179648 | tf_op jit(solution)/shard_map/psum | solution.py:46
  118.3 0.6 copy-start.5
  118.5 0.8 copy-start.2
  119.3 340.4 %reduce-scatter.5.cloned.1.call-start = ((), (), s32[]{:S(2)}) async-start(), calls=%async_computation.4 | async-start | bytes 557056 | tf_op jit(solution)/shard_map/reduce_scatter | solution.py:63
  405.4 3.7 copy-start.6
  409.1 313.0 %reduce-scatter.3.cloned.1.call-start = ((), (), s32[]{:S(2)}) async-start(), calls=%async_computation.3 | async-start | bytes 4259840 | tf_op jit(solution)/shard_map/reduce_scatter | solution.py:62
  411.8 47.9 %copy-start.3 = (bf16[16,1024]{1,0:T(8,128)(2,1)S(1)}, bf16[16,1024]{1,0:T(8,128)(2,1)}, u32[]{:S(2)}) copy-start(bf16[16,1024]{1,0:T(8,128)(2,1)} %convolution_convert_fusion.2) | copy-start | bytes 98308
  411.9 310.3 %copy-start.1 = (bf16[768,1024]{1,0:T(8,128)(2,1)S(1)}, bf16[768,1024]{1,0:T(8,128)(2,1)}, u32[]{:S(2)}) copy-start(bf16[768,1024]{1,0:T(8,128)(2,1)} %param.6) | copy-start | bytes 4718596
Sparse Core Ops, SparseCore 0:
  12.3 102.4 all-gather.1
  119.7 283.9 all-reduce.2
  409.2 50.4 reduce-scatter.4
  464.9 257.2 reduce-scatter.2
where the time goes:
time: 732 us; the launch traced here: 731 us
  waiting for transfers between devices  664 us (91%)
  blocking collectives  28.7 us (4%)
  matrix products  18.7 us (3%)
  between operations  13.9 us (2%)
    psum x1, waiting for transfers between devices, shards(): row_grid, col_grid = lax.psum((row_grid, col_grid), ('outer', 'inner'))  284 us
    reduce_scatter x1, waiting for transfers between devices, shards(): lax.psum_scatter(code_term, 'inner', scatter_dimension=0, tiled=True)  260 us
    all_gather x1, waiting for transfers between devices, shards(): code_group = lax.all_gather(own_code, 'inner', axis=0, tiled=True)  73.8 us
    reduce_scatter x1, waiting for transfers between devices, shards(): lax.psum_scatter(text_term.astype(jnp.bfloat16), 'outer', scatter_dimensi...  46.4 us
    all_gather x1, blocking collectives, shards(): text_group = lax.all_gather(own_text, 'outer', axis=0, tiled=True)  28.7 us
  transfers between devices with their start and end apart: 4, of which 4 were waited for; matrix products, arithmetic and copies ran while one was open for 1% of the time, Pallas kernels for 0%

commit v1 on v0

v1 whole, which is shorter than its diff:
```python
import math

import jax
import jax.numpy as jnp
from jax import lax
from jax.sharding import Mesh
from jax.sharding import PartitionSpec as P

score_scale = 0.1
CODE = ("zl", "y")
TEXT = ("x", "zh")


def fan_out(block, axes):
    members = lax.axis_size(axes)
    spread = jnp.broadcast_to(block[None], (members,) + block.shape)
    spread = lax.optimization_barrier(spread)
    return lax.all_to_all(spread, axes, split_axis=0, concat_axis=0, tiled=True)


def shards(code_tokens, text_tokens, code_weight, text_weight):
    f32, bf16 = jnp.float32, jnp.bfloat16
    here, _, depth = code_tokens.shape
    core = lax.axis_index("c")
    code_row = lax.axis_index(("c",) + CODE) * here
    text_row = lax.axis_index(TEXT) * here

    code_rows = jnp.mean(code_tokens.astype(f32), axis=1).astype(bf16)
    text_rows = jnp.mean(text_tokens.astype(f32), axis=1).astype(bf16)
    code_group = fan_out(code_rows, CODE).reshape(-1, depth)
    code_group = lax.all_gather(code_group, "c", axis=0, tiled=True)
    text_group = fan_out(text_rows, TEXT).reshape(-1, depth)

    code_proj = jnp.dot(code_group, code_weight, preferred_element_type=f32).astype(bf16)
    text_proj = jnp.dot(text_group, text_weight, preferred_element_type=f32).astype(bf16)
    nt = (((1,), (1,)), ((), ()))
    scores = lax.dot_general(code_proj, text_proj, nt, preferred_element_type=f32) * score_scale
    exps = jnp.exp(scores)
    row_part = jnp.sum(exps, axis=1)
    col_part = jnp.sum(exps, axis=0)
    row_part = jnp.sum(lax.all_gather(row_part, "c", axis=0), axis=0)
    row_total = jnp.sum(fan_out(row_part, CODE), axis=0)
    col_total = jnp.sum(fan_out(col_part, TEXT), axis=0)

    own = jnp.eye(here, dtype=f32)
    own_scores = jnp.sum(lax.dynamic_slice(scores, (code_row, text_row), (here, here)) * own, axis=1)
    own_row_total = lax.dynamic_slice_in_dim(row_total, code_row, here)
    own_col_total = lax.dynamic_slice_in_dim(col_total, text_row, here)
    pair_loss = 0.5 * (jnp.log(own_row_total) + jnp.log(own_col_total)) - own_scores

    rows = lax.broadcasted_iota(jnp.int32, scores.shape, 0) - code_row
    cols = lax.broadcasted_iota(jnp.int32, scores.shape, 1) - text_row
    paired = (rows == cols) & (rows >= 0) & (rows < here)
    mixing = 0.5 * (exps / row_total[:, None] + exps / col_total[None, :])
    mixing = (mixing - jnp.where(paired, 1.0, 0.0)).astype(bf16)

    text_back = lax.dot_general(text_proj, code_weight, nt, preferred_element_type=f32).astype(bf16)
    code_back = lax.dot_general(code_proj, text_weight, nt, preferred_element_type=f32).astype(bf16)
    code_term = jnp.dot(mixing, text_back, preferred_element_type=f32)
    text_term = lax.dot_general(
        mixing, code_back, (((0,), (0,)), ((), ())), preferred_element_type=f32
    )

    code_term = code_term.reshape(2, -1, here, depth)
    theirs = lax.dynamic_index_in_dim(code_term, 1 - core, 0, keepdims=False).astype(bf16)
    mine = lax.dynamic_index_in_dim(code_term, core, 0, keepdims=False)
    theirs = lax.ppermute(theirs, "c", [(0, 1), (1, 0)])
    code_parts = (mine + theirs.astype(f32)).astype(bf16)
    code_parts = lax.all_to_all(code_parts, CODE, split_axis=0, concat_axis=0, tiled=True)
    text_parts = text_term.reshape(-1, here, depth).astype(bf16)
    text_parts = lax.all_to_all(text_parts, TEXT, split_axis=0, concat_axis=0, tiled=True)
    grad_code = score_scale * jnp.sum(code_parts.astype(f32), axis=0)
    grad_text = score_scale * jnp.sum(text_parts.astype(f32), axis=0)
    return pair_loss, grad_code.astype(bf16), grad_text.astype(bf16)


def solution(mesh):
    n_outer, n_inner = mesh.shape["outer"], mesh.shape["inner"]
    side = math.isqrt(n_inner)
    fine = Mesh(
        mesh.devices.reshape(n_outer // 2, 2, side // 2, 2, side), ("x", "c", "zh", "zl", "y")
    )
    every = P(fine.axis_names)
    return jax.shard_map(
        shards,
        mesh=fine,
        in_specs=(every, every, P(), P()),
        out_specs=(every, every, every),
        check_vma=False,
    )
```

time: 732 us -> 164 us (0.22)
  the two profiles are of different devices: /device:TPU:2 before, /device:TPU:34 now
where the time goes in v1:
time: 164 us; the launch traced here: 163 us
  waiting for transfers between devices  78.6 us (48%)
  starting transfers between devices  56.1 us (34%)
  matrix products  14.5 us (9%)
  other arithmetic  5.18 us (3%)
  blocking collectives  4.14 us (3%)
  local copies, waits for them, and re-layouts  3.89 us (2%)
    all_to_all x4, waiting for transfers between devices, fan_out(): return lax.all_to_all(spread, axes, split_axis=0, concat_axis=0, tiled=True)  46.2 us
    all_to_all x4, starting transfers between devices, fan_out(): return lax.all_to_all(spread, axes, split_axis=0, concat_axis=0, tiled=True)  44 us
    all_to_all x1, waiting for transfers between devices, shards(): lax.all_to_all(text_parts, TEXT, split_axis=0, concat_axis=0, tiled=True)  22.8 us
    all_to_all x1, waiting for transfers between devices, shards(): lax.all_to_all(code_parts, CODE, split_axis=0, concat_axis=0, tiled=True)  7.67 us
    all_to_all x1, starting transfers between devices, shards(): lax.all_to_all(code_parts, CODE, split_axis=0, concat_axis=0, tiled=True)  5.51 us
    all_to_all x1, starting transfers between devices, shards(): lax.all_to_all(text_parts, TEXT, split_axis=0, concat_axis=0, tiled=True)  4.7 us
    dot_general x1, matrix products, shards(): lax.dot_general(mixing, code_back, (((0,), (0,)), ((), ())), preferred_el...  4.66 us
    dot_general x1, matrix products, shards(): code_term = jnp.dot(mixing, text_back, preferred_element_type=f32)  3.57 us
  transfers between devices with their start and end apart: 7, of which 7 were waited for; matrix products, arithmetic and copies ran while one was open for 6% of the time, Pallas kernels for 0%

profile of v1, /device:TPU:34, one launch (start us, length us, event | category | flops | bytes accessed | tf_op | source)
XLA Modules:
  0.0 163.2 jit_solution(13583188797312794273)
XLA Ops:
  0.7 1.3 convert_reduce_fusion.3
  1.9 0.8 broadcast_in_dim.14
  2.7 10.4 %all-to-all-start = ((bf16[16,16,768]{2,1,0:T(8,128)(2,1)}), bf16[16,16,768]{2,1,0:T(8,128)(2,1)S(1)}, u32[]{:S(2)}, u32[]{:S(2)}) async-start(bf16[16,16,768]{2,1,0:T(8,128)(2,1)} %broadcast_in_dim.14), calls=%async_computation | async-start | bytes 786432 | tf_op jit(solution)/shard_map/all_to_all | solution.py:18
  13.3 1.0 broadcast_in_dim.15
  14.2 10.8 %all-to-all-done = bf16[16,16,768]{2,1,0:T(8,128)(2,1)S(1)} async-done(((bf16[16,16,768]{2,1,0:T(8,128)(2,1)}), bf16[16,16,768]{2,1,0:T(8,128)(2,1)S(1)}, u32[]{:S(2)}, u32[]{:S(2)}) %all-to-all-start) | async-done | bytes 393248 | tf_op jit(solution)/shard_map/all_to_all | solution.py:18
  25.1 20.5 %all-to-all-start.1 = ((bf16[32,16,768]{2,1,0:T(8,128)(2,1)}), bf16[32,16,768]{2,1,0:T(8,128)(2,1)S(1)}, u32[]{:S(2)}, u32[]{:S(2)}) async-start(bf16[32,16,768]{2,1,0:T(8,128)(2,1)} %broadcast_in_dim.15), calls=%async_computation.1 | async-start | bytes 1572864 | tf_op jit(solution)/shard_map/all_to_all | solution.py:18
  45.5 2.4 %all_gather.9 = bf16[512,768]{1,0:T(8,128)(2,1)S(1)} all-gather(bf16[256,768]{1,0:T(8,128)(2,1)S(1)} %bitcast.21), channel_id=1, replica_groups=mesh['x'=8,'c'=2,'zh'=4,'zl'=2,'y'=8] {'c'}, dimensions={0}, use_global_device_ids=true | all-gather | bytes 1179648 | tf_op jit(solution)/shard_map/all_gather | solution.py:31
  47.9 2.0 %convolution_convert_fusion.1 = bf16[512,1024]{1,0:T(8,128)(2,1)} fusion(bf16[512,768]{1,0:T(8,128)(2,1)S(1)} %all_gather.9, bf16[768,1024]{1,0:T(8,128)(2,1)S(1)} %copy-done), kind=kOutput, calls=%fused_computation.2 | convolution fusion | flops 805830656 | bytes 3407872 | tf_op jit(solution)/shard_map/dot_general | solution.py:34
  49.9 18.3 %all-to-all-done.1 = bf16[32,16,768]{2,1,0:T(8,128)(2,1)S(1)} async-done(((bf16[32,16,768]{2,1,0:T(8,128)(2,1)}), bf16[32,16,768]{2,1,0:T(8,128)(2,1)S(1)}, u32[]{:S(2)}, u32[]{:S(2)}) %all-to-all-start.1) | async-done | bytes 786464 | tf_op jit(solution)/shard_map/all_to_all | solution.py:18
  68.2 2.5 %convolution_convert_fusion = bf16[512,1024]{1,0:T(8,128)(2,1)S(1)} fusion(bf16[512,768]{1,0:T(8,128)(2,1)S(1)} %bitcast.24, bf16[768,1024]{1,0:T(8,128)(2,1)} %param.7), kind=kOutput, calls=%fused_computation.1 | convolution fusion | flops 805830656 | bytes 3407872 | tf_op jit(solution)/shard_map/dot_general | solution.py:35
  70.7 1.8 %exponential_reduce_fusion.1 = (f32[512]{0:T(512)S(1)}, f32[512]{0:T(512)S(1)}, f32[512,512]{0,1:T(8,128)}) fusion(bf16[512,1024]{1,0:T(8,128)(2,1)S(1)} %copy-done.4, bf16[512,1024]{1,0:T(8,128)(2,1)S(1)} %convolution_convert_fusion), kind=kOutput, calls=%fused_computation.10 | convolution fusion | flops 537656320 | bytes 3149824 | tf_op jit(solution)/shard_map/dot_general | solution.py:37
  72.5 1.8 %all-gather.1 = f32[2,1,512]{2,1,0:T(1,128)S(1)} all-gather(f32[1,1,512]{2,1,0:T(1,128)S(1)} %bitcast.25), channel_id=2, replica_groups=mesh['x'=8,'c'=2,'zh'=4,'zl'=2,'y'=8] {'c'}, dimensions={0}, use_global_device_ids=true | all-gather | bytes 6144 | tf_op jit(solution)/shard_map/all_gather | solution.py:41
  74.3 0.6 all_to_all.26
  74.9 6.8 %all-to-all-start.2 = ((f32[16,1,512]{2,1,0:T(1,128)}), f32[16,1,512]{2,1,0:T(1,128)S(1)}, u32[]{:S(2)}, u32[]{:S(2)}) async-start(f32[16,1,512]{2,1,0:T(1,128)} %all_to_all.26), calls=%async_computation.2 | async-start | bytes 65536 | tf_op jit(solution)/shard_map/all_to_all | solution.py:18
  81.8 0.7 all_to_all.28
  82.4 5.8 %all-to-all-done.2 = f32[16,1,512]{2,1,0:T(1,128)S(1)} async-done(((f32[16,1,512]{2,1,0:T(1,128)}), f32[16,1,512]{2,1,0:T(1,128)S(1)}, u32[]{:S(2)}, u32[]{:S(2)}) %all-to-all-start.2) | async-done | bytes 32800 | tf_op jit(solution)/shard_map/all_to_all | solution.py:18
  88.2 6.3 %all-to-all-start.3 = ((f32[32,1,512]{2,1,0:T(1,128)}), f32[32,1,512]{2,1,0:T(1,128)S(1)}, u32[]{:S(2)}, u32[]{:S(2)}) async-start(f32[32,1,512]{2,1,0:T(1,128)} %all_to_all.28), calls=%async_computation.3 | async-start | bytes 131072 | tf_op jit(solution)/shard_map/all_to_all | solution.py:18
  94.6 11.3 %all-to-all-done.3 = f32[32,1,512]{2,1,0:T(1,128)S(1)} async-done(((f32[32,1,512]{2,1,0:T(1,128)}), f32[32,1,512]{2,1,0:T(1,128)S(1)}, u32[]{:S(2)}, u32[]{:S(2)}) %all-to-all-start.3) | async-done | bytes 65568 | tf_op jit(solution)/shard_map/all_to_all | solution.py:18
  106.0 3.6 %fusion = f32[512,768]{1,0:T(8,128)S(1)} fusion(bf16[512,1024]{1,0:T(8,128)(2,1)} %copy-done.5, bf16[768,1024]{1,0:T(8,128)(2,1)S(1)} %copy-done, f32[512,512]{0,1:T(8,128)} %get-tuple-element.5, s32[512]{0:T(512)S(1)} %get-tuple-element.9, f32[512]{0:T(512)S(1)} %reduce_sum.96, f32[512]{0:T(512)S(1)} %reduce_sum.94, s32[512]{0:T(512)S(1)} %get-tuple-element.8, ...), kind=kOutput, calls=%fused_computation.7 | convolution fusion | flops 1210974208 | bytes 5252096 | tf_op jit(solution)/shard_map/dot_general | solution.py:59
  109.6 0.8 fusion.2
  110.4 1.9 %collective-permute-start = (bf16[16,16,768]{2,1,0:T(8,128)(2,1)}, bf16[16,16,768]{2,1,0:T(8,128)(2,1)S(1)}, u32[]{:S(2)}, u32[]{:S(2)}) collective-permute-start(bf16[16,16,768]{2,1,0:T(8,128)(2,1)} %fusion.2), channel_id=1, source_target_pairs={{0,64},{64,0},{1,65},{65,1},{2,66},{66,2},{3,67},{67,3},{4,68},{68... | collective-permute-start | bytes 1179656 | tf_op jit(solution)/shard_map/ppermute | solution.py:67
  112.4 1.9 %collective-permute-done = bf16[16,16,768]{2,1,0:T(8,128)(2,1)S(1)} collective-permute-done((bf16[16,16,768]{2,1,0:T(8,128)(2,1)}, bf16[16,16,768]{2,1,0:T(8,128)(2,1)S(1)}, u32[]{:S(2)}, u32[]{:S(2)}) %collective-permute-start) | collective-permute-done | bytes 393248 | tf_op jit(solution)/shard_map/ppermute | solution.py:67
  114.3 0.8 fusion.1
  115.1 5.5 %all-to-all-start.4 = ((bf16[16,16,768]{2,1,0:T(8,128)(2,1)}), bf16[16,16,768]{2,1,0:T(8,128)(2,1)S(1)}, u32[]{:S(2)}, u32[]{:S(2)}) async-start(bf16[16,16,768]{2,1,0:T(8,128)(2,1)} %fusion.1), calls=%async_computation.4 | async-start | bytes 786432 | tf_op jit(solution)/shard_map/all_to_all | solution.py:69
  120.6 4.7 %convolution_convert_fusion.2 = bf16[512,768]{1,0:T(8,128)(2,1)} fusion(bf16[512,1024]{1,0:T(8,128)(2,1)} %convolution_convert_fusion.1, bf16[768,1024]{1,0:T(8,128)(2,1)} %param.7, f32[512,512]{0,1:T(8,128)} %get-tuple-element.5, s32[512]{0:T(512)S(1)} %get-tuple-element.9, f32[512]{0:T(512)S(1)} %reduce_sum.96, f32[512]{0:T(512)S(1)} %reduce_sum.94, ...), kind=kOutput, calls=%fused_computation.3 | convolution fusion | flops 1211367424 | bytes 4465664 | tf_op jit(solution)/shard_map/dot_general | solution.py:60
  125.3 7.7 %all-to-all-done.4 = bf16[16,16,768]{2,1,0:T(8,128)(2,1)S(1)} async-done(((bf16[16,16,768]{2,1,0:T(8,128)(2,1)}), bf16[16,16,768]{2,1,0:T(8,128)(2,1)S(1)}, u32[]{:S(2)}, u32[]{:S(2)}) %all-to-all-start.4) | async-done | bytes 393248 | tf_op jit(solution)/shard_map/all_to_all | solution.py:69
  132.9 4.7 %all-to-all-start.5 = ((bf16[32,16,768]{2,1,0:T(8,128)(2,1)}), bf16[32,16,768]{2,1,0:T(8,128)(2,1)S(1)}, u32[]{:S(2)}, u32[]{:S(2)}) async-start(bf16[32,16,768]{2,1,0:T(8,128)(2,1)} %bitcast.6), calls=%async_computation.5 | async-start | bytes 1572864 | tf_op jit(solution)/shard_map/all_to_all | solution.py:71
  137.6 0.8 select_reduce_fusion
  138.4 0.6 multiply_subtract_fusion
  139.1 0.6 multiply_convert_fusion.1
  139.7 22.8 %all-to-all-done.5 = bf16[32,16,768]{2,1,0:T(8,128)(2,1)S(1)} async-done(((bf16[32,16,768]{2,1,0:T(8,128)(2,1)}), bf16[32,16,768]{2,1,0:T(8,128)(2,1)S(1)}, u32[]{:S(2)}, u32[]{:S(2)}) %all-to-all-start.5) | async-done | bytes 786464 | tf_op jit(solution)/shard_map/all_to_all | solution.py:71
  162.6 0.6 multiply_convert_fusion
  (24 shorter events, 0.5 us)
Async XLA Ops:
  0.6 47.3 %copy-start = (bf16[768,1024]{1,0:T(8,128)(2,1)S(1)}, bf16[768,1024]{1,0:T(8,128)(2,1)}, u32[]{:S(2)}) copy-start(bf16[768,1024]{1,0:T(8,128)(2,1)} %param.6) | copy-start | bytes 4718596
  0.6 12.5 %copy-start.1 = (bf16[16,16,768]{2,1,0:T(8,128)(2,1)S(1)}, bf16[16,16,768]{2,1,0:T(8,128)(2,1)}, u32[]{:S(2)}) copy-start(bf16[16,16,768]{2,1,0:T(8,128)(2,1)} %param.5) | copy-start | bytes 1179652
  2.7 22.3 %all-to-all-start = ((bf16[16,16,768]{2,1,0:T(8,128)(2,1)}), bf16[16,16,768]{2,1,0:T(8,128)(2,1)S(1)}, u32[]{:S(2)}, u32[]{:S(2)}) async-start(bf16[16,16,768]{2,1,0:T(8,128)(2,1)} %broadcast_in_dim.14), calls=%async_computation | async-start | bytes 786432 | tf_op jit(solution)/shard_map/all_to_all | solution.py:18
  25.1 43.2 %all-to-all-start.1 = ((bf16[32,16,768]{2,1,0:T(8,128)(2,1)}), bf16[32,16,768]{2,1,0:T(8,128)(2,1)S(1)}, u32[]{:S(2)}, u32[]{:S(2)}) async-start(bf16[32,16,768]{2,1,0:T(8,128)(2,1)} %broadcast_in_dim.15), calls=%async_computation.1 | async-start | bytes 1572864 | tf_op jit(solution)/shard_map/all_to_all | solution.py:18
  68.2 2.5 %copy-start.4 = (bf16[512,1024]{1,0:T(8,128)(2,1)S(1)}, bf16[512,1024]{1,0:T(8,128)(2,1)}, u32[]{:S(2)}) copy-start(bf16[512,1024]{1,0:T(8,128)(2,1)} %convolution_convert_fusion.1) | copy-start | bytes 3145732
  70.7 1.8 %copy-start.5 = (bf16[512,1024]{1,0:T(8,128)(2,1)}, bf16[512,1024]{1,0:T(8,128)(2,1)S(1)}, u32[]{:S(2)}) copy-start(bf16[512,1024]{1,0:T(8,128)(2,1)S(1)} %convolution_convert_fusion) | copy-start | bytes 3145732
  74.9 13.3 %all-to-all-start.2 = ((f32[16,1,512]{2,1,0:T(1,128)}), f32[16,1,512]{2,1,0:T(1,128)S(1)}, u32[]{:S(2)}, u32[]{:S(2)}) async-start(f32[16,1,512]{2,1,0:T(1,128)} %all_to_all.26), calls=%async_computation.2 | async-start | bytes 65536 | tf_op jit(solution)/shard_map/all_to_all | solution.py:18
  88.2 17.8 %all-to-all-start.3 = ((f32[32,1,512]{2,1,0:T(1,128)}), f32[32,1,512]{2,1,0:T(1,128)S(1)}, u32[]{:S(2)}, u32[]{:S(2)}) async-start(f32[32,1,512]{2,1,0:T(1,128)} %all_to_all.28), calls=%async_computation.3 | async-start | bytes 131072 | tf_op jit(solution)/shard_map/all_to_all | solution.py:18
  94.5 15.1 %copy-start.2 = (pred[512]{0:T(512)(128)(4,1)}, pred[512]{0:T(512)(128)(4,1)S(1)}, u32[]{:S(2)}) copy-start(pred[512]{0:T(512)(128)(4,1)S(1)} %get-tuple-element.6) | copy-start | bytes 1540
  94.5 15.1 %copy-start.3 = (pred[512]{0:T(512)(128)(4,1)}, pred[512]{0:T(512)(128)(4,1)S(1)}, u32[]{:S(2)}) copy-start(pred[512]{0:T(512)(128)(4,1)S(1)} %get-tuple-element.7) | copy-start | bytes 1540
  110.4 3.8 %collective-permute-start = (bf16[16,16,768]{2,1,0:T(8,128)(2,1)}, bf16[16,16,768]{2,1,0:T(8,128)(2,1)S(1)}, u32[]{:S(2)}, u32[]{:S(2)}) collective-permute-start(bf16[16,16,768]{2,1,0:T(8,128)(2,1)} %fusion.2), channel_id=1, source_target_pairs={{0,64},{64,0},{1,65},{65,1},{2,66},{66,2},{3,67},{67,3},{4,68},{68... | collective-permute-start | bytes 1179656 | tf_op jit(solution)/shard_map/ppermute | solution.py:67
  115.1 17.8 %all-to-all-start.4 = ((bf16[16,16,768]{2,1,0:T(8,128)(2,1)}), bf16[16,16,768]{2,1,0:T(8,128)(2,1)S(1)}, u32[]{:S(2)}, u32[]{:S(2)}) async-start(bf16[16,16,768]{2,1,0:T(8,128)(2,1)} %fusion.1), calls=%async_computation.4 | async-start | bytes 786432 | tf_op jit(solution)/shard_map/all_to_all | solution.py:69
  132.9 29.6 %all-to-all-start.5 = ((bf16[32,16,768]{2,1,0:T(8,128)(2,1)}), bf16[32,16,768]{2,1,0:T(8,128)(2,1)S(1)}, u32[]{:S(2)}, u32[]{:S(2)}) async-start(bf16[32,16,768]{2,1,0:T(8,128)(2,1)} %bitcast.6), calls=%async_computation.5 | async-start | bytes 1572864 | tf_op jit(solution)/shard_map/all_to_all | solution.py:71

commit v2 on v1

v2 whole, which is shorter than its diff:
```python
import math

import jax
import jax.numpy as jnp
from jax import lax
from jax.sharding import Mesh
from jax.sharding import PartitionSpec as P

score_scale = 0.1
CODE = ("y", "c", "zl")
TEXT = ("x", "zh")


def fan_out(block, axes):
    members = lax.axis_size(axes)
    spread = jnp.broadcast_to(block[None], (members,) + block.shape)
    spread = lax.optimization_barrier(spread)
    return lax.all_to_all(spread, axes, split_axis=0, concat_axis=0, tiled=True)


def gather_code(block):
    pair = lax.all_gather(block, "zl", axis=0, tiled=True)
    return lax.all_gather(pair, ("y", "c"), axis=0, tiled=True)


def add_half(parts, axis, name):
    me = lax.axis_index(name)
    mine = lax.dynamic_index_in_dim(parts, me, axis, keepdims=False)
    theirs = lax.dynamic_index_in_dim(parts, 1 - me, axis, keepdims=False).astype(jnp.bfloat16)
    theirs = lax.ppermute(theirs, name, [(0, 1), (1, 0)])
    return mine.astype(jnp.float32) + theirs.astype(jnp.float32)


def shards(code_tokens, text_tokens, code_weight, text_weight):
    f32, bf16 = jnp.float32, jnp.bfloat16
    here, _, depth = code_tokens.shape
    code_row = lax.axis_index(CODE) * here
    text_row = lax.axis_index(TEXT) * here

    text_rows = jnp.mean(text_tokens.astype(f32), axis=1).astype(bf16)
    text_group = fan_out(text_rows, TEXT).reshape(-1, depth)
    code_rows = jnp.mean(code_tokens.astype(f32), axis=1).astype(bf16)
    code_group = gather_code(code_rows)

    code_proj = jnp.dot(code_group, code_weight, preferred_element_type=f32).astype(bf16)
    text_proj = jnp.dot(text_group, text_weight, preferred_element_type=f32).astype(bf16)
    nt = (((1,), (1,)), ((), ()))
    scores = lax.dot_general(code_proj, text_proj, nt, preferred_element_type=f32) * score_scale
    exps = jnp.exp(scores)
    row_part = jnp.sum(exps, axis=1)
    col_part = jnp.sum(exps, axis=0)
    col_total = jnp.sum(fan_out(col_part, TEXT), axis=0)
    row_total = jnp.sum(gather_code(row_part[None]), axis=0)
    text_back = lax.dot_general(text_proj, code_weight, nt, preferred_element_type=f32).astype(bf16)
    code_back = lax.dot_general(code_proj, text_weight, nt, preferred_element_type=f32).astype(bf16)
    text_back, code_back = lax.optimization_barrier((text_back, code_back))

    own = jnp.eye(here, dtype=f32)
    own_scores = jnp.sum(lax.dynamic_slice(scores, (code_row, text_row), (here, here)) * own, axis=1)
    own_row_total = lax.dynamic_slice_in_dim(row_total, code_row, here)
    own_col_total = lax.dynamic_slice_in_dim(col_total, text_row, here)
    pair_loss = 0.5 * (jnp.log(own_row_total) + jnp.log(own_col_total)) - own_scores

    rows = lax.broadcasted_iota(jnp.int32, scores.shape, 0) - code_row
    cols = lax.broadcasted_iota(jnp.int32, scores.shape, 1) - text_row
    paired = (rows == cols) & (rows >= 0) & (rows < here)
    mixing = 0.5 * (exps / row_total[:, None] + exps / col_total[None, :])
    mixing = (mixing - jnp.where(paired, 1.0, 0.0)).astype(bf16)

    text_term = lax.dot_general(
        mixing, code_back, (((0,), (0,)), ((), ())), preferred_element_type=f32
    )
    text_parts = text_term.reshape(-1, here, depth).astype(bf16)
    mixing, text_parts = lax.optimization_barrier((mixing, text_parts))
    text_parts = lax.all_to_all(text_parts, TEXT, split_axis=0, concat_axis=0, tiled=True)
    code_term = jnp.dot(mixing, text_back, preferred_element_type=f32)
    code_parts = code_term.reshape(-1, 2, 2, here, depth)
    code_parts = add_half(code_parts, 1, "c")
    code_parts = add_half(code_parts, 1, "zl").astype(bf16)
    code_parts, text_parts = lax.optimization_barrier((code_parts, text_parts))
    code_parts = lax.all_to_all(code_parts, "y", split_axis=0, concat_axis=0, tiled=True)
    grad_code = score_scale * jnp.sum(code_parts.astype(f32), axis=0)
    grad_text = score_scale * jnp.sum(text_parts.astype(f32), axis=0)
    return pair_loss, grad_code.astype(bf16), grad_text.astype(bf16)


def solution(mesh):
    n_outer, n_inner = mesh.shape["outer"], mesh.shape["inner"]
    side = math.isqrt(n_inner)
    fine = Mesh(
        mesh.devices.reshape(n_outer // 2, 2, side // 2, 2, side), ("x", "c", "zh", "zl", "y")
    )
    every = P(fine.axis_names)
    return jax.shard_map(
        shards,
        mesh=fine,
        in_specs=(every, every, P(), P()),
        out_specs=(every, every, every),
        check_vma=False,
    )
```

time: 164 us -> 165 us (level)
  the two profiles are of different devices: /device:TPU:34 before, /device:TPU:4 now
where the time goes in v2:
time: 165 us; the launch traced here: 164 us
  blocking collectives  58.7 us (36%)
  starting transfers between devices  54.8 us (33%)
  waiting for transfers between devices  23.6 us (14%)
  matrix products  14.3 us (9%)
  other arithmetic  6.75 us (4%)
  local copies, waits for them, and re-layouts  4.75 us (3%)
    all_gather x2, blocking collectives, gather_code(): return lax.all_gather(pair, ('y', 'c'), axis=0, tiled=True)  35.3 us
    all_to_all x2, starting transfers between devices, fan_out(): return lax.all_to_all(spread, axes, split_axis=0, concat_axis=0, tiled=True)  33 us
    all_gather x2, blocking collectives, gather_code(): pair = lax.all_gather(block, 'zl', axis=0, tiled=True)  23.4 us
    ppermute x2, waiting for transfers between devices, add_half(): theirs = lax.ppermute(theirs, name, [(0, 1), (1, 0)])  14.6 us
    all_to_all x1, starting transfers between devices, shards(): lax.all_to_all(text_parts, TEXT, split_axis=0, concat_axis=0, tiled=True)  12.2 us
    all_to_all x1, waiting for transfers between devices, shards(): lax.all_to_all(code_parts, 'y', split_axis=0, concat_axis=0, tiled=True)  9.04 us
    all_to_all x1, starting transfers between devices, shards(): lax.all_to_all(code_parts, 'y', split_axis=0, concat_axis=0, tiled=True)  4.85 us
    ppermute x2, starting transfers between devices, add_half(): theirs = lax.ppermute(theirs, name, [(0, 1), (1, 0)])  4.75 us
  transfers between devices with their start and end apart: 6, of which 3 were waited for; matrix products, arithmetic and copies ran while one was open for 9% of the time, Pallas kernels for 0%

profile of v2, /device:TPU:4, one launch (start us, length us, event | category | flops | bytes accessed | tf_op | source)
XLA Modules:
  0.0 163.7 jit_solution(2898846107617791477)
XLA Ops:
  0.7 1.3 convert_reduce_fusion.1
  1.9 1.0 broadcast_in_dim.12
  2.9 21.3 %all-to-all-start = ((bf16[32,16,768]{2,1,0:T(8,128)(2,1)}), bf16[32,16,768]{2,1,0:T(8,128)(2,1)S(1)}, u32[]{:S(2)}, u32[]{:S(2)}) async-start(bf16[32,16,768]{2,1,0:T(8,128)(2,1)} %broadcast_in_dim.12), calls=%async_computation | async-start | bytes 1572864 | tf_op jit(solution)/shard_map/all_to_all | solution.py:18
  24.4 19.1 %all_gather.12 = bf16[32,768]{1,0:T(8,128)(2,1)S(1)} all-gather(bf16[16,768]{1,0:T(8,128)(2,1)S(1)} %multiply_convert_fusion.3), channel_id=1, replica_groups=mesh['x'=8,'c'=2,'zh'=4,'zl'=2,'y'=8] {'zl'}, dimensions={0}, use_global_device_ids=true | all-gather | bytes 73728 | tf_op jit(solution)/shard_map/all_gather | solution.py:22
  43.5 20.5 %all_gather.13 = bf16[512,768]{1,0:T(8,128)(2,1)S(1)} all-gather(bf16[32,768]{1,0:T(8,128)(2,1)S(1)} %all_gather.12), channel_id=1, replica_groups=mesh['x'=8,'c'=2,'zh'=4,'zl'=2,'y'=8] {'y','c'}, dimensions={0}, use_global_device_ids=true | all-gather | bytes 835584 | tf_op jit(solution)/shard_map/all_gather | solution.py:23
  64.1 2.4 %convolution_convert_fusion.1 = bf16[512,1024]{1,0:T(8,128)(2,1)S(1)} fusion(bf16[512,768]{1,0:T(8,128)(2,1)S(1)} %all_gather.13, bf16[768,1024]{1,0:T(8,128)(2,1)} %param.6), kind=kOutput, calls=%fused_computation.2 | convolution fusion | flops 805830656 | bytes 3407872 | tf_op jit(solution)/shard_map/dot_general | solution.py:45
  66.5 1.0 copy-done.5
  67.5 1.9 %convolution_convert_fusion.3 = bf16[512,768]{1,0:T(8,128)(2,1)} fusion(bf16[512,1024]{1,0:T(8,128)(2,1)S(1)} %convolution_convert_fusion.1, bf16[768,1024]{1,0:T(8,128)(2,1)S(1)} %copy-done), kind=kOutput, calls=%fused_computation.4 | convolution fusion | flops 805699584 | bytes 3407872 | tf_op jit(solution)/shard_map/dot_general | solution.py:55
  69.4 1.0 convolution_convert_fusion
  70.6 0.9 exponential_reduce_fusion.1
  71.7 0.7 all_to_all.16
  72.4 11.6 %all-to-all-start.1 = ((f32[32,1,512]{2,1,0:T(1,128)}), f32[32,1,512]{2,1,0:T(1,128)S(1)}, u32[]{:S(2)}, u32[]{:S(2)}) async-start(f32[32,1,512]{2,1,0:T(1,128)} %all_to_all.16), calls=%async_computation.1 | async-start | bytes 131072 | tf_op jit(solution)/shard_map/all_to_all | solution.py:18
  84.0 3.6 %convolution_convert_fusion.4 = bf16[512,768]{1,0:T(8,128)(2,1)} fusion(bf16[512,1024]{1,0:T(8,128)(2,1)} %copy-done.4, bf16[768,1024]{1,0:T(8,128)(2,1)} %param.6), kind=kOutput, calls=%fused_computation.5 | convolution fusion | flops 805699584 | bytes 3407872 | tf_op jit(solution)/shard_map/dot_general | solution.py:54
  87.7 4.3 %all-gather.1 = f32[2,1,512]{2,1,0:T(1,128)S(1)} all-gather(f32[1,1,512]{2,1,0:T(1,128)S(1)} %bitcast.33), channel_id=2, replica_groups=mesh['x'=8,'c'=2,'zh'=4,'zl'=2,'y'=8] {'zl'}, dimensions={0}, use_global_device_ids=true | all-gather | bytes 6144 | tf_op jit(solution)/shard_map/all_gather | solution.py:22
  92.0 14.7 %all-gather.2 = f32[16,2,512]{2,1,0:T(2,128)S(1)} all-gather(f32[1,2,512]{2,1,0:T(2,128)S(1)} %copy.7), channel_id=1, replica_groups=mesh['x'=8,'c'=2,'zh'=4,'zl'=2,'y'=8] {'y','c'}, dimensions={0}, use_global_device_ids=true | all-gather | bytes 69632 | tf_op jit(solution)/shard_map/all_gather | solution.py:23
  107.4 0.8 copy-done.1
  108.2 2.6 %convolution_convert_fusion.2 = bf16[512,768]{1,0:T(8,128)(2,1)} fusion(bf16[512,512]{0,1:T(8,128)(2,1)S(1)} %subtract_convert_fusion, bf16[512,768]{1,0:T(8,128)(2,1)} %convolution_convert_fusion.3), kind=kOutput, calls=%fused_computation.3 | convolution fusion | flops 403046400 | bytes 2097152 | tf_op jit(solution)/shard_map/dot_general | solution.py:70
  110.8 12.2 %all-to-all-start.2 = ((bf16[32,16,768]{2,1,0:T(8,128)(2,1)}), bf16[32,16,768]{2,1,0:T(8,128)(2,1)}, u32[]{:S(2)}, u32[]{:S(2)}) async-start(bf16[32,16,768]{2,1,0:T(8,128)(2,1)} %bitcast.3), calls=%async_computation.2 | async-start | bytes 1572864 | tf_op jit(solution)/shard_map/all_to_all | solution.py:75
  123.1 1.9 %fusion.5 = f32[512,768]{1,0:T(8,128)S(1)} fusion(bf16[512,512]{0,1:T(8,128)(2,1)} %copy-done.1, bf16[512,768]{1,0:T(8,128)(2,1)} %convolution_convert_fusion.4), kind=kOutput, calls=%fused_computation.31 | convolution fusion | flops 402653184 | bytes 2883584 | tf_op jit(solution)/shard_map/dot_general | solution.py:76
  125.0 0.8 fusion
  125.8 1.9 %collective-permute-start = (bf16[8,2,16,768]{3,2,1,0:T(8,128)(2,1)}, bf16[8,2,16,768]{3,2,1,0:T(8,128)(2,1)S(1)}, u32[]{:S(2)}, u32[]{:S(2)}) collective-permute-start(bf16[8,2,16,768]{3,2,1,0:T(8,128)(2,1)} %fusion), channel_id=1, source_target_pairs={{0,64},{64,0},{1,65},{65,1},{2,66},{66,2},{3,67},{67,3},{4,68},{68... | collective-permute-start | bytes 1179656 | tf_op jit(solution)/shard_map/ppermute | solution.py:30
  127.7 0.8 select_reduce_fusion
  128.5 1.1 collective-permute-done
  129.7 2.8 %collective-permute-start.1 = (bf16[8,16,768]{2,1,0:T(8,128)(2,1)S(1)}, bf16[8,16,768]{2,1,0:T(8,128)(2,1)S(1)}, u32[]{:S(2)}, u32[]{:S(2)}) collective-permute-start(bf16[8,16,768]{2,1,0:T(8,128)(2,1)S(1)} %fusion.2), channel_id=1, source_target_pairs={{0,8},{8,0},{1,9},{9,1},{2,10},{10,2},{3,11},{11,3},{4,12},{12,4},... | collective-permute-start | bytes 589832 | tf_op jit(solution)/shard_map/ppermute | solution.py:30
  132.6 0.6 multiply_subtract_fusion
  133.2 13.5 %collective-permute-done.1 = bf16[8,16,768]{2,1,0:T(8,128)(2,1)S(1)} collective-permute-done((bf16[8,16,768]{2,1,0:T(8,128)(2,1)S(1)}, bf16[8,16,768]{2,1,0:T(8,128)(2,1)S(1)}, u32[]{:S(2)}, u32[]{:S(2)}) %collective-permute-start.1) | collective-permute-done | bytes 196640 | tf_op jit(solution)/shard_map/ppermute | solution.py:30
  146.6 0.7 fusion.1
  147.3 4.8 %all-to-all-start.3 = ((bf16[8,16,768]{2,1,0:T(8,128)(2,1)}), bf16[8,16,768]{2,1,0:T(8,128)(2,1)S(1)}, u32[]{:S(2)}, u32[]{:S(2)}) async-start(bf16[8,16,768]{2,1,0:T(8,128)(2,1)} %fusion.1), calls=%async_computation.3 | async-start | bytes 393216 | tf_op jit(solution)/shard_map/all_to_all | solution.py:81
  152.2 1.3 convert_reduce_fusion
  153.4 0.6 multiply_convert_fusion
  154.1 9.0 %all-to-all-done.3 = bf16[8,16,768]{2,1,0:T(8,128)(2,1)S(1)} async-done(((bf16[8,16,768]{2,1,0:T(8,128)(2,1)}), bf16[8,16,768]{2,1,0:T(8,128)(2,1)S(1)}, u32[]{:S(2)}, u32[]{:S(2)}) %all-to-all-start.3) | async-done | bytes 196640 | tf_op jit(solution)/shard_map/all_to_all | solution.py:81
  163.1 0.6 multiply_convert_fusion.1
  (28 shorter events, 1.4 us)
Async XLA Ops:
  0.6 66.8 %copy-start = (bf16[768,1024]{1,0:T(8,128)(2,1)S(1)}, bf16[768,1024]{1,0:T(8,128)(2,1)}, u32[]{:S(2)}) copy-start(bf16[768,1024]{1,0:T(8,128)(2,1)} %param.7) | copy-start | bytes 4718596
  0.6 23.6 %copy-start.3 = (bf16[16,16,768]{2,1,0:T(8,128)(2,1)S(1)}, bf16[16,16,768]{2,1,0:T(8,128)(2,1)}, u32[]{:S(2)}) copy-start(bf16[16,16,768]{2,1,0:T(8,128)(2,1)} %param.4) | copy-start | bytes 1179652
  2.9 66.5 %all-to-all-start = ((bf16[32,16,768]{2,1,0:T(8,128)(2,1)}), bf16[32,16,768]{2,1,0:T(8,128)(2,1)S(1)}, u32[]{:S(2)}, u32[]{:S(2)}) async-start(bf16[32,16,768]{2,1,0:T(8,128)(2,1)} %broadcast_in_dim.12), calls=%async_computation | async-start | bytes 1572864 | tf_op jit(solution)/shard_map/all_to_all | solution.py:18
  66.5 1.0 copy-start.5
  69.4 1.2 copy-start.6
  70.6 1.0 copy-start.4
  71.7 35.2 %copy-start.2 = (f32[512,512]{0,1:T(8,128)}, f32[512,512]{0,1:T(8,128)S(1)}, u32[]{:S(2)}) copy-start(f32[512,512]{0,1:T(8,128)S(1)} %get-tuple-element.17) | copy-start | bytes 3145732
  72.4 34.4 %all-to-all-start.1 = ((f32[32,1,512]{2,1,0:T(1,128)}), f32[32,1,512]{2,1,0:T(1,128)S(1)}, u32[]{:S(2)}, u32[]{:S(2)}) async-start(f32[32,1,512]{2,1,0:T(1,128)} %all_to_all.16), calls=%async_computation.1 | async-start | bytes 131072 | tf_op jit(solution)/shard_map/all_to_all | solution.py:18
  107.4 0.8 copy-start.1
  110.8 36.5 %all-to-all-start.2 = ((bf16[32,16,768]{2,1,0:T(8,128)(2,1)}), bf16[32,16,768]{2,1,0:T(8,128)(2,1)}, u32[]{:S(2)}, u32[]{:S(2)}) async-start(bf16[32,16,768]{2,1,0:T(8,128)(2,1)} %bitcast.3), calls=%async_computation.2 | async-start | bytes 1572864 | tf_op jit(solution)/shard_map/all_to_all | solution.py:75
  125.8 3.8 %collective-permute-start = (bf16[8,2,16,768]{3,2,1,0:T(8,128)(2,1)}, bf16[8,2,16,768]{3,2,1,0:T(8,128)(2,1)S(1)}, u32[]{:S(2)}, u32[]{:S(2)}) collective-permute-start(bf16[8,2,16,768]{3,2,1,0:T(8,128)(2,1)} %fusion), channel_id=1, source_target_pairs={{0,64},{64,0},{1,65},{65,1},{2,66},{66,2},{3,67},{67,3},{4,68},{68... | collective-permute-start | bytes 1179656 | tf_op jit(solution)/shard_map/ppermute | solution.py:30
  129.7 16.9 %collective-permute-start.1 = (bf16[8,16,768]{2,1,0:T(8,128)(2,1)S(1)}, bf16[8,16,768]{2,1,0:T(8,128)(2,1)S(1)}, u32[]{:S(2)}, u32[]{:S(2)}) collective-permute-start(bf16[8,16,768]{2,1,0:T(8,128)(2,1)S(1)} %fusion.2), channel_id=1, source_target_pairs={{0,8},{8,0},{1,9},{9,1},{2,10},{10,2},{3,11},{11,3},{4,12},{12,4},... | collective-permute-start | bytes 589832 | tf_op jit(solution)/shard_map/ppermute | solution.py:30
  147.3 15.8 %all-to-all-start.3 = ((bf16[8,16,768]{2,1,0:T(8,128)(2,1)}), bf16[8,16,768]{2,1,0:T(8,128)(2,1)S(1)}, u32[]{:S(2)}, u32[]{:S(2)}) async-start(bf16[8,16,768]{2,1,0:T(8,128)(2,1)} %fusion.1), calls=%async_computation.3 | async-start | bytes 393216 | tf_op jit(solution)/shard_map/all_to_all | solution.py:81

commit v3 on v2

--- a/solution.py
+++ b/solution.py
@@ -37,24 +37,24 @@
     code_row = lax.axis_index(CODE) * here
     text_row = lax.axis_index(TEXT) * here
 
+    code_rows = jnp.mean(code_tokens.astype(f32), axis=1).astype(bf16)
     text_rows = jnp.mean(text_tokens.astype(f32), axis=1).astype(bf16)
+    code_pair = lax.all_gather(code_rows, "zl", axis=0, tiled=True)
+    code_pair, text_rows = lax.optimization_barrier((code_pair, text_rows))
     text_group = fan_out(text_rows, TEXT).reshape(-1, depth)
-    code_rows = jnp.mean(code_tokens.astype(f32), axis=1).astype(bf16)
-    code_group = gather_code(code_rows)
+    code_group = lax.all_gather(code_pair, ("y", "c"), axis=0, tiled=True)
 
+    nt = (((1,), (1,)), ((), ()))
     code_proj = jnp.dot(code_group, code_weight, preferred_element_type=f32).astype(bf16)
+    code_back = lax.dot_general(code_proj, text_weight, nt, preferred_element_type=f32).astype(bf16)
+    code_back = lax.optimization_barrier(code_back)
     text_proj = jnp.dot(text_group, text_weight, preferred_element_type=f32).astype(bf16)
-    nt = (((1,), (1,)), ((), ()))
     scores = lax.dot_general(code_proj, text_proj, nt, preferred_element_type=f32) * score_scale
     exps = jnp.exp(scores)
     row_part = jnp.sum(exps, axis=1)
     col_part = jnp.sum(exps, axis=0)
     col_total = jnp.sum(fan_out(col_part, TEXT), axis=0)
     row_total = jnp.sum(gather_code(row_part[None]), axis=0)
-    text_back = lax.dot_general(text_proj, code_weight, nt, preferred_element_type=f32).astype(bf16)
-    code_back = lax.dot_general(code_proj, text_weight, nt, preferred_element_type=f32).astype(bf16)
-    text_back, code_back = lax.optimization_barrier((text_back, code_back))
-
     own = jnp.eye(here, dtype=f32)
     own_scores = jnp.sum(lax.dynamic_slice(scores, (code_row, text_row), (here, here)) * own, axis=1)
     own_row_total = lax.dynamic_slice_in_dim(row_total, code_row, here)
@@ -71,14 +71,14 @@
         mixing, code_back, (((0,), (0,)), ((), ())), preferred_element_type=f32
     )
     text_parts = text_term.reshape(-1, here, depth).astype(bf16)
-    mixing, text_parts = lax.optimization_barrier((mixing, text_parts))
+    mixing, text_proj, text_parts = lax.optimization_barrier((mixing, text_proj, text_parts))
     text_parts = lax.all_to_all(text_parts, TEXT, split_axis=0, concat_axis=0, tiled=True)
+    text_back = lax.dot_general(text_proj, code_weight, nt, preferred_element_type=f32).astype(bf16)
     code_term = jnp.dot(mixing, text_back, preferred_element_type=f32)
-    code_parts = code_term.reshape(-1, 2, 2, here, depth)
-    code_parts = add_half(code_parts, 1, "c")
-    code_parts = add_half(code_parts, 1, "zl").astype(bf16)
+    code_parts = add_half(code_term.reshape(-1, 2, 2 * here, depth), 1, "c")
+    code_parts = code_parts.reshape(-1, here, depth).astype(bf16)
     code_parts, text_parts = lax.optimization_barrier((code_parts, text_parts))
-    code_parts = lax.all_to_all(code_parts, "y", split_axis=0, concat_axis=0, tiled=True)
+    code_parts = lax.all_to_all(code_parts, ("y", "zl"), split_axis=0, concat_axis=0, tiled=True)
     grad_code = score_scale * jnp.sum(code_parts.astype(f32), axis=0)
     grad_text = score_scale * jnp.sum(text_parts.astype(f32), axis=0)
     return pair_loss, grad_code.astype(bf16), grad_text.astype(bf16)

time: 165 us -> 150 us (0.909)
  the two profiles are of different devices: /device:TPU:4 before, /device:TPU:2 now
where the time goes in v3:
time: 150 us; the launch traced here: 149 us
  starting transfers between devices  52.9 us (35%)
  blocking collectives  45.4 us (30%)
  waiting for transfers between devices  25.6 us (17%)
  matrix products  13.6 us (9%)
  other arithmetic  7.78 us (5%)
  local copies, waits for them, and re-layouts  3.27 us (2%)
    all_to_all x2, starting transfers between devices, fan_out(): return lax.all_to_all(spread, axes, split_axis=0, concat_axis=0, tiled=True)  32.7 us
    all_gather x1, blocking collectives, shards(): code_group = lax.all_gather(code_pair, ('y', 'c'), axis=0, tiled=True)  20.5 us
    all_gather x1, blocking collectives, gather_code(): return lax.all_gather(pair, ('y', 'c'), axis=0, tiled=True)  14.7 us
    all_to_all x1, waiting for transfers between devices, shards(): lax.all_to_all(text_parts, TEXT, split_axis=0, concat_axis=0, tiled=True)  13.3 us
    all_to_all x1, starting transfers between devices, shards(): lax.all_to_all(text_parts, TEXT, split_axis=0, concat_axis=0, tiled=True)  12.2 us
    all_to_all x1, waiting for transfers between devices, shards(): lax.all_to_all(code_parts, ('y', 'zl'), split_axis=0, concat_axis=0, tile...  10.6 us
    all_to_all x1, starting transfers between devices, shards(): lax.all_to_all(code_parts, ('y', 'zl'), split_axis=0, concat_axis=0, tile...  6.19 us
    all_gather x1, blocking collectives, shards(): code_pair = lax.all_gather(code_rows, 'zl', axis=0, tiled=True)  5.74 us
  transfers between devices with their start and end apart: 5, of which 3 were waited for; matrix products, arithmetic and copies ran while one was open for 10% of the time, Pallas kernels for 0%

profile of v3, /device:TPU:2, one launch (start us, length us, event | category | flops | bytes accessed | tf_op | source)
XLA Modules:
  0.0 149.4 jit_solution(14800106993193385209)
XLA Ops:
  0.6 1.2 convert_reduce_fusion.3
  1.9 5.7 %all_gather.12 = bf16[32,768]{1,0:T(8,128)(2,1)S(1)} all-gather(bf16[16,768]{1,0:T(8,128)(2,1)S(1)} %multiply_convert_fusion.3), channel_id=1, replica_groups=mesh['x'=8,'c'=2,'zh'=4,'zl'=2,'y'=8] {'zl'}, dimensions={0}, use_global_device_ids=true | all-gather | bytes 73728 | tf_op jit(solution)/shard_map/all_gather | solution.py:42
  7.6 1.1 convert_reduce_fusion.2
  8.8 1.0 broadcast_in_dim.12
  9.8 20.5 %all-to-all-start = ((bf16[32,16,768]{2,1,0:T(8,128)(2,1)}), bf16[32,16,768]{2,1,0:T(8,128)(2,1)S(1)}, u32[]{:S(2)}, u32[]{:S(2)}) async-start(bf16[32,16,768]{2,1,0:T(8,128)(2,1)} %broadcast_in_dim.12), calls=%async_computation | async-start | bytes 1572864 | tf_op jit(solution)/shard_map/all_to_all | solution.py:18
  30.3 20.5 %all_gather.13 = bf16[512,768]{1,0:T(8,128)(2,1)S(1)} all-gather(bf16[32,768]{1,0:T(8,128)(2,1)S(1)} %all_gather.12), channel_id=1, replica_groups=mesh['x'=8,'c'=2,'zh'=4,'zl'=2,'y'=8] {'y','c'}, dimensions={0}, use_global_device_ids=true | all-gather | bytes 835584 | tf_op jit(solution)/shard_map/all_gather | solution.py:45
  50.8 2.4 %convolution_convert_fusion.1 = bf16[512,1024]{1,0:T(8,128)(2,1)S(1)} fusion(bf16[512,768]{1,0:T(8,128)(2,1)S(1)} %all_gather.13, bf16[768,1024]{1,0:T(8,128)(2,1)} %param.6), kind=kOutput, calls=%fused_computation.2 | convolution fusion | flops 805830656 | bytes 3407872 | tf_op jit(solution)/shard_map/dot_general | solution.py:48
  53.2 1.9 %convolution_convert_fusion.4 = bf16[512,768]{1,0:T(8,128)(2,1)} fusion(bf16[512,1024]{1,0:T(8,128)(2,1)S(1)} %convolution_convert_fusion.1, bf16[768,1024]{1,0:T(8,128)(2,1)S(1)} %copy-done), kind=kOutput, calls=%fused_computation.5 | convolution fusion | flops 805699584 | bytes 3407872 | tf_op jit(solution)/shard_map/dot_general | solution.py:49
  55.2 1.0 convolution_convert_fusion
  56.2 0.2 copy-done.4
  56.4 0.9 exponential_reduce_fusion.1
  57.3 0.1 copy-done.2
  57.4 0.7 all_to_all.16
  58.1 12.2 %all-to-all-start.1 = ((f32[32,1,512]{2,1,0:T(1,128)}), f32[32,1,512]{2,1,0:T(1,128)S(1)}, u32[]{:S(2)}, u32[]{:S(2)}) async-start(f32[32,1,512]{2,1,0:T(1,128)} %all_to_all.16), calls=%async_computation.1 | async-start | bytes 131072 | tf_op jit(solution)/shard_map/all_to_all | solution.py:18
  70.3 4.4 %all-gather.1 = f32[2,1,512]{2,1,0:T(1,128)S(1)} all-gather(f32[1,1,512]{2,1,0:T(1,128)S(1)} %bitcast.29), channel_id=2, replica_groups=mesh['x'=8,'c'=2,'zh'=4,'zl'=2,'y'=8] {'zl'}, dimensions={0}, use_global_device_ids=true | all-gather | bytes 6144 | tf_op jit(solution)/shard_map/all_gather | solution.py:22
  74.7 14.7 %all-gather.2 = f32[16,2,512]{2,1,0:T(2,128)S(1)} all-gather(f32[1,2,512]{2,1,0:T(2,128)S(1)} %copy.7), channel_id=1, replica_groups=mesh['x'=8,'c'=2,'zh'=4,'zl'=2,'y'=8] {'y','c'}, dimensions={0}, use_global_device_ids=true | all-gather | bytes 69632 | tf_op jit(solution)/shard_map/all_gather | solution.py:23
  89.6 0.5 subtract_convert_fusion
  90.1 2.6 %convolution_convert_fusion.3 = bf16[512,768]{1,0:T(8,128)(2,1)} fusion(bf16[512,512]{0,1:T(8,128)(2,1)S(1)} %subtract_convert_fusion, bf16[512,768]{1,0:T(8,128)(2,1)} %convolution_convert_fusion.4), kind=kOutput, calls=%fused_computation.4 | convolution fusion | flops 403046400 | bytes 2097152 | tf_op jit(solution)/shard_map/dot_general | solution.py:70
  92.7 12.2 %all-to-all-start.2 = ((bf16[32,16,768]{2,1,0:T(8,128)(2,1)}), bf16[32,16,768]{2,1,0:T(8,128)(2,1)S(1)}, u32[]{:S(2)}, u32[]{:S(2)}) async-start(bf16[32,16,768]{2,1,0:T(8,128)(2,1)} %bitcast.3), calls=%async_computation.2 | async-start | bytes 1572864 | tf_op jit(solution)/shard_map/all_to_all | solution.py:75
  104.9 4.9 %fusion = f32[512,768]{1,0:T(8,128)} fusion(bf16[512,512]{0,1:T(8,128)(2,1)S(1)} %subtract_convert_fusion, bf16[512,1024]{1,0:T(8,128)(2,1)} %copy-done.2, bf16[768,1024]{1,0:T(8,128)(2,1)} %param.6), kind=kOutput, calls=%fused_computation.7 | convolution fusion | flops 1208352768 | bytes 4718592 | tf_op jit(solution)/shard_map/dot_general | solution.py:77
  109.7 1.2 fusion.2
  110.9 1.9 %collective-permute-start = (bf16[8,32,768]{2,1,0:T(8,128)(2,1)S(1)}, bf16[8,32,768]{2,1,0:T(8,128)(2,1)S(1)}, u32[]{:S(2)}, u32[]{:S(2)}) collective-permute-start(bf16[8,32,768]{2,1,0:T(8,128)(2,1)S(1)} %fusion.2), channel_id=1, source_target_pairs={{0,64},{64,0},{1,65},{65,1},{2,66},{66,2},{3,67},{67,3},{4,68},{68... | collective-permute-start | bytes 1179656 | tf_op jit(solution)/shard_map/ppermute | solution.py:30
  112.9 1.7 %collective-permute-done = bf16[8,32,768]{2,1,0:T(8,128)(2,1)S(1)} collective-permute-done((bf16[8,32,768]{2,1,0:T(8,128)(2,1)S(1)}, bf16[8,32,768]{2,1,0:T(8,128)(2,1)S(1)}, u32[]{:S(2)}, u32[]{:S(2)}) %collective-permute-start) | collective-permute-done | bytes 393248 | tf_op jit(solution)/shard_map/ppermute | solution.py:30
  114.5 2.0 %fusion.1 = bf16[8,32,768]{2,1,0:T(8,128)(2,1)} fusion(bf16[8,32,768]{2,1,0:T(8,128)(2,1)S(1)} %collective-permute-done, f32[8,2,32,768]{3,2,1,0:T(8,128)} %bitcast.26, s32[]{:T(128)S(6)} %select_n.22), kind=kLoop, calls=%fused_computation.12 | loop fusion | flops 589824 | bytes 1572868 | tf_op jit(solution)/shard_map/convert_element_type | solution.py:79
  116.5 13.3 %all-to-all-done.2 = bf16[32,16,768]{2,1,0:T(8,128)(2,1)S(1)} async-done(((bf16[32,16,768]{2,1,0:T(8,128)(2,1)}), bf16[32,16,768]{2,1,0:T(8,128)(2,1)S(1)}, u32[]{:S(2)}, u32[]{:S(2)}) %all-to-all-start.2) | async-done | bytes 786464 | tf_op jit(solution)/shard_map/all_to_all | solution.py:75
  129.8 6.2 %all-to-all-start.3 = ((bf16[16,16,768]{2,1,0:T(8,128)(2,1)}), bf16[16,16,768]{2,1,0:T(8,128)(2,1)S(1)}, u32[]{:S(2)}, u32[]{:S(2)}) async-start(bf16[16,16,768]{2,1,0:T(8,128)(2,1)} %bitcast.7), calls=%async_computation.3 | async-start | bytes 786432 | tf_op jit(solution)/shard_map/all_to_all | solution.py:81
  136.0 0.8 select_reduce_fusion
  136.8 0.6 multiply_subtract_fusion
  137.4 0.1 convert_reduce_fusion
  137.5 0.6 multiply_convert_fusion
  138.1 10.6 %all-to-all-done.3 = bf16[16,16,768]{2,1,0:T(8,128)(2,1)S(1)} async-done(((bf16[16,16,768]{2,1,0:T(8,128)(2,1)}), bf16[16,16,768]{2,1,0:T(8,128)(2,1)S(1)}, u32[]{:S(2)}, u32[]{:S(2)}) %all-to-all-start.3) | async-done | bytes 393248 | tf_op jit(solution)/shard_map/all_to_all | solution.py:81
  148.8 0.6 multiply_convert_fusion.1
  (19 shorter events, 0.2 us)
Async XLA Ops:
  0.6 52.6 %copy-start = (bf16[768,1024]{1,0:T(8,128)(2,1)S(1)}, bf16[768,1024]{1,0:T(8,128)(2,1)}, u32[]{:S(2)}) copy-start(bf16[768,1024]{1,0:T(8,128)(2,1)} %param.7) | copy-start | bytes 4718596
  9.8 45.4 %all-to-all-start = ((bf16[32,16,768]{2,1,0:T(8,128)(2,1)}), bf16[32,16,768]{2,1,0:T(8,128)(2,1)S(1)}, u32[]{:S(2)}, u32[]{:S(2)}) async-start(bf16[32,16,768]{2,1,0:T(8,128)(2,1)} %broadcast_in_dim.12), calls=%async_computation | async-start | bytes 1572864 | tf_op jit(solution)/shard_map/all_to_all | solution.py:18
  53.2 1.9 %copy-start.3 = (bf16[512,1024]{1,0:T(8,128)(2,1)}, bf16[512,1024]{1,0:T(8,128)(2,1)S(1)}, u32[]{:S(2)}) copy-start(bf16[512,1024]{1,0:T(8,128)(2,1)S(1)} %convolution_convert_fusion.1) | copy-start | bytes 3145732
  55.2 1.2 copy-start.4
  56.4 1.0 copy-start.2
  57.4 35.3 %copy-start.1 = (f32[512,512]{0,1:T(8,128)}, f32[512,512]{0,1:T(8,128)S(1)}, u32[]{:S(2)}) copy-start(f32[512,512]{0,1:T(8,128)S(1)} %get-tuple-element.19) | copy-start | bytes 3145732
  58.1 31.4 %all-to-all-start.1 = ((f32[32,1,512]{2,1,0:T(1,128)}), f32[32,1,512]{2,1,0:T(1,128)S(1)}, u32[]{:S(2)}, u32[]{:S(2)}) async-start(f32[32,1,512]{2,1,0:T(1,128)} %all_to_all.16), calls=%async_computation.1 | async-start | bytes 131072 | tf_op jit(solution)/shard_map/all_to_all | solution.py:18
  92.7 37.1 %all-to-all-start.2 = ((bf16[32,16,768]{2,1,0:T(8,128)(2,1)}), bf16[32,16,768]{2,1,0:T(8,128)(2,1)S(1)}, u32[]{:S(2)}, u32[]{:S(2)}) async-start(bf16[32,16,768]{2,1,0:T(8,128)(2,1)} %bitcast.3), calls=%async_computation.2 | async-start | bytes 1572864 | tf_op jit(solution)/shard_map/all_to_all | solution.py:75
  110.9 3.6 %collective-permute-start = (bf16[8,32,768]{2,1,0:T(8,128)(2,1)S(1)}, bf16[8,32,768]{2,1,0:T(8,128)(2,1)S(1)}, u32[]{:S(2)}, u32[]{:S(2)}) collective-permute-start(bf16[8,32,768]{2,1,0:T(8,128)(2,1)S(1)} %fusion.2), channel_id=1, source_target_pairs={{0,64},{64,0},{1,65},{65,1},{2,66},{66,2},{3,67},{67,3},{4,68},{68... | collective-permute-start | bytes 1179656 | tf_op jit(solution)/shard_map/ppermute | solution.py:30
  129.8 18.9 %all-to-all-start.3 = ((bf16[16,16,768]{2,1,0:T(8,128)(2,1)}), bf16[16,16,768]{2,1,0:T(8,128)(2,1)S(1)}, u32[]{:S(2)}, u32[]{:S(2)}) async-start(bf16[16,16,768]{2,1,0:T(8,128)(2,1)} %bitcast.7), calls=%async_computation.3 | async-start | bytes 786432 | tf_op jit(solution)/shard_map/all_to_all | solution.py:81

commit v4 on v2

v4 whole, which is shorter than its diff:
```python
import math

import jax
import jax.numpy as jnp
from jax import lax
from jax.sharding import Mesh
from jax.sharding import PartitionSpec as P

score_scale = 0.1
CODE = ("yh", "yl", "c", "zl")
TEXT = ("xl", "xh", "zh")


def fan_out(block, axes):
    members = lax.axis_size(axes)
    spread = jnp.broadcast_to(block[None], (members,) + block.shape)
    spread = lax.optimization_barrier(spread)
    return lax.all_to_all(spread, axes, split_axis=0, concat_axis=0, tiled=True)


def add_half(term, name):
    me = lax.axis_index(name)
    theirs = lax.ppermute(term(1 - me).astype(jnp.bfloat16), name, [(0, 1), (1, 0)])
    return (term(me).astype(jnp.float32) + theirs.astype(jnp.float32)).astype(jnp.bfloat16)


def shards(code_tokens, text_tokens, code_weight, text_weight):
    f32, bf16 = jnp.float32, jnp.bfloat16
    nt = (((1,), (1,)), ((), ()))
    here, _, depth = code_tokens.shape
    code_row = lax.axis_index(CODE) * here
    text_row = lax.axis_index(TEXT) * here

    code_rows = jnp.mean(code_tokens.astype(f32), axis=1).astype(bf16)
    text_rows = jnp.mean(text_tokens.astype(f32), axis=1).astype(bf16)
    code_pair = lax.all_gather(code_rows, "zl", axis=0, tiled=True)
    code_pair, text_rows = lax.optimization_barrier((code_pair, text_rows))
    text_group = fan_out(text_rows, TEXT).reshape(-1, depth)
    code_group = lax.all_gather(code_pair, CODE[:3], axis=0, tiled=True)

    code_proj = jnp.dot(code_group, code_weight, preferred_element_type=f32).astype(bf16)
    text_proj = jnp.dot(text_group, text_weight, preferred_element_type=f32).astype(bf16)
    scores = lax.dot_general(code_proj, text_proj, nt, preferred_element_type=f32) * score_scale
    exps = jnp.exp(scores)
    row_part = jnp.sum(exps, axis=1)
    col_part = jnp.sum(exps, axis=0)
    col_parts = fan_out(col_part, TEXT)
    row_part = jnp.sum(lax.all_gather(row_part, ("zl", "c"), axis=0), axis=0)
    row_part, col_parts, code_proj, text_proj = lax.optimization_barrier(
        (row_part, col_parts, code_proj, text_proj)
    )
    col_total = jnp.sum(col_parts, axis=0)
    row_total = jnp.sum(fan_out(row_part, CODE[:2]), axis=0)
    text_back = lax.dot_general(text_proj, code_weight, nt, preferred_element_type=f32).astype(bf16)
    code_back = lax.dot_general(code_proj, text_weight, nt, preferred_element_type=f32).astype(bf16)
    text_back, code_back = lax.optimization_barrier((text_back, code_back))

    own = jnp.eye(here, dtype=f32)
    own_scores = jnp.sum(lax.dynamic_slice(scores, (code_row, text_row), (here, here)) * own, axis=1)
    own_row_total = lax.dynamic_slice_in_dim(row_total, code_row, here)
    own_col_total = lax.dynamic_slice_in_dim(col_total, text_row, here)
    pair_loss = 0.5 * (jnp.log(own_row_total) + jnp.log(own_col_total)) - own_scores

    rows = lax.broadcasted_iota(jnp.int32, scores.shape, 0) - code_row
    cols = lax.broadcasted_iota(jnp.int32, scores.shape, 1) - text_row
    paired = (rows == cols) & (rows >= 0) & (rows < here)
    mixing = 0.5 * (exps / row_total[:, None] + exps / col_total[None, :])
    mixing = (mixing - jnp.where(paired, 1.0, 0.0)).astype(bf16)

    def text_half(half):
        part = lax.dynamic_index_in_dim(mixing.reshape(-1, 2, cols_half), half, 1, keepdims=False)
        return lax.dot_general(part, code_back, (((0,), (0,)), ((), ())), preferred_element_type=f32)

    def code_half(half):
        part = lax.dynamic_index_in_dim(by_core, half, 1, keepdims=False)
        return jnp.dot(part.reshape(-1, part.shape[-1]), text_back, preferred_element_type=f32)

    cols_half = mixing.shape[1] // 2
    by_core = mixing.reshape(-1, 2, 2 * here, mixing.shape[1])
    text_parts = add_half(text_half, "xl").reshape(-1, here, depth)
    text_parts = lax.all_to_all(text_parts, TEXT[1:], split_axis=0, concat_axis=0, tiled=True)
    by_row = add_half(code_half, "c").reshape(-1, 2, 2 * here, depth)
    code_parts = add_half(lambda i: lax.dynamic_index_in_dim(by_row, i, 1, keepdims=False), "yl")
    code_parts, text_parts = lax.optimization_barrier((code_parts, text_parts))
    code_parts = code_parts.reshape(-1, here, depth)
    code_parts = lax.all_to_all(code_parts, ("yh", "zl"), split_axis=0, concat_axis=0, tiled=True)
    grad_code = score_scale * jnp.sum(code_parts.astype(f32), axis=0)
    grad_text = score_scale * jnp.sum(text_parts.astype(f32), axis=0)
    return pair_loss, grad_code.astype(bf16), grad_text.astype(bf16)


def solution(mesh):
    n_outer, n_inner = mesh.shape["outer"], mesh.shape["inner"]
    side = math.isqrt(n_inner)
    sizes = (n_outer // 4, 2, 2, side // 2, 2, side // 2, 2)
    fine = Mesh(mesh.devices.reshape(sizes), ("xh", "xl", "c", "zh", "zl", "yh", "yl"))
    every = P(fine.axis_names)
    return jax.shard_map(
        shards,
        mesh=fine,
        in_specs=(every, every, P(), P()),
        out_specs=(every, every, every),
        check_vma=False,
    )
```

time: 165 us -> 150 us (0.909)
  blocking collectives: 58.7 us -> 31.5 us
  waiting for transfers between devices: 23.6 us -> 32.2 us
  starting transfers between devices: 54.8 us -> 57.7 us
    all_gather x4 -> x3, blocking collectives: 58.7 us -> 31.5 us  [the longest x1 20.5 us: shards(): code_group = lax.all_gather(code_pair, CODE[:3], axis=0, tiled=True)]
    all_to_all x2 -> x3, waiting for transfers between devices: 0.01 us -> 11.2 us  [fan_out(): return lax.all_to_all(spread, axes, split_axis=0, concat_axis=0, tiled=True)]
    ppermute x2 -> x3, waiting for transfers between devices: 14.6 us -> 8.02 us  [add_half(): lax.ppermute(term(1 - me).astype(jnp.bfloat16), name, [(0, 1), (1, 0)])]
    all_to_all x2, waiting for transfers between devices: 9.04 us -> 13 us  [the longest x1 8.42 us: shards(): lax.all_to_all(code_parts, ('yh', 'zl'), split_axis=0, concat_axis=0, til...]
    ppermute x2 -> x3, starting transfers between devices: 4.75 us -> 7.25 us  [add_half(): lax.ppermute(term(1 - me).astype(jnp.bfloat16), name, [(0, 1), (1, 0)])]
    unnamed x15 -> x13, local copies, waits for them, and re-layouts: 2.21 us -> 0.03 us
    all_to_all x2 -> x3, starting transfers between devices: 33 us -> 34.6 us  [fan_out(): return lax.all_to_all(spread, axes, split_axis=0, concat_axis=0, tiled=True)]
    dot_general x2 -> x4, matrix products: 4.52 us -> 6.08 us  [the longest x2 4.6 us: text_half(): lax.dot_general(part, code_back, (((0,), (0,)), ((), ())), preferred_elem...]
  transfers between devices with their start and end apart: 6 -> 8, of which waited for: 3 -> 7; matrix products, arithmetic and copies ran while one was open for 9% -> 9% of each run, Pallas kernels for 0% -> 0%
where the time goes in v4:
time: 150 us; the launch traced here: 149 us
  starting transfers between devices  57.7 us (38%)
  waiting for transfers between devices  32.2 us (21%)
  blocking collectives  31.5 us (21%)
  matrix products  15.6 us (10%)
  other arithmetic  7.65 us (5%)
  local copies, waits for them, and re-layouts  3.25 us (2%)
    all_to_all x3, starting transfers between devices, fan_out(): return lax.all_to_all(spread, axes, split_axis=0, concat_axis=0, tiled=True)  34.6 us
    all_gather x1, blocking collectives, shards(): code_group = lax.all_gather(code_pair, CODE[:3], axis=0, tiled=True)  20.5 us
    all_to_all x3, waiting for transfers between devices, fan_out(): return lax.all_to_all(spread, axes, split_axis=0, concat_axis=0, tiled=True)  11.2 us
    all_to_all x1, waiting for transfers between devices, shards(): lax.all_to_all(code_parts, ('yh', 'zl'), split_axis=0, concat_axis=0, til...  8.42 us
    ppermute x3, waiting for transfers between devices, add_half(): lax.ppermute(term(1 - me).astype(jnp.bfloat16), name, [(0, 1), (1, 0)])  8.02 us
    all_to_all x1, starting transfers between devices, shards(): lax.all_to_all(code_parts, ('yh', 'zl'), split_axis=0, concat_axis=0, til...  7.97 us
    all_to_all x1, starting transfers between devices, shards(): lax.all_to_all(text_parts, TEXT[1:], split_axis=0, concat_axis=0, tiled=T...  7.86 us
    ppermute x3, starting transfers between devices, add_half(): lax.ppermute(term(1 - me).astype(jnp.bfloat16), name, [(0, 1), (1, 0)])  7.25 us
  transfers between devices with their start and end apart: 8, of which 7 were waited for; matrix products, arithmetic and copies ran while one was open for 9% of the time, Pallas kernels for 0%

profile of v4, /device:TPU:4, one launch (start us, length us, event | category | flops | bytes accessed | tf_op | source)
XLA Modules:
  0.0 148.7 jit_solution(4951821950921251460)
XLA Ops:
  0.6 1.2 convert_reduce_fusion.2
  1.9 5.7 %all_gather.12 = bf16[32,768]{1,0:T(8,128)(2,1)S(1)} all-gather(bf16[16,768]{1,0:T(8,128)(2,1)S(1)} %multiply_convert_fusion.3), channel_id=1, replica_groups=mesh['xh'=4,'xl'=2,'c'=2,'zh'=4,'zl'=2,'yh'=4,'yl'=2] {'zl'}, dimensions={0}, use_global_device_ids=true | all-gather | bytes 73728 | tf_op jit(solution)/shard_map/all_gather | solution.py:36
  7.6 1.1 convert_reduce_fusion.1
  8.8 0.9 broadcast_in_dim.12
  9.7 20.4 %all-to-all-start = ((bf16[32,16,768]{2,1,0:T(8,128)(2,1)}), bf16[32,16,768]{2,1,0:T(8,128)(2,1)S(1)}, u32[]{:S(2)}, u32[]{:S(2)}) async-start(bf16[32,16,768]{2,1,0:T(8,128)(2,1)} %broadcast_in_dim.12), calls=%async_computation | async-start | bytes 1572864 | tf_op jit(solution)/shard_map/all_to_all | solution.py:18
  30.2 20.5 %all_gather.13 = bf16[512,768]{1,0:T(8,128)(2,1)S(1)} all-gather(bf16[32,768]{1,0:T(8,128)(2,1)S(1)} %all_gather.12), channel_id=1, replica_groups=mesh['xh'=4,'xl'=2,'c'=2,'zh'=4,'zl'=2,'yh'=4,'yl'=2] {'yh','yl','c'}, dimensions={0}, use_global_device_ids=true | all-gather | bytes 835584 | tf_op jit(solution)/shard_map/all_gather | solution.py:39
  50.7 1.0 convolution_convert_fusion.1
  51.7 2.5 %all-to-all-done = bf16[32,16,768]{2,1,0:T(8,128)(2,1)S(1)} async-done(((bf16[32,16,768]{2,1,0:T(8,128)(2,1)}), bf16[32,16,768]{2,1,0:T(8,128)(2,1)S(1)}, u32[]{:S(2)}, u32[]{:S(2)}) %all-to-all-start) | async-done | bytes 786464 | tf_op jit(solution)/shard_map/all_to_all | solution.py:18
  54.2 2.4 %convolution_convert_fusion = bf16[512,1024]{1,0:T(8,128)(2,1)S(1)} fusion(bf16[512,768]{1,0:T(8,128)(2,1)S(1)} %bitcast.48, bf16[768,1024]{1,0:T(8,128)(2,1)} %param.7), kind=kOutput, calls=%fused_computation | convolution fusion | flops 805830656 | bytes 3407872 | tf_op jit(solution)/shard_map/dot_general | solution.py:42
  56.6 1.8 %exponential_reduce_fusion = (f32[512]{0:T(512)S(1)}, f32[512]{0:T(512)S(1)}, f32[512,512]{0,1:T(8,128)}) fusion(bf16[512,1024]{1,0:T(8,128)(2,1)S(1)} %convolution_convert_fusion.1, bf16[512,1024]{1,0:T(8,128)(2,1)S(1)} %convolution_convert_fusion), kind=kOutput, calls=%fused_computation.8 | convolution fusion | flops 537656320 | bytes 3149824 | tf_op jit(solution)/shard_map/dot_general | solution.py:43
  59.1 10.1 %all-to-all-start.1 = ((f32[32,1,512]{2,1,0:T(1,128)}), f32[32,1,512]{2,1,0:T(1,128)S(1)}, u32[]{:S(2)}, u32[]{:S(2)}) async-start(f32[32,1,512]{2,1,0:T(1,128)} %all_to_all.24), calls=%async_computation.1 | async-start | bytes 131072 | tf_op jit(solution)/shard_map/all_to_all | solution.py:18
  69.2 5.2 %all-gather.1 = f32[4,1,512]{2,1,0:T(1,128)S(1)} all-gather(f32[1,1,512]{2,1,0:T(1,128)S(1)} %bitcast.50), channel_id=2, replica_groups=mesh['xh'=4,'xl'=2,'c'=2,'zh'=4,'zl'=2,'yh'=4,'yl'=2] {'zl','c'}, dimensions={0}, use_global_device_ids=true | all-gather | bytes 10240 | tf_op jit(solution)/shard_map/all_gather | solution.py:48
  74.4 5.4 %all-to-all-done.1 = f32[32,1,512]{2,1,0:T(1,128)S(1)} async-done(((f32[32,1,512]{2,1,0:T(1,128)}), f32[32,1,512]{2,1,0:T(1,128)S(1)}, u32[]{:S(2)}, u32[]{:S(2)}) %all-to-all-start.1) | async-done | bytes 65568 | tf_op jit(solution)/shard_map/all_to_all | solution.py:18
  80.5 4.1 %all-to-all-start.2 = ((f32[8,1,512]{2,1,0:T(1,128)}), f32[8,1,512]{2,1,0:T(1,128)S(1)}, u32[]{:S(2)}, u32[]{:S(2)}) async-start(f32[8,1,512]{2,1,0:T(1,128)} %all_to_all.27), calls=%async_computation.2 | async-start | bytes 32768 | tf_op jit(solution)/shard_map/all_to_all | solution.py:18
  84.5 2.4 %convolution_convert_fusion.3 = bf16[512,768]{1,0:T(8,128)(2,1)S(1)} fusion(bf16[512,1024]{1,0:T(8,128)(2,1)} %copy-done.5, bf16[768,1024]{1,0:T(8,128)(2,1)S(1)} %copy-done), kind=kOutput, calls=%fused_computation.3 | convolution fusion | flops 805699584 | bytes 3407872 | tf_op jit(solution)/shard_map/dot_general | solution.py:54
  87.0 2.0 %convolution_convert_fusion.2 = bf16[512,768]{1,0:T(8,128)(2,1)} fusion(bf16[512,1024]{1,0:T(8,128)(2,1)S(1)} %copy-done.4, bf16[768,1024]{1,0:T(8,128)(2,1)S(1)} %copy-done.2), kind=kOutput, calls=%fused_computation.2 | convolution fusion | flops 805699584 | bytes 3407872 | tf_op jit(solution)/shard_map/dot_general | solution.py:55
  89.0 3.4 %all-to-all-done.2 = f32[8,1,512]{2,1,0:T(1,128)S(1)} async-done(((f32[8,1,512]{2,1,0:T(1,128)}), f32[8,1,512]{2,1,0:T(1,128)S(1)}, u32[]{:S(2)}, u32[]{:S(2)}) %all-to-all-start.2) | async-done | bytes 16416 | tf_op jit(solution)/shard_map/all_to_all | solution.py:18
  92.3 1.7 %subtract_convert_fusion = bf16[512,512]{0,1:T(8,128)(2,1)S(1)} fusion(f32[512,512]{0,1:T(8,128)} %get-tuple-element.27, s32[512]{0:T(512)S(1)} %get-tuple-element.31, f32[512]{0:T(512)S(1)} %reduce_sum.96, f32[512]{0:T(512)S(1)} %reduce_sum.95, s32[512]{0:T(512)S(1)} %get-tuple-element.30, pred[512]{0:T(512)(128)(4,1)S(1)} %get-tuple-element.28, ...), kind=kLoop, calls=%fused_computation.7 | loop fusion | flops 2621440 | bytes 1582080 | tf_op jit(solution)/shard_map/convert_element_type | solution.py:68
  94.3 2.3 %convolution_convert_fusion.4 = bf16[256,768]{1,0:T(8,128)(2,1)} fusion(bf16[512,768]{1,0:T(8,128)(2,1)} %convolution_convert_fusion.2, bf16[512,2,256]{0,2,1:T(8,128)(2,1)S(1)} %bitcast.41, s32[]{:T(128)S(6)} %select_n.41), kind=kOutput, calls=%fused_computation.5 | convolution fusion | flops 201523200 | bytes 1441796 | tf_op jit(solution)/shard_map/dot_general | solution.py:72
  96.6 2.5 %collective-permute-start.2 = (bf16[256,768]{1,0:T(8,128)(2,1)}, bf16[256,768]{1,0:T(8,128)(2,1)}, u32[]{:S(2)}, u32[]{:S(2)}) collective-permute-start(bf16[256,768]{1,0:T(8,128)(2,1)} %convolution_convert_fusion.4), channel_id=1, source_target_pairs={{0,128},{128,0},{1,129},{129,1},{2,130},{130,2},{3,131},{131,3},{4... | collective-permute-start | bytes 1179656 | tf_op jit(solution)/shard_map/ppermute | solution.py:23
  99.1 0.8 constant_dynamic-slice_fusion
  99.9 1.1 convolution_convert_fusion.5
  101.0 2.0 %collective-permute-start = (bf16[256,768]{1,0:T(8,128)(2,1)}, bf16[256,768]{1,0:T(8,128)(2,1)S(1)}, u32[]{:S(2)}, u32[]{:S(2)}) collective-permute-start(bf16[256,768]{1,0:T(8,128)(2,1)} %convolution_convert_fusion.5), channel_id=1, source_target_pairs={{0,64},{64,0},{1,65},{65,1},{2,66},{66,2},{3,67},{67,3},{4,68},{68... | collective-permute-start | bytes 1179656 | tf_op jit(solution)/shard_map/ppermute | solution.py:23
  103.0 0.8 select_reduce_fusion
  103.8 3.7 %collective-permute-done.2 = bf16[256,768]{1,0:T(8,128)(2,1)} collective-permute-done((bf16[256,768]{1,0:T(8,128)(2,1)}, bf16[256,768]{1,0:T(8,128)(2,1)}, u32[]{:S(2)}, u32[]{:S(2)}) %collective-permute-start.2) | collective-permute-done | bytes 393248 | tf_op jit(solution)/shard_map/ppermute | solution.py:23
  107.6 2.3 %add_convert_fusion = bf16[256,768]{1,0:T(8,128)(2,1)} fusion(bf16[256,768]{1,0:T(8,128)(2,1)} %collective-permute-done.2, bf16[512,768]{1,0:T(8,128)(2,1)} %convolution_convert_fusion.2, bf16[512,2,256]{0,2,1:T(8,128)(2,1)S(1)} %bitcast.42, s32[]{:T(128)S(6)} %select_n.40), kind=kOutput, calls=%fused_computation.11 | convolution fusion | flops 201916416 | bytes 1835012 | tf_op jit(solution)/shard_map/dot_general | solution.py:72
  109.9 7.9 %all-to-all-start.3 = ((bf16[16,16,768]{2,1,0:T(8,128)(2,1)}), bf16[16,16,768]{2,1,0:T(8,128)(2,1)S(1)}, u32[]{:S(2)}, u32[]{:S(2)}) async-start(bf16[16,16,768]{2,1,0:T(8,128)(2,1)} %bitcast.11), calls=%async_computation.3 | async-start | bytes 786432 | tf_op jit(solution)/shard_map/all_to_all | solution.py:81
  118.2 2.7 %collective-permute-start.1 = (bf16[4,32,768]{2,1,0:T(8,128)(2,1)S(1)}, bf16[4,32,768]{2,1,0:T(8,128)(2,1)S(1)}, u32[]{:S(2)}, u32[]{:S(2)}) collective-permute-start(bf16[4,32,768]{2,1,0:T(8,128)(2,1)S(1)} %dynamic-slice_bitcast_fusion), channel_id=1, source_target_pairs={{0,1},{1,0},{2,3},{3,2},{4,5},{5,4},{6,7},{7,6},{8,9},{9,8},{10,11... | collective-permute-start | bytes 589832 | tf_op jit(solution)/shard_map/ppermute | solution.py:23
  121.5 4.3 %collective-permute-done.1 = bf16[4,32,768]{2,1,0:T(8,128)(2,1)S(1)} collective-permute-done((bf16[4,32,768]{2,1,0:T(8,128)(2,1)S(1)}, bf16[4,32,768]{2,1,0:T(8,128)(2,1)S(1)}, u32[]{:S(2)}, u32[]{:S(2)}) %collective-permute-start.1) | collective-permute-done | bytes 196640 | tf_op jit(solution)/shard_map/ppermute | solution.py:23
  126.5 4.5 %all-to-all-done.3 = bf16[16,16,768]{2,1,0:T(8,128)(2,1)S(1)} async-done(((bf16[16,16,768]{2,1,0:T(8,128)(2,1)}), bf16[16,16,768]{2,1,0:T(8,128)(2,1)S(1)}, u32[]{:S(2)}, u32[]{:S(2)}) %all-to-all-start.3) | async-done | bytes 393248 | tf_op jit(solution)/shard_map/all_to_all | solution.py:81
  131.0 8.0 %all-to-all-start.4 = ((bf16[8,16,768]{2,1,0:T(8,128)(2,1)}), bf16[8,16,768]{2,1,0:T(8,128)(2,1)S(1)}, u32[]{:S(2)}, u32[]{:S(2)}) async-start(bf16[8,16,768]{2,1,0:T(8,128)(2,1)} %bitcast.12), calls=%async_computation.4 | async-start | bytes 393216 | tf_op jit(solution)/shard_map/all_to_all | solution.py:86
  139.7 8.4 %all-to-all-done.4 = bf16[8,16,768]{2,1,0:T(8,128)(2,1)S(1)} async-done(((bf16[8,16,768]{2,1,0:T(8,128)(2,1)}), bf16[8,16,768]{2,1,0:T(8,128)(2,1)S(1)}, u32[]{:S(2)}, u32[]{:S(2)}) %all-to-all-start.4) | async-done | bytes 196640 | tf_op jit(solution)/shard_map/all_to_all | solution.py:86
  (34 shorter events, 4.7 us)
Async XLA Ops:
  0.6 50.1 %copy-start = (bf16[768,1024]{1,0:T(8,128)(2,1)S(1)}, bf16[768,1024]{1,0:T(8,128)(2,1)}, u32[]{:S(2)}) copy-start(bf16[768,1024]{1,0:T(8,128)(2,1)} %param.6) | copy-start | bytes 4718596
  9.7 44.5 %all-to-all-start = ((bf16[32,16,768]{2,1,0:T(8,128)(2,1)}), bf16[32,16,768]{2,1,0:T(8,128)(2,1)S(1)}, u32[]{:S(2)}, u32[]{:S(2)}) async-start(bf16[32,16,768]{2,1,0:T(8,128)(2,1)} %broadcast_in_dim.12), calls=%async_computation | async-start | bytes 1572864 | tf_op jit(solution)/shard_map/all_to_all | solution.py:18
  51.7 4.9 %copy-start.3 = (bf16[512,1024]{1,0:T(8,128)(2,1)}, bf16[512,1024]{1,0:T(8,128)(2,1)S(1)}, u32[]{:S(2)}) copy-start(bf16[512,1024]{1,0:T(8,128)(2,1)S(1)} %convolution_convert_fusion.1) | copy-start | bytes 3145732
  56.6 1.8 %copy-start.5 = (bf16[512,1024]{1,0:T(8,128)(2,1)}, bf16[512,1024]{1,0:T(8,128)(2,1)S(1)}, u32[]{:S(2)}) copy-start(bf16[512,1024]{1,0:T(8,128)(2,1)S(1)} %convolution_convert_fusion) | copy-start | bytes 3145732
  59.1 20.7 %all-to-all-start.1 = ((f32[32,1,512]{2,1,0:T(1,128)}), f32[32,1,512]{2,1,0:T(1,128)S(1)}, u32[]{:S(2)}, u32[]{:S(2)}) async-start(f32[32,1,512]{2,1,0:T(1,128)} %all_to_all.24), calls=%async_computation.1 | async-start | bytes 131072 | tf_op jit(solution)/shard_map/all_to_all | solution.py:18
  80.5 11.9 %all-to-all-start.2 = ((f32[8,1,512]{2,1,0:T(1,128)}), f32[8,1,512]{2,1,0:T(1,128)S(1)}, u32[]{:S(2)}, u32[]{:S(2)}) async-start(f32[8,1,512]{2,1,0:T(1,128)} %all_to_all.27), calls=%async_computation.2 | async-start | bytes 32768 | tf_op jit(solution)/shard_map/all_to_all | solution.py:18
  84.5 2.4 %copy-start.2 = (bf16[768,1024]{1,0:T(8,128)(2,1)S(1)}, bf16[768,1024]{1,0:T(8,128)(2,1)}, u32[]{:S(2)}) copy-start(bf16[768,1024]{1,0:T(8,128)(2,1)} %param.7) | copy-start | bytes 4718596
  84.5 2.4 %copy-start.4 = (bf16[512,1024]{1,0:T(8,128)(2,1)S(1)}, bf16[512,1024]{1,0:T(8,128)(2,1)}, u32[]{:S(2)}) copy-start(bf16[512,1024]{1,0:T(8,128)(2,1)} %copy-done.3) | copy-start | bytes 3145732
  96.6 11.0 %collective-permute-start.2 = (bf16[256,768]{1,0:T(8,128)(2,1)}, bf16[256,768]{1,0:T(8,128)(2,1)}, u32[]{:S(2)}, u32[]{:S(2)}) collective-permute-start(bf16[256,768]{1,0:T(8,128)(2,1)} %convolution_convert_fusion.4), channel_id=1, source_target_pairs={{0,128},{128,0},{1,129},{129,1},{2,130},{130,2},{3,131},{131,3},{4... | collective-permute-start | bytes 1179656 | tf_op jit(solution)/shard_map/ppermute | solution.py:23
  101.0 16.8 %copy-start.1 = (bf16[8,1,32,512]{3,2,1,0:T(8,128)(2,1)S(1)}, bf16[8,1,32,512]{3,2,1,0:T(8,128)(2,1)}, u32[]{:S(2)}) copy-start(bf16[8,1,32,512]{3,2,1,0:T(8,128)(2,1)} %get-tuple-element.26) | copy-start | bytes 786436
  101.0 16.8 %collective-permute-start = (bf16[256,768]{1,0:T(8,128)(2,1)}, bf16[256,768]{1,0:T(8,128)(2,1)S(1)}, u32[]{:S(2)}, u32[]{:S(2)}) collective-permute-start(bf16[256,768]{1,0:T(8,128)(2,1)} %convolution_convert_fusion.5), channel_id=1, source_target_pairs={{0,64},{64,0},{1,65},{65,1},{2,66},{66,2},{3,67},{67,3},{4,68},{68... | collective-permute-start | bytes 1179656 | tf_op jit(solution)/shard_map/ppermute | solution.py:23
  109.9 21.1 %all-to-all-start.3 = ((bf16[16,16,768]{2,1,0:T(8,128)(2,1)}), bf16[16,16,768]{2,1,0:T(8,128)(2,1)S(1)}, u32[]{:S(2)}, u32[]{:S(2)}) async-start(bf16[16,16,768]{2,1,0:T(8,128)(2,1)} %bitcast.11), calls=%async_computation.3 | async-start | bytes 786432 | tf_op jit(solution)/shard_map/all_to_all | solution.py:81
  118.2 7.6 %collective-permute-start.1 = (bf16[4,32,768]{2,1,0:T(8,128)(2,1)S(1)}, bf16[4,32,768]{2,1,0:T(8,128)(2,1)S(1)}, u32[]{:S(2)}, u32[]{:S(2)}) collective-permute-start(bf16[4,32,768]{2,1,0:T(8,128)(2,1)S(1)} %dynamic-slice_bitcast_fusion), channel_id=1, source_target_pairs={{0,1},{1,0},{2,3},{3,2},{4,5},{5,4},{6,7},{7,6},{8,9},{9,8},{10,11... | collective-permute-start | bytes 589832 | tf_op jit(solution)/shard_map/ppermute | solution.py:23
  131.0 17.1 %all-to-all-start.4 = ((bf16[8,16,768]{2,1,0:T(8,128)(2,1)}), bf16[8,16,768]{2,1,0:T(8,128)(2,1)S(1)}, u32[]{:S(2)}, u32[]{:S(2)}) async-start(bf16[8,16,768]{2,1,0:T(8,128)(2,1)} %bitcast.12), calls=%async_computation.4 | async-start | bytes 393216 | tf_op jit(solution)/shard_map/all_to_all | solution.py:86

commit v5 on v3

v5 whole, which is shorter than its diff:
```python
import math

import jax
import jax.numpy as jnp
from jax import lax
from jax.experimental import pallas as pl
from jax.experimental.pallas import tpu as pltpu
from jax.sharding import Mesh
from jax.sharding import PartitionSpec as P

score_scale = 0.1
CODE = ("yh", "yl", "c", "zl")
TEXT = ("x", "zh")


def pool_kernel(code_ref, text_ref, code_out, text_out):
    for tokens, out in ((code_ref, code_out), (text_ref, text_out)):
        total = jnp.sum(tokens[...].astype(jnp.float32), axis=1)
        rows = (total * (1.0 / tokens.shape[1])).astype(jnp.bfloat16)
        out[...] = rows if out is code_out else jnp.broadcast_to(rows[None], out.shape)


def pool(code_tokens, text_tokens, copies):
    here, _, depth = code_tokens.shape
    return pl.pallas_call(
        pool_kernel,
        out_shape=(
            jax.ShapeDtypeStruct((here, depth), jnp.bfloat16),
            jax.ShapeDtypeStruct((copies, here, depth), jnp.bfloat16),
        ),
    )(code_tokens, text_tokens)


def exchange(parts, axes):
    return lax.all_to_all(parts, axes, split_axis=0, concat_axis=0, tiled=True)


def fan_out(block, axes):
    members = lax.axis_size(axes)
    spread = jnp.broadcast_to(block[None], (members,) + block.shape)
    return exchange(lax.optimization_barrier(spread), axes)


def swap(block, name):
    return lax.ppermute(block, name, [(0, 1), (1, 0)])


def code_sum_kernel(core_ref, mixing_ref, text_ref, weight_ref, mine_ref, theirs_ref, back_ref, rows_ref):
    nt = (((1,), (1,)), ((), ()))
    step = text_ref.shape[0] // 2
    for i in range(2):
        part = text_ref[i * step : (i + 1) * step, :]
        back = lax.dot_general(part, weight_ref[...], nt, preferred_element_type=jnp.float32)
        back_ref[i * step : (i + 1) * step, :] = back.astype(jnp.bfloat16)
    chunk = 32
    for core, out_ref in ((1 - core_ref[0], theirs_ref), (core_ref[0], mine_ref)):
        for i in range(out_ref.shape[0] // chunk):
            start = pl.multiple_of(core * chunk + 2 * i * chunk, chunk)
            rows_ref[i * chunk : (i + 1) * chunk, :] = mixing_ref[pl.ds(start, chunk), :]
        total = jnp.dot(rows_ref[...], back_ref[...], preferred_element_type=jnp.float32)
        out_ref[...] = total.astype(out_ref.dtype)


def code_sum(core, mixing, text_proj, weight):
    rows, cols = mixing.shape
    depth = weight.shape[0]
    vmem = pl.BlockSpec(memory_space=pltpu.VMEM)
    half = jax.ShapeDtypeStruct((rows // 2, depth), jnp.bfloat16)
    return pl.pallas_call(
        code_sum_kernel,
        out_shape=(half, half),
        in_specs=[pl.BlockSpec(memory_space=pltpu.SMEM), vmem, vmem, vmem],
        out_specs=(vmem, vmem),
        scratch_shapes=[
            pltpu.VMEM((cols, depth), jnp.bfloat16),
            pltpu.VMEM((rows // 2, cols), jnp.bfloat16),
        ],
        compiler_params=pltpu.CompilerParams(vmem_limit_bytes=32 << 20),
        cost_estimate=pl.CostEstimate(flops=1 << 28, bytes_accessed=1 << 20, transcendentals=0),
    )(core.reshape(1), mixing, text_proj, weight)


def shards(code_tokens, text_tokens, code_weight, text_weight):
    f32, bf16 = jnp.float32, jnp.bfloat16
    nt = (((1,), (1,)), ((), ()))
    here, _, depth = code_tokens.shape
    code_row = lax.axis_index(CODE) * here
    text_row = lax.axis_index(TEXT) * here

    code_rows, text_rows = pool(code_tokens, text_tokens, lax.axis_size(TEXT))
    code_pair = lax.all_gather(code_rows, "zl", axis=0, tiled=True)
    code_pair, text_rows = lax.optimization_barrier((code_pair, text_rows))
    text_group = exchange(text_rows, TEXT).reshape(-1, depth)
    code_group = lax.all_gather(code_pair, CODE[:3], axis=0, tiled=True)

    code_proj = jnp.dot(code_group, code_weight, preferred_element_type=f32).astype(bf16)
    code_back = lax.dot_general(code_proj, text_weight, nt, preferred_element_type=f32).astype(bf16)
    code_back, text_group = lax.optimization_barrier((code_back, text_group))
    text_proj = jnp.dot(text_group, text_weight, preferred_element_type=f32).astype(bf16)
    scores = lax.dot_general(code_proj, text_proj, nt, preferred_element_type=f32) * score_scale
    exps = jnp.exp(scores)
    row_part = jnp.sum(exps, axis=1)
    col_part = jnp.sum(exps, axis=0)
    row_part = row_part + swap(row_part, "zl")
    col_total = jnp.sum(fan_out(col_part, TEXT), axis=0)
    row_total = jnp.sum(lax.all_gather(row_part, CODE[:3], axis=0), axis=0)

    own = jnp.eye(here, dtype=f32)
    own_scores = jnp.sum(lax.dynamic_slice(scores, (code_row, text_row), (here, here)) * own, axis=1)
    own_row_total = lax.dynamic_slice_in_dim(row_total, code_row, here)
    own_col_total = lax.dynamic_slice_in_dim(col_total, text_row, here)
    pair_loss = 0.5 * (jnp.log(own_row_total) + jnp.log(own_col_total)) - own_scores

    rows = lax.broadcasted_iota(jnp.int32, scores.shape, 0) - code_row
    cols = lax.broadcasted_iota(jnp.int32, scores.shape, 1) - text_row
    paired = (rows == cols) & (rows >= 0) & (rows < here)
    mixing = 0.5 * (exps / row_total[:, None] + exps / col_total[None, :])
    mixing = (mixing - jnp.where(paired, 1.0, 0.0)).astype(bf16)

    text_term = lax.dot_general(
        mixing, code_back, (((0,), (0,)), ((), ())), preferred_element_type=f32
    )
    text_proj, text_parts = lax.optimization_barrier((text_proj, text_term.astype(bf16)))
    text_parts = exchange(text_parts.reshape(-1, here, depth), TEXT)

    mine, theirs = code_sum(lax.axis_index("c"), mixing, text_proj, code_weight)
    code_parts = (mine.astype(f32) + swap(theirs, "c").astype(f32)).astype(bf16)
    code_parts = code_parts.reshape(-1, 2, 2 * here, depth)
    side = lax.axis_index("yl")
    mine = lax.dynamic_index_in_dim(code_parts, side, 1, keepdims=False)
    theirs = lax.dynamic_index_in_dim(code_parts, 1 - side, 1, keepdims=False)
    code_parts = (mine.astype(f32) + swap(theirs, "yl").astype(f32)).astype(bf16)
    code_parts, text_parts = lax.optimization_barrier((code_parts, text_parts))
    code_parts = exchange(code_parts.reshape(-1, here, depth), ("yh", "zl"))
    grad_code = score_scale * jnp.sum(code_parts.astype(f32), axis=0)
    grad_text = score_scale * jnp.sum(text_parts.astype(f32), axis=0)
    return pair_loss, grad_code.astype(bf16), grad_text.astype(bf16)


def solution(mesh):
    n_outer, n_inner = mesh.shape["outer"], mesh.shape["inner"]
    side = math.isqrt(n_inner)
    sizes = (n_outer // 2, 2, side // 2, 2, side // 2, 2)
    fine = Mesh(mesh.devices.reshape(sizes), ("x", "c", "zh", "zl", "yh", "yl"))
    every = P(fine.axis_names)
    return jax.shard_map(
        shards,
        mesh=fine,
        in_specs=(every, every, P(), P()),
        out_specs=(every, every, every),
        check_vma=False,
    )
```

time: 150 us -> 150 us (level)
  starting transfers between devices: 52.9 us -> 60.2 us
  Pallas kernels: 0 us -> 4.46 us
  blocking collectives: 45.4 us -> 41.2 us
  matrix products: 13.6 us -> 9.53 us
  waiting for transfers between devices: 25.6 us -> 22.8 us
    all_to_all x4, waiting for transfers between devices: 23.9 us -> 15.4 us  [exchange(): return lax.all_to_all(parts, axes, split_axis=0, concat_axis=0, tiled=True)]
    ppermute x1 -> x3, starting transfers between devices: 1.92 us -> 9.26 us  [swap(): return lax.ppermute(block, name, [(0, 1), (1, 0)])]
    ppermute x1 -> x3, waiting for transfers between devices: 1.69 us -> 7.38 us  [swap(): return lax.ppermute(block, name, [(0, 1), (1, 0)])]
    dot_general x1 -> x0, matrix products: 4.89 us -> none  [shards(): code_term = jnp.dot(mixing, text_back, preferred_element_type=f32)]
    all_gather x3 -> x2, blocking collectives: 39.7 us -> 35.2 us  [the longest x1 20.5 us: shards(): code_group = lax.all_gather(code_pair, CODE[:3], axis=0, tiled=True)]
    pallas_call x0 -> x2, Pallas kernels: none -> 4.46 us  [the longest x1 2.42 us: pool(): pl.pallas_call(pool_kernel, out_shape=(jax.ShapeDtypeStruct((here, depth)...]
    reduce_sum x3 -> x1, other arithmetic: 2.42 us -> 0.04 us  [shards(): row_total = jnp.sum(lax.all_gather(row_part, CODE[:3], axis=0), axis=0)]
    unnamed x11 -> x10, local copies, waits for them, and re-layouts: 0.38 us -> 2.4 us
  transfers between devices with their start and end apart: 5 -> 7, of which waited for: 3 -> 5; matrix products, arithmetic and copies ran while one was open for 10% -> 5% of each run, Pallas kernels for 0% -> 1%
where the time goes in v5:
time: 150 us; the launch traced here: 149 us
  starting transfers between devices  60.2 us (40%)
  blocking collectives  41.2 us (27%)
  waiting for transfers between devices  22.8 us (15%)
  matrix products  9.53 us (6%)
  other arithmetic  6.7 us (4%)
  Pallas kernels  4.46 us (3%)
  local copies, waits for them, and re-layouts  3.1 us (2%)
    all_to_all x4, starting transfers between devices, exchange(): return lax.all_to_all(parts, axes, split_axis=0, concat_axis=0, tiled=True)  50.9 us
    all_gather x1, blocking collectives, shards(): code_group = lax.all_gather(code_pair, CODE[:3], axis=0, tiled=True)  20.5 us
    all_to_all x4, waiting for transfers between devices, exchange(): return lax.all_to_all(parts, axes, split_axis=0, concat_axis=0, tiled=True)  15.4 us
    all_gather x1, blocking collectives, shards(): row_total = jnp.sum(lax.all_gather(row_part, CODE[:3], axis=0), axis=0)  14.6 us
    ppermute x3, starting transfers between devices, swap(): return lax.ppermute(block, name, [(0, 1), (1, 0)])  9.26 us
    ppermute x3, waiting for transfers between devices, swap(): return lax.ppermute(block, name, [(0, 1), (1, 0)])  7.38 us
    all_gather x1, blocking collectives, shards(): code_pair = lax.all_gather(code_rows, 'zl', axis=0, tiled=True)  6 us
  transfers between devices with their start and end apart: 7, of which 5 were waited for; matrix products, arithmetic and copies ran while one was open for 5% of the time, Pallas kernels for 1%

profile of v5, /device:TPU:2, one launch (start us, length us, event | category | flops | bytes accessed | tf_op | source)
XLA Modules:
  0.0 148.8 jit_solution(14947097728380394268)
XLA Ops:
  0.7 2.4 %shard_map.67 = (bf16[16,768]{1,0:T(8,128)(2,1)}, bf16[32,16,768]{2,1,0:T(8,128)(2,1)}) custom-call(bf16[16,16,768]{2,1,0:T(8,128)(2,1)} %code_ref.1, bf16[16,16,768]{2,1,0:T(8,128)(2,1)} %text_ref.1), custom_call_target="tpu_custom_call" | custom-call | tf_op jit(solution)/shard_map/pallas_call | solution.py:25
  3.1 6.0 %all_gather.12 = bf16[32,768]{1,0:T(8,128)(2,1)S(1)} all-gather(bf16[16,768]{1,0:T(8,128)(2,1)} %get-tuple-element.15), channel_id=1, replica_groups=mesh['x'=8,'c'=2,'zh'=4,'zl'=2,'yh'=4,'yl'=2] {'zl'}, dimensions={0}, use_global_device_ids=true | all-gather | bytes 73728 | tf_op jit(solution)/shard_map/all_gather | solution.py:91
  9.1 20.5 %all-to-all-start = ((bf16[32,16,768]{2,1,0:T(8,128)(2,1)}), bf16[32,16,768]{2,1,0:T(8,128)(2,1)}, u32[]{:S(2)}, u32[]{:S(2)}) async-start(bf16[32,16,768]{2,1,0:T(8,128)(2,1)} %get-tuple-element.18), calls=%async_computation | async-start | bytes 1572864 | tf_op jit(solution)/shard_map/all_to_all | solution.py:35
  29.6 20.5 %all_gather.13 = bf16[512,768]{1,0:T(8,128)(2,1)S(1)} all-gather(bf16[32,768]{1,0:T(8,128)(2,1)S(1)} %all_gather.12), channel_id=1, replica_groups=mesh['x'=8,'c'=2,'zh'=4,'zl'=2,'yh'=4,'yl'=2] {'yh','yl','c'}, dimensions={0}, use_global_device_ids=true | all-gather | bytes 835584 | tf_op jit(solution)/shard_map/all_gather | solution.py:94
  50.2 1.0 convolution_convert_fusion.1
  51.2 1.0 copy-done.3
  52.2 2.0 %convolution_convert_fusion.3 = bf16[512,768]{1,0:T(8,128)(2,1)} fusion(bf16[512,1024]{1,0:T(8,128)(2,1)S(1)} %convolution_convert_fusion.1, bf16[768,1024]{1,0:T(8,128)(2,1)S(1)} %copy-done), kind=kOutput, calls=%fused_computation.4 | convolution fusion | flops 805699584 | bytes 3407872 | tf_op jit(solution)/shard_map/dot_general | solution.py:97
  54.1 2.2 %convolution_convert_fusion.text_ref = bf16[512,1024]{1,0:T(8,128)(2,1)S(1)} fusion(bf16[512,768]{1,0:T(8,128)(2,1)} %bitcast, bf16[768,1024]{1,0:T(8,128)(2,1)S(1)} %copy-done), kind=kOutput, calls=%fused_computation.1 | convolution fusion | flops 805830656 | bytes 3407872 | tf_op jit(solution)/shard_map/dot_general | solution.py:99
  56.3 1.8 %exponential_reduce_fusion.1 = (f32[512]{0:T(512)S(1)}, f32[512]{0:T(512)S(1)}, f32[512,512]{1,0:T(8,128)}) fusion(bf16[512,1024]{1,0:T(8,128)(2,1)S(1)} %copy-done.4, bf16[512,1024]{1,0:T(8,128)(2,1)S(1)} %convolution_convert_fusion.text_ref), kind=kOutput, calls=%fused_computation.8 | convolution fusion | flops 537656320 | bytes 3149824 | tf_op jit(solution)/shard_map/dot_general | solution.py:100
  58.1 0.7 all_to_all.16
  58.8 12.2 %all-to-all-start.1 = ((f32[32,1,512]{2,1,0:T(1,128)}), f32[32,1,512]{2,1,0:T(1,128)S(1)}, u32[]{:S(2)}, u32[]{:S(2)}) async-start(f32[32,1,512]{2,1,0:T(1,128)} %all_to_all.16), calls=%async_computation.1 | async-start | bytes 131072 | tf_op jit(solution)/shard_map/all_to_all | solution.py:35
  71.0 3.9 %collective-permute-start = (f32[512]{0:T(512)S(1)}, f32[512]{0:T(512)S(1)}, u32[]{:S(2)}, u32[]{:S(2)}) collective-permute-start(f32[512]{0:T(512)S(1)} %get-tuple-element.27), channel_id=1, source_target_pairs={{0,8},{8,0},{1,9},{9,1},{2,10},{10,2},{3,11},{11,3},{4,12},{12,4},... | collective-permute-start | bytes 6152 | tf_op jit(solution)/shard_map/ppermute | solution.py:45
  74.9 1.6 %collective-permute-done = f32[512]{0:T(512)S(1)} collective-permute-done((f32[512]{0:T(512)S(1)}, f32[512]{0:T(512)S(1)}, u32[]{:S(2)}, u32[]{:S(2)}) %collective-permute-start) | collective-permute-done | bytes 2080 | tf_op jit(solution)/shard_map/ppermute | solution.py:45
  76.5 14.6 %all-gather.1 = f32[16,1,512]{2,1,0:T(1,128)S(1)} all-gather(f32[1,1,512]{2,1,0:T(1,128)S(1)} %bitcast.24), channel_id=2, replica_groups=mesh['x'=8,'c'=2,'zh'=4,'zl'=2,'yh'=4,'yl'=2] {'yh','yl','c'}, dimensions={0}, use_global_device_ids=true | all-gather | bytes 34816 | tf_op jit(solution)/shard_map/all_gather | solution.py:106
  91.3 1.8 %subtract_convert_fusion.mixing_ref = bf16[512,512]{1,0:T(8,128)(2,1)S(1)} fusion(f32[512,512]{1,0:T(8,128)} %get-tuple-element.29, s32[512]{0:T(512)S(1)} %get-tuple-element.32, f32[512]{0:T(512)S(1)} %reduce_sum.66, f32[512]{0:T(512)S(1)} %reduce_sum.64, s32[512]{0:T(512)S(1)} %get-tuple-element.33, pred[512]{0:T(512)(128)(4,1)S(1)} %get-tuple-element.30, ...), kind=kLoop, calls=%fused_computation.6 | loop fusion | flops 2621440 | bytes 1582080 | tf_op jit(solution)/shard_map/convert_element_type | solution.py:118
  93.0 2.6 %convolution_convert_fusion.2 = bf16[512,768]{1,0:T(8,128)(2,1)} fusion(bf16[512,512]{1,0:T(8,128)(2,1)S(1)} %subtract_convert_fusion.mixing_ref, bf16[512,768]{1,0:T(8,128)(2,1)} %convolution_convert_fusion.3), kind=kOutput, calls=%fused_computation.3 | convolution fusion | flops 403046400 | bytes 2097152 | tf_op jit(solution)/shard_map/dot_general | solution.py:120
  95.7 12.2 %all-to-all-start.2 = ((bf16[32,16,768]{2,1,0:T(8,128)(2,1)}), bf16[32,16,768]{2,1,0:T(8,128)(2,1)}, u32[]{:S(2)}, u32[]{:S(2)}) async-start(bf16[32,16,768]{2,1,0:T(8,128)(2,1)} %bitcast.23), calls=%async_computation.2 | async-start | bytes 1572864 | tf_op jit(solution)/shard_map/all_to_all | solution.py:35
  107.9 1.4 copy-done.2
  109.3 2.0 %shard_map.68 = (bf16[256,768]{1,0:T(8,128)(2,1)S(1)}, bf16[256,768]{1,0:T(8,128)(2,1)}) custom-call(s32[1]{0:T(128)} %bitcast.2.core_ref, bf16[512,512]{1,0:T(8,128)(2,1)S(1)} %subtract_convert_fusion.mixing_ref, bf16[512,1024]{1,0:T(8,128)(2,1)S(1)} %convolution_convert_fusion.text_ref, bf16[768,1024]{1,0:T(8,128)(2,1)S(1)} %copy-done.2), custom_call_target="tpu_custom_call" | custom-call | flops 268435456 | bytes 1048576 | tf_op jit(solution)/shard_map/pallas_call | solution.py:69
  111.3 1.9 %collective-permute-start.1 = (bf16[256,768]{1,0:T(8,128)(2,1)}, bf16[256,768]{1,0:T(8,128)(2,1)S(1)}, u32[]{:S(2)}, u32[]{:S(2)}) collective-permute-start(bf16[256,768]{1,0:T(8,128)(2,1)} %get-tuple-element.23), channel_id=1, source_target_pairs={{0,64},{64,0},{1,65},{65,1},{2,66},{66,2},{3,67},{67,3},{4,68},{68... | collective-permute-start | bytes 1179656 | tf_op jit(solution)/shard_map/ppermute | solution.py:45
  113.2 0.9 select_reduce_fusion
  114.1 1.0 collective-permute-done.1
  115.2 3.5 %collective-permute-start.2 = (bf16[4,32,768]{2,1,0:T(8,128)(2,1)S(1)}, bf16[4,32,768]{2,1,0:T(8,128)(2,1)S(1)}, u32[]{:S(2)}, u32[]{:S(2)}) collective-permute-start(bf16[4,32,768]{2,1,0:T(8,128)(2,1)S(1)} %dynamic-slice_bitcast_fusion), channel_id=1, source_target_pairs={{0,1},{1,0},{2,3},{3,2},{4,5},{5,4},{6,7},{7,6},{8,9},{9,8},{10,11... | collective-permute-start | bytes 589832 | tf_op jit(solution)/shard_map/ppermute | solution.py:45
  118.7 0.6 multiply_subtract_fusion
  119.3 4.8 %collective-permute-done.2 = bf16[4,32,768]{2,1,0:T(8,128)(2,1)S(1)} collective-permute-done((bf16[4,32,768]{2,1,0:T(8,128)(2,1)S(1)}, bf16[4,32,768]{2,1,0:T(8,128)(2,1)S(1)}, u32[]{:S(2)}, u32[]{:S(2)}) %collective-permute-start.2) | collective-permute-done | bytes 196640 | tf_op jit(solution)/shard_map/ppermute | solution.py:45
  124.1 0.7 fusion
  124.8 8.1 %all-to-all-done.2 = bf16[32,16,768]{2,1,0:T(8,128)(2,1)} async-done(((bf16[32,16,768]{2,1,0:T(8,128)(2,1)}), bf16[32,16,768]{2,1,0:T(8,128)(2,1)}, u32[]{:S(2)}, u32[]{:S(2)}) %all-to-all-start.2) | async-done | bytes 786464 | tf_op jit(solution)/shard_map/all_to_all | solution.py:35
  132.8 6.0 %all-to-all-start.3 = ((bf16[8,16,768]{2,1,0:T(8,128)(2,1)}), bf16[8,16,768]{2,1,0:T(8,128)(2,1)S(1)}, u32[]{:S(2)}, u32[]{:S(2)}) async-start(bf16[8,16,768]{2,1,0:T(8,128)(2,1)} %bitcast.7), calls=%async_computation.3 | async-start | bytes 393216 | tf_op jit(solution)/shard_map/all_to_all | solution.py:35
  138.9 1.3 convert_reduce_fusion
  140.1 0.6 multiply_convert_fusion
  140.8 7.4 %all-to-all-done.3 = bf16[8,16,768]{2,1,0:T(8,128)(2,1)S(1)} async-done(((bf16[8,16,768]{2,1,0:T(8,128)(2,1)}), bf16[8,16,768]{2,1,0:T(8,128)(2,1)S(1)}, u32[]{:S(2)}, u32[]{:S(2)}) %all-to-all-start.3) | async-done | bytes 196640 | tf_op jit(solution)/shard_map/all_to_all | solution.py:35
  148.2 0.6 multiply_convert_fusion.1
  (19 shorter events, 0.3 us)
Async XLA Ops:
  0.6 51.5 %copy-start = (bf16[768,1024]{1,0:T(8,128)(2,1)S(1)}, bf16[768,1024]{1,0:T(8,128)(2,1)}, u32[]{:S(2)}) copy-start(bf16[768,1024]{1,0:T(8,128)(2,1)} %param.7) | copy-start | bytes 4718596
  0.6 49.5 %copy-start.1 = (bf16[768,1024]{1,0:T(8,128)(2,1)S(1)}, bf16[768,1024]{1,0:T(8,128)(2,1)}, u32[]{:S(2)}) copy-start(bf16[768,1024]{1,0:T(8,128)(2,1)} %weight_ref.1) | copy-start | bytes 4718596
  9.1 45.0 %all-to-all-start = ((bf16[32,16,768]{2,1,0:T(8,128)(2,1)}), bf16[32,16,768]{2,1,0:T(8,128)(2,1)}, u32[]{:S(2)}, u32[]{:S(2)}) async-start(bf16[32,16,768]{2,1,0:T(8,128)(2,1)} %get-tuple-element.18), calls=%async_computation | async-start | bytes 1572864 | tf_op jit(solution)/shard_map/all_to_all | solution.py:35
  51.2 1.0 copy-start.3
  54.1 2.2 %copy-start.4 = (bf16[512,1024]{1,0:T(8,128)(2,1)S(1)}, bf16[512,1024]{1,0:T(8,128)(2,1)}, u32[]{:S(2)}) copy-start(bf16[512,1024]{1,0:T(8,128)(2,1)} %copy-done.3) | copy-start | bytes 3145732
  58.8 32.4 %all-to-all-start.1 = ((f32[32,1,512]{2,1,0:T(1,128)}), f32[32,1,512]{2,1,0:T(1,128)S(1)}, u32[]{:S(2)}, u32[]{:S(2)}) async-start(f32[32,1,512]{2,1,0:T(1,128)} %all_to_all.16), calls=%async_computation.1 | async-start | bytes 131072 | tf_op jit(solution)/shard_map/all_to_all | solution.py:35
  71.0 5.5 %collective-permute-start = (f32[512]{0:T(512)S(1)}, f32[512]{0:T(512)S(1)}, u32[]{:S(2)}, u32[]{:S(2)}) collective-permute-start(f32[512]{0:T(512)S(1)} %get-tuple-element.27), channel_id=1, source_target_pairs={{0,8},{8,0},{1,9},{9,1},{2,10},{10,2},{3,11},{11,3},{4,12},{12,4},... | collective-permute-start | bytes 6152 | tf_op jit(solution)/shard_map/ppermute | solution.py:45
  95.7 37.2 %all-to-all-start.2 = ((bf16[32,16,768]{2,1,0:T(8,128)(2,1)}), bf16[32,16,768]{2,1,0:T(8,128)(2,1)}, u32[]{:S(2)}, u32[]{:S(2)}) async-start(bf16[32,16,768]{2,1,0:T(8,128)(2,1)} %bitcast.23), calls=%async_computation.2 | async-start | bytes 1572864 | tf_op jit(solution)/shard_map/all_to_all | solution.py:35
  107.8 1.4 copy-start.2
  111.3 3.8 %collective-permute-start.1 = (bf16[256,768]{1,0:T(8,128)(2,1)}, bf16[256,768]{1,0:T(8,128)(2,1)S(1)}, u32[]{:S(2)}, u32[]{:S(2)}) collective-permute-start(bf16[256,768]{1,0:T(8,128)(2,1)} %get-tuple-element.23), channel_id=1, source_target_pairs={{0,64},{64,0},{1,65},{65,1},{2,66},{66,2},{3,67},{67,3},{4,68},{68... | collective-permute-start | bytes 1179656 | tf_op jit(solution)/shard_map/ppermute | solution.py:45
  115.2 8.8 %collective-permute-start.2 = (bf16[4,32,768]{2,1,0:T(8,128)(2,1)S(1)}, bf16[4,32,768]{2,1,0:T(8,128)(2,1)S(1)}, u32[]{:S(2)}, u32[]{:S(2)}) collective-permute-start(bf16[4,32,768]{2,1,0:T(8,128)(2,1)S(1)} %dynamic-slice_bitcast_fusion), channel_id=1, source_target_pairs={{0,1},{1,0},{2,3},{3,2},{4,5},{5,4},{6,7},{7,6},{8,9},{9,8},{10,11... | collective-permute-start | bytes 589832 | tf_op jit(solution)/shard_map/ppermute | solution.py:45
  132.8 15.3 %all-to-all-start.3 = ((bf16[8,16,768]{2,1,0:T(8,128)(2,1)}), bf16[8,16,768]{2,1,0:T(8,128)(2,1)S(1)}, u32[]{:S(2)}, u32[]{:S(2)}) async-start(bf16[8,16,768]{2,1,0:T(8,128)(2,1)} %bitcast.7), calls=%async_computation.3 | async-start | bytes 393216 | tf_op jit(solution)/shard_map/all_to_all | solution.py:35

commit v6 on v5

--- a/solution.py
+++ b/solution.py
@@ -10,6 +10,7 @@
 
 score_scale = 0.1
 CODE = ("yh", "yl", "c", "zl")
+ROWS = ("c", "zl", "yh", "yl")
 TEXT = ("x", "zh")
 
 
@@ -84,6 +85,7 @@
     f32, bf16 = jnp.float32, jnp.bfloat16
     nt = (((1,), (1,)), ((), ()))
     here, _, depth = code_tokens.shape
+    core, side = lax.axis_index("c"), lax.axis_index("yl")
     code_row = lax.axis_index(CODE) * here
     text_row = lax.axis_index(TEXT) * here
 
@@ -101,9 +103,14 @@
     exps = jnp.exp(scores)
     row_part = jnp.sum(exps, axis=1)
     col_part = jnp.sum(exps, axis=0)
-    row_part = row_part + swap(row_part, "zl")
-    col_total = jnp.sum(fan_out(col_part, TEXT), axis=0)
-    row_total = jnp.sum(lax.all_gather(row_part, CODE[:3], axis=0), axis=0)
+    lanes = math.gcd(col_part.size, 128)
+    live = (scores, exps, code_back, text_proj, code_row, text_row, core, side)
+    row_part, col_part, *live = lax.optimization_barrier((row_part, col_part, *live))
+    row_parts, col_part, *live = lax.optimization_barrier((fan_out(row_part.reshape(-1, lanes), ROWS), col_part, *live))
+    row_parts, col_parts, *live = lax.optimization_barrier((row_parts, fan_out(col_part.reshape(-1, lanes), TEXT), *live))
+    scores, exps, code_back, text_proj, code_row, text_row, core, side = live
+    row_total = jnp.sum(row_parts, axis=0).reshape(-1)
+    col_total = jnp.sum(col_parts, axis=0).reshape(-1)
 
     own = jnp.eye(here, dtype=f32)
     own_scores = jnp.sum(lax.dynamic_slice(scores, (code_row, text_row), (here, here)) * own, axis=1)
@@ -123,10 +130,9 @@
     text_proj, text_parts = lax.optimization_barrier((text_proj, text_term.astype(bf16)))
     text_parts = exchange(text_parts.reshape(-1, here, depth), TEXT)
 
-    mine, theirs = code_sum(lax.axis_index("c"), mixing, text_proj, code_weight)
+    mine, theirs = code_sum(core, mixing, text_proj, code_weight)
     code_parts = (mine.astype(f32) + swap(theirs, "c").astype(f32)).astype(bf16)
     code_parts = code_parts.reshape(-1, 2, 2 * here, depth)
-    side = lax.axis_index("yl")
     mine = lax.dynamic_index_in_dim(code_parts, side, 1, keepdims=False)
     theirs = lax.dynamic_index_in_dim(code_parts, 1 - side, 1, keepdims=False)
     code_parts = (mine.astype(f32) + swap(theirs, "yl").astype(f32)).astype(bf16)

time: 150 us -> 144 us (0.960)
  starting transfers between devices: 60.2 us -> 33.9 us
  blocking collectives: 41.2 us -> 64.4 us
  waiting for transfers between devices: 22.8 us -> 20.2 us
    all_to_all x0 -> x2, blocking collectives: none -> 37.9 us  [exchange(): return lax.all_to_all(parts, axes, split_axis=0, concat_axis=0, tiled=True)]
    all_to_all x4 -> x3, starting transfers between devices: 50.9 us -> 29.2 us  [exchange(): return lax.all_to_all(parts, axes, split_axis=0, concat_axis=0, tiled=True)]
    all_gather x1 -> x0, blocking collectives: 14.6 us -> none  [shards(): row_total = jnp.sum(lax.all_gather(row_part, CODE[:3], axis=0), axis=0)]
    ppermute x3 -> x2, starting transfers between devices: 9.26 us -> 4.68 us  [swap(): return lax.ppermute(block, name, [(0, 1), (1, 0)])]
    all_to_all x4 -> x3, waiting for transfers between devices: 15.4 us -> 13.8 us  [exchange(): return lax.all_to_all(parts, axes, split_axis=0, concat_axis=0, tiled=True)]
    ppermute x3 -> x2, waiting for transfers between devices: 7.38 us -> 6.42 us  [swap(): return lax.ppermute(block, name, [(0, 1), (1, 0)])]
  transfers between devices with their start and end apart: 7 -> 5, of which waited for: 5 -> 4; matrix products, arithmetic and copies ran while one was open for 5% -> 5% of each run, Pallas kernels for 1% -> 1%
where the time goes in v6:
time: 144 us; the launch traced here: 143 us
  blocking collectives  64.4 us (45%)
  starting transfers between devices  33.9 us (24%)
  waiting for transfers between devices  20.2 us (14%)
  matrix products  9.92 us (7%)
  other arithmetic  6.68 us (5%)
  Pallas kernels  4.44 us (3%)
  local copies, waits for them, and re-layouts  2.45 us (2%)
    all_to_all x2, blocking collectives, exchange(): return lax.all_to_all(parts, axes, split_axis=0, concat_axis=0, tiled=True)  37.9 us
    all_to_all x3, starting transfers between devices, exchange(): return lax.all_to_all(parts, axes, split_axis=0, concat_axis=0, tiled=True)  29.2 us
    all_gather x1, blocking collectives, shards(): code_group = lax.all_gather(code_pair, CODE[:3], axis=0, tiled=True)  20.5 us
    all_to_all x3, waiting for transfers between devices, exchange(): return lax.all_to_all(parts, axes, split_axis=0, concat_axis=0, tiled=True)  13.8 us
    ppermute x2, waiting for transfers between devices, swap(): return lax.ppermute(block, name, [(0, 1), (1, 0)])  6.42 us
    all_gather x1, blocking collectives, shards(): code_pair = lax.all_gather(code_rows, 'zl', axis=0, tiled=True)  6 us
    ppermute x2, starting transfers between devices, swap(): return lax.ppermute(block, name, [(0, 1), (1, 0)])  4.68 us
  transfers between devices with their start and end apart: 5, of which 4 were waited for; matrix products, arithmetic and copies ran while one was open for 5% of the time, Pallas kernels for 1%

profile of v6, /device:TPU:2, one launch (start us, length us, event | category | flops | bytes accessed | tf_op | source)
XLA Modules:
  0.0 142.8 jit_solution(1271994438036017664)
XLA Ops:
  0.6 0.0 copy-start
  0.6 0.0 copy-start.1
  0.7 2.4 %shard_map.67 = (bf16[16,768]{1,0:T(8,128)(2,1)}, bf16[32,16,768]{2,1,0:T(8,128)(2,1)}) custom-call(bf16[16,16,768]{2,1,0:T(8,128)(2,1)} %code_ref.1, bf16[16,16,768]{2,1,0:T(8,128)(2,1)} %text_ref.1), custom_call_target="tpu_custom_call" | custom-call | tf_op jit(solution)/shard_map/pallas_call | solution.py:26
  3.1 6.0 %all_gather.6 = bf16[32,768]{1,0:T(8,128)(2,1)S(1)} all-gather(bf16[16,768]{1,0:T(8,128)(2,1)} %get-tuple-element.45), channel_id=1, replica_groups=mesh['x'=8,'c'=2,'zh'=4,'zl'=2,'yh'=4,'yl'=2] {'zl'}, dimensions={0}, use_global_device_ids=true | all-gather | bytes 73728 | tf_op jit(solution)/shard_map/all_gather | solution.py:93
  9.1 20.5 %all-to-all-start = ((bf16[32,16,768]{2,1,0:T(8,128)(2,1)}), bf16[32,16,768]{2,1,0:T(8,128)(2,1)}, u32[]{:S(2)}, u32[]{:S(2)}) async-start(bf16[32,16,768]{2,1,0:T(8,128)(2,1)} %get-tuple-element.48), calls=%async_computation | async-start | bytes 1572864 | tf_op jit(solution)/shard_map/all_to_all | solution.py:36
  29.6 20.5 %all_gather.7 = bf16[512,768]{1,0:T(8,128)(2,1)S(1)} all-gather(bf16[32,768]{1,0:T(8,128)(2,1)S(1)} %all_gather.6), channel_id=1, replica_groups=mesh['x'=8,'c'=2,'zh'=4,'zl'=2,'yh'=4,'yl'=2] {'yh','yl','c'}, dimensions={0}, use_global_device_ids=true | all-gather | bytes 835584 | tf_op jit(solution)/shard_map/all_gather | solution.py:96
  50.2 1.0 convolution_convert_fusion.1
  51.2 1.0 copy-done.3
  52.1 1.9 %convolution_convert_fusion.3 = bf16[512,768]{1,0:T(8,128)(2,1)} fusion(bf16[512,1024]{1,0:T(8,128)(2,1)S(1)} %convolution_convert_fusion.1, bf16[768,1024]{1,0:T(8,128)(2,1)S(1)} %copy-done), kind=kOutput, calls=%fused_computation.4 | convolution fusion | flops 805699584 | bytes 3407872 | tf_op jit(solution)/shard_map/dot_general | solution.py:99
  54.1 2.2 %convolution_convert_fusion.text_ref = bf16[512,1024]{1,0:T(8,128)(2,1)S(1)} fusion(bf16[512,768]{1,0:T(8,128)(2,1)} %bitcast, bf16[768,1024]{1,0:T(8,128)(2,1)S(1)} %copy-done), kind=kOutput, calls=%fused_computation.1 | convolution fusion | flops 805830656 | bytes 3407872 | tf_op jit(solution)/shard_map/dot_general | solution.py:101
  56.3 2.1 %exponential_reduce_fusion = (f32[512]{0:T(512)S(1)}, f32[512]{0:T(512)S(1)}, f32[512,512]{1,0:T(8,128)}, f32[512,512]{1,0:T(8,128)}) fusion(bf16[512,1024]{1,0:T(8,128)(2,1)S(1)} %copy-done.4, bf16[512,1024]{1,0:T(8,128)(2,1)S(1)} %convolution_convert_fusion.text_ref), kind=kOutput, calls=%fused_computation.21 | convolution fusion | flops 537656320 | bytes 4198400 | tf_op jit(solution)/shard_map/dot_general | solution.py:102
  58.5 16.9 %all_to_all.25 = f32[32,4,128]{2,1,0:T(4,128)S(1)} all-to-all(f32[32,4,128]{2,1,0:T(4,128)S(1)} %broadcast_in_dim.23), channel_id=1, replica_groups=mesh['x'=8,'c'=2,'zh'=4,'zl'=2,'yh'=4,'yl'=2] {'c','zl','yh','yl'}, dimensions={0} | all-to-all | bytes 131072 | tf_op jit(solution)/shard_map/all_to_all | solution.py:36
  75.4 21.0 %all_to_all.26 = f32[32,4,128]{2,1,0:T(4,128)S(1)} all-to-all(f32[32,4,128]{2,1,0:T(4,128)S(1)} %broadcast_in_dim.25), channel_id=1, replica_groups=mesh['x'=8,'c'=2,'zh'=4,'zl'=2,'yh'=4,'yl'=2] {'x','zh'}, dimensions={0} | all-to-all | bytes 131072 | tf_op jit(solution)/shard_map/all_to_all | solution.py:36
  96.5 1.7 %subtract_convert_fusion.mixing_ref = bf16[512,512]{1,0:T(8,128)(2,1)S(1)} fusion(f32[512,512]{1,0:T(8,128)} %get-tuple-element.77, s32[512]{0:T(512)S(1)} %get-tuple-element.91, f32[512]{0:T(512)S(1)} %bitcast.27, f32[512]{0:T(512)S(1)} %bitcast.29, s32[512]{0:T(512)S(1)} %get-tuple-element.92, pred[512]{0:T(512)(128)(4,1)S(1)} %get-tuple-element.93, ...), kind=kLoop, calls=%fused_computation.6 | loop fusion | flops 2621440 | bytes 1582080 | tf_op jit(solution)/shard_map/convert_element_type | solution.py:125
  98.2 2.7 %convolution_convert_fusion.2 = bf16[512,768]{1,0:T(8,128)(2,1)} fusion(bf16[512,512]{1,0:T(8,128)(2,1)S(1)} %subtract_convert_fusion.mixing_ref, bf16[512,768]{1,0:T(8,128)(2,1)} %convolution_convert_fusion.3), kind=kOutput, calls=%fused_computation.3 | convolution fusion | flops 403046400 | bytes 2097152 | tf_op jit(solution)/shard_map/dot_general | solution.py:127
  100.9 5.3 %all-to-all-start.3 = ((bf16[32,16,768]{2,1,0:T(8,128)(2,1)}), bf16[32,16,768]{2,1,0:T(8,128)(2,1)}, u32[]{:S(2)}, u32[]{:S(2)}) async-start(bf16[32,16,768]{2,1,0:T(8,128)(2,1)} %bitcast.26), calls=%async_computation.3 | async-start | bytes 1572864 | tf_op jit(solution)/shard_map/all_to_all | solution.py:36
  106.2 1.4 copy-done.2
  107.6 2.0 %shard_map.68 = (bf16[256,768]{1,0:T(8,128)(2,1)S(1)}, bf16[256,768]{1,0:T(8,128)(2,1)}) custom-call(s32[1]{0:T(128)} %bitcast.5.core_ref, bf16[512,512]{1,0:T(8,128)(2,1)S(1)} %subtract_convert_fusion.mixing_ref, bf16[512,1024]{1,0:T(8,128)(2,1)S(1)} %convolution_convert_fusion.text_ref, bf16[768,1024]{1,0:T(8,128)(2,1)S(1)} %copy-done.2), custom_call_target="tpu_custom_call" | custom-call | flops 268435456 | bytes 1048576 | tf_op jit(solution)/shard_map/pallas_call | solution.py:70
  109.6 1.9 %collective-permute-start = (bf16[256,768]{1,0:T(8,128)(2,1)}, bf16[256,768]{1,0:T(8,128)(2,1)S(1)}, u32[]{:S(2)}, u32[]{:S(2)}) collective-permute-start(bf16[256,768]{1,0:T(8,128)(2,1)} %get-tuple-element.82), channel_id=1, source_target_pairs={{0,64},{64,0},{1,65},{65,1},{2,66},{66,2},{3,67},{67,3},{4,68},{68... | collective-permute-start | bytes 1179656 | tf_op jit(solution)/shard_map/ppermute | solution.py:46
  111.5 0.9 select_reduce_fusion
  112.4 1.0 collective-permute-done
  113.4 0.1 add_convert_fusion
  113.5 2.8 %collective-permute-start.1 = (bf16[4,32,768]{2,1,0:T(8,128)(2,1)S(1)}, bf16[4,32,768]{2,1,0:T(8,128)(2,1)S(1)}, u32[]{:S(2)}, u32[]{:S(2)}) collective-permute-start(bf16[4,32,768]{2,1,0:T(8,128)(2,1)S(1)} %dynamic-slice_bitcast_fusion), channel_id=1, source_target_pairs={{0,1},{1,0},{2,3},{3,2},{4,5},{5,4},{6,7},{7,6},{8,9},{9,8},{10,11... | collective-permute-start | bytes 589832 | tf_op jit(solution)/shard_map/ppermute | solution.py:46
  116.3 0.6 multiply_subtract_fusion
  116.9 5.5 %collective-permute-done.1 = bf16[4,32,768]{2,1,0:T(8,128)(2,1)S(1)} collective-permute-done((bf16[4,32,768]{2,1,0:T(8,128)(2,1)S(1)}, bf16[4,32,768]{2,1,0:T(8,128)(2,1)S(1)}, u32[]{:S(2)}, u32[]{:S(2)}) %collective-permute-start.1) | collective-permute-done | bytes 196640 | tf_op jit(solution)/shard_map/ppermute | solution.py:46
  122.4 0.7 fusion
  123.1 6.5 %all-to-all-done.3 = bf16[32,16,768]{2,1,0:T(8,128)(2,1)} async-done(((bf16[32,16,768]{2,1,0:T(8,128)(2,1)}), bf16[32,16,768]{2,1,0:T(8,128)(2,1)}, u32[]{:S(2)}, u32[]{:S(2)}) %all-to-all-start.3) | async-done | bytes 786464 | tf_op jit(solution)/shard_map/all_to_all | solution.py:36
  129.6 3.4 %all-to-all-start.4 = ((bf16[8,16,768]{2,1,0:T(8,128)(2,1)}), bf16[8,16,768]{2,1,0:T(8,128)(2,1)S(1)}, u32[]{:S(2)}, u32[]{:S(2)}) async-start(bf16[8,16,768]{2,1,0:T(8,128)(2,1)} %bitcast.10), calls=%async_computation.4 | async-start | bytes 393216 | tf_op jit(solution)/shard_map/all_to_all | solution.py:36
  133.0 1.3 convert_reduce_fusion
  134.3 0.6 multiply_convert_fusion
  134.9 7.2 %all-to-all-done.4 = bf16[8,16,768]{2,1,0:T(8,128)(2,1)S(1)} async-done(((bf16[8,16,768]{2,1,0:T(8,128)(2,1)}), bf16[8,16,768]{2,1,0:T(8,128)(2,1)S(1)}, u32[]{:S(2)}, u32[]{:S(2)}) %all-to-all-start.4) | async-done | bytes 196640 | tf_op jit(solution)/shard_map/all_to_all | solution.py:36
  142.2 0.6 multiply_convert_fusion.1
  (15 shorter events, 0.2 us)
Async XLA Ops:
  0.6 51.5 %copy-start = (bf16[768,1024]{1,0:T(8,128)(2,1)S(1)}, bf16[768,1024]{1,0:T(8,128)(2,1)}, u32[]{:S(2)}) copy-start(bf16[768,1024]{1,0:T(8,128)(2,1)} %param.7) | copy-start | bytes 4718596
  0.6 49.5 %copy-start.1 = (bf16[768,1024]{1,0:T(8,128)(2,1)S(1)}, bf16[768,1024]{1,0:T(8,128)(2,1)}, u32[]{:S(2)}) copy-start(bf16[768,1024]{1,0:T(8,128)(2,1)} %weight_ref.1) | copy-start | bytes 4718596
  9.1 45.0 %all-to-all-start = ((bf16[32,16,768]{2,1,0:T(8,128)(2,1)}), bf16[32,16,768]{2,1,0:T(8,128)(2,1)}, u32[]{:S(2)}, u32[]{:S(2)}) async-start(bf16[32,16,768]{2,1,0:T(8,128)(2,1)} %get-tuple-element.48), calls=%async_computation | async-start | bytes 1572864 | tf_op jit(solution)/shard_map/all_to_all | solution.py:36
  51.1 1.0 copy-start.3
  54.1 2.2 %copy-start.4 = (bf16[512,1024]{1,0:T(8,128)(2,1)S(1)}, bf16[512,1024]{1,0:T(8,128)(2,1)}, u32[]{:S(2)}) copy-start(bf16[512,1024]{1,0:T(8,128)(2,1)} %copy-done.3) | copy-start | bytes 3145732
  100.9 28.8 %all-to-all-start.3 = ((bf16[32,16,768]{2,1,0:T(8,128)(2,1)}), bf16[32,16,768]{2,1,0:T(8,128)(2,1)}, u32[]{:S(2)}, u32[]{:S(2)}) async-start(bf16[32,16,768]{2,1,0:T(8,128)(2,1)} %bitcast.26), calls=%async_computation.3 | async-start | bytes 1572864 | tf_op jit(solution)/shard_map/all_to_all | solution.py:36
  106.2 1.4 copy-start.2
  109.6 3.8 %collective-permute-start = (bf16[256,768]{1,0:T(8,128)(2,1)}, bf16[256,768]{1,0:T(8,128)(2,1)S(1)}, u32[]{:S(2)}, u32[]{:S(2)}) collective-permute-start(bf16[256,768]{1,0:T(8,128)(2,1)} %get-tuple-element.82), channel_id=1, source_target_pairs={{0,64},{64,0},{1,65},{65,1},{2,66},{66,2},{3,67},{67,3},{4,68},{68... | collective-permute-start | bytes 1179656 | tf_op jit(solution)/shard_map/ppermute | solution.py:46
  113.5 8.8 %collective-permute-start.1 = (bf16[4,32,768]{2,1,0:T(8,128)(2,1)S(1)}, bf16[4,32,768]{2,1,0:T(8,128)(2,1)S(1)}, u32[]{:S(2)}, u32[]{:S(2)}) collective-permute-start(bf16[4,32,768]{2,1,0:T(8,128)(2,1)S(1)} %dynamic-slice_bitcast_fusion), channel_id=1, source_target_pairs={{0,1},{1,0},{2,3},{3,2},{4,5},{5,4},{6,7},{7,6},{8,9},{9,8},{10,11... | collective-permute-start | bytes 589832 | tf_op jit(solution)/shard_map/ppermute | solution.py:46
  129.6 12.5 %all-to-all-start.4 = ((bf16[8,16,768]{2,1,0:T(8,128)(2,1)}), bf16[8,16,768]{2,1,0:T(8,128)(2,1)S(1)}, u32[]{:S(2)}, u32[]{:S(2)}) async-start(bf16[8,16,768]{2,1,0:T(8,128)(2,1)} %bitcast.10), calls=%async_computation.4 | async-start | bytes 393216 | tf_op jit(solution)/shard_map/all_to_all | solution.py:36

commit v7 on v6

--- a/solution.py
+++ b/solution.py
@@ -40,6 +40,87 @@
     members = lax.axis_size(axes)
     spread = jnp.broadcast_to(block[None], (members,) + block.shape)
     return exchange(lax.optimization_barrier(spread), axes)
+
+
+def score_kernel(text_ref, weight_ref, code_ref, proj_ref, exps_ref, row_ref, col_ref):
+    nt = (((1,), (1,)), ((), ()))
+    lanes = row_ref.shape[2]
+    step = text_ref.shape[0] // 2
+    row_sum = jnp.zeros((code_ref.shape[0], lanes), jnp.float32)
+    for i in range(2):
+        part = jnp.dot(
+            text_ref[i * step : (i + 1) * step, :], weight_ref[...], preferred_element_type=jnp.float32
+        ).astype(jnp.bfloat16)
+        proj_ref[i * step : (i + 1) * step, :] = part
+        scores = lax.dot_general(code_ref[...], part, nt, preferred_element_type=jnp.float32)
+        exps = jnp.exp(scores * score_scale)
+        exps_ref[:, i * step : (i + 1) * step] = exps
+        col_sum = jnp.sum(exps, axis=0, keepdims=True)
+        for j in range(step // lanes):
+            row_sum += exps[:, j * lanes : (j + 1) * lanes]
+            at = i * (step // lanes) + j
+            total = jnp.broadcast_to(col_sum[:, j * lanes : (j + 1) * lanes], (col_ref.shape[0], lanes))
+            col_ref[:, at, :] = total
+    row_sum = jnp.sum(row_sum.T, axis=0, keepdims=True)
+    for j in range(row_ref.shape[1]):
+        total = jnp.broadcast_to(row_sum[:, j * lanes : (j + 1) * lanes], (row_ref.shape[0], lanes))
+        row_ref[:, j, :] = total
+
+
+def score_blocks(text_group, weight, code_proj, row_copies, col_copies):
+    f32 = jnp.float32
+    rows, width = code_proj.shape
+    cols = text_group.shape[0]
+    lanes = math.gcd(cols // 2, 128)
+    return pl.pallas_call(
+        score_kernel,
+        out_shape=(
+            jax.ShapeDtypeStruct((cols, width), jnp.bfloat16),
+            jax.ShapeDtypeStruct((rows, cols), f32),
+            jax.ShapeDtypeStruct((row_copies, rows // lanes, lanes), f32),
+            jax.ShapeDtypeStruct((col_copies, cols // lanes, lanes), f32),
+        ),
+        compiler_params=pltpu.CompilerParams(vmem_limit_bytes=40 << 20),
+    )(text_group, weight, code_proj)
+
+
+def mix_kernel(place_ref, exps_ref, row_ref, col_ref, back_ref, mixing_ref, sum_ref):
+    lanes = row_ref.shape[2]
+    here = place_ref[2]
+    row_scale = 0.5 / jnp.sum(row_ref[...], axis=0)
+    col_scale = 0.5 / jnp.sum(col_ref[...], axis=0)
+    shape = (lanes, lanes)
+    apart = lax.broadcasted_iota(jnp.int32, shape, 0) - lax.broadcasted_iota(jnp.int32, shape, 1)
+    down = lax.broadcasted_iota(jnp.int32, shape, 0)
+    for i in range(row_ref.shape[1]):
+        rows = slice(i * lanes, (i + 1) * lanes)
+        by_row = jnp.broadcast_to(row_scale[i : i + 1, :], shape).T
+        first = down + (i * lanes - place_ref[0])
+        inside = (first >= 0) & (first < here)
+        for j in range(col_ref.shape[1]):
+            cols = slice(j * lanes, (j + 1) * lanes)
+            part = exps_ref[rows, cols] * (by_row + col_scale[j : j + 1, :])
+            paired = inside & (apart == place_ref[0] - place_ref[1] + (j - i) * lanes)
+            mixing_ref[rows, cols] = (part - jnp.where(paired, 1.0, 0.0)).astype(jnp.bfloat16)
+    total = lax.dot_general(
+        mixing_ref[...], back_ref[...], (((0,), (0,)), ((), ())), preferred_element_type=jnp.float32
+    )
+    sum_ref[...] = total.astype(jnp.bfloat16)
+
+
+def mix(place, exps, row_parts, col_parts, code_back):
+    rows, cols = exps.shape
+    vmem = pl.BlockSpec(memory_space=pltpu.VMEM)
+    return pl.pallas_call(
+        mix_kernel,
+        out_shape=(
+            jax.ShapeDtypeStruct((rows, cols), jnp.bfloat16),
+            jax.ShapeDtypeStruct((cols, code_back.shape[1]), jnp.bfloat16),
+        ),
+        in_specs=[pl.BlockSpec(memory_space=pltpu.SMEM), vmem, vmem, vmem, vmem],
+        out_specs=(vmem, vmem),
+        compiler_params=pltpu.CompilerParams(vmem_limit_bytes=40 << 20),
+    )(place, exps, row_parts, col_parts, code_back)
 
 
 def swap(block, name):
@@ -98,36 +179,26 @@
     code_proj = jnp.dot(code_group, code_weight, preferred_element_type=f32).astype(bf16)
     code_back = lax.dot_general(code_proj, text_weight, nt, preferred_element_type=f32).astype(bf16)
     code_back, text_group = lax.optimization_barrier((code_back, text_group))
-    text_proj = jnp.dot(text_group, text_weight, preferred_element_type=f32).astype(bf16)
-    scores = lax.dot_general(code_proj, text_proj, nt, preferred_element_type=f32) * score_scale
-    exps = jnp.exp(scores)
-    row_part = jnp.sum(exps, axis=1)
-    col_part = jnp.sum(exps, axis=0)
-    lanes = math.gcd(col_part.size, 128)
-    live = (scores, exps, code_back, text_proj, code_row, text_row, core, side)
-    row_part, col_part, *live = lax.optimization_barrier((row_part, col_part, *live))
-    row_parts, col_part, *live = lax.optimization_barrier((fan_out(row_part.reshape(-1, lanes), ROWS), col_part, *live))
-    row_parts, col_parts, *live = lax.optimization_barrier((row_parts, fan_out(col_part.reshape(-1, lanes), TEXT), *live))
-    scores, exps, code_back, text_proj, code_row, text_row, core, side = live
+    text_proj, exps, row_parts, col_parts = score_blocks(
+        text_group, text_weight, code_proj, lax.axis_size(ROWS), lax.axis_size(TEXT)
+    )
+    live = (exps, code_proj, code_back, text_proj, code_row, text_row, core, side)
+    row_parts, col_parts, *live = lax.optimization_barrier((exchange(row_parts, ROWS), col_parts, *live))
+    row_parts, col_parts, *live = lax.optimization_barrier((row_parts, exchange(col_parts, TEXT), *live))
+    exps, code_proj, code_back, text_proj, code_row, text_row, core, side = live
     row_total = jnp.sum(row_parts, axis=0).reshape(-1)
     col_total = jnp.sum(col_parts, axis=0).reshape(-1)
 
-    own = jnp.eye(here, dtype=f32)
-    own_scores = jnp.sum(lax.dynamic_slice(scores, (code_row, text_row), (here, here)) * own, axis=1)
+    own_code = lax.dynamic_slice_in_dim(code_proj, code_row, here).astype(f32)
+    own_text = lax.dynamic_slice_in_dim(text_proj, text_row, here).astype(f32)
+    own_scores = jnp.sum(own_code * own_text, axis=1) * score_scale
     own_row_total = lax.dynamic_slice_in_dim(row_total, code_row, here)
     own_col_total = lax.dynamic_slice_in_dim(col_total, text_row, here)
     pair_loss = 0.5 * (jnp.log(own_row_total) + jnp.log(own_col_total)) - own_scores
 
-    rows = lax.broadcasted_iota(jnp.int32, scores.shape, 0) - code_row
-    cols = lax.broadcasted_iota(jnp.int32, scores.shape, 1) - text_row
-    paired = (rows == cols) & (rows >= 0) & (rows < here)
-    mixing = 0.5 * (exps / row_total[:, None] + exps / col_total[None, :])
-    mixing = (mixing - jnp.where(paired, 1.0, 0.0)).astype(bf16)
-
-    text_term = lax.dot_general(
-        mixing, code_back, (((0,), (0,)), ((), ())), preferred_element_type=f32
-    )
-    text_proj, text_parts = lax.optimization_barrier((text_proj, text_term.astype(bf16)))
+    place = jnp.stack([code_row, text_row, jnp.int32(here)])
+    mixing, text_parts = mix(place, exps, row_parts, col_parts, code_back)
+    text_proj, text_parts = lax.optimization_barrier((text_proj, text_parts))
     text_parts = exchange(text_parts.reshape(-1, here, depth), TEXT)
 
     mine, theirs = code_sum(core, mixing, text_proj, code_weight)

time: 144 us -> 144 us (level)
  blocking collectives: 64.4 us -> 48 us
  starting transfers between devices: 33.9 us -> 41.6 us
  waiting for transfers between devices: 20.2 us -> 27.3 us
  matrix products: 9.92 us -> 4.4 us
  Pallas kernels: 4.44 us -> 9.06 us
  local copies, waits for them, and re-layouts: 2.45 us -> 6.35 us
    all_to_all x2 -> x1, blocking collectives: 37.9 us -> 21.5 us  [exchange(): return lax.all_to_all(parts, axes, split_axis=0, concat_axis=0, tiled=True)]
    all_to_all x3 -> x4, starting transfers between devices: 29.2 us -> 37 us  [exchange(): return lax.all_to_all(parts, axes, split_axis=0, concat_axis=0, tiled=True)]
    all_to_all x3 -> x4, waiting for transfers between devices: 13.8 us -> 21 us  [exchange(): return lax.all_to_all(parts, axes, split_axis=0, concat_axis=0, tiled=True)]
    dot_general x3 -> x0, matrix products: 6.99 us -> none  [the longest x1 2.66 us: shards(): lax.dot_general(mixing, code_back, (((0,), (0,)), ((), ())), preferred_el...]
    pallas_call x0 -> x2, Pallas kernels: none -> 4.76 us  [the longest x1 2.39 us: score_blocks(): pl.pallas_call(score_kernel, out_shape=(jax.ShapeDtypeStruct((cols, width...]
    unnamed x10 -> x16, local copies, waits for them, and re-layouts: 2.41 us -> 6.32 us
    convert_element_type x1 -> x0, other arithmetic: 1.73 us -> none  [shards(): mixing = (mixing - jnp.where(paired, 1.0, 0.0)).astype(bf16)]
    dot_general x1, matrix products: 0.98 us -> 2.51 us  [shards(): jnp.dot(code_group, code_weight, preferred_element_type=f32).astype(bf16)]
  transfers between devices with their start and end apart: 5 -> 6, of which waited for: 4 -> 5; matrix products, arithmetic and copies ran while one was open for 5% -> 7% of each run, Pallas kernels for 1% -> 1%
where the time goes in v7:
time: 144 us
  blocking collectives  48 us (33%)
  starting transfers between devices  41.6 us (29%)
  waiting for transfers between devices  27.3 us (19%)
  Pallas kernels  9.06 us (6%)
  local copies, waits for them, and re-layouts  6.35 us (4%)
  other arithmetic  6.02 us (4%)
  matrix products  4.4 us (3%)
    all_to_all x4, starting transfers between devices, exchange(): return lax.all_to_all(parts, axes, split_axis=0, concat_axis=0, tiled=True)  37 us
    all_to_all x1, blocking collectives, exchange(): return lax.all_to_all(parts, axes, split_axis=0, concat_axis=0, tiled=True)  21.5 us
    all_to_all x4, waiting for transfers between devices, exchange(): return lax.all_to_all(parts, axes, split_axis=0, concat_axis=0, tiled=True)  21 us
    all_gather x1, blocking collectives, shards(): code_group = lax.all_gather(code_pair, CODE[:3], axis=0, tiled=True)  20.5 us
    ppermute x2, waiting for transfers between devices, swap(): return lax.ppermute(block, name, [(0, 1), (1, 0)])  6.33 us
    unnamed x16, local copies, waits for them, and re-layouts  6.32 us
    all_gather x1, blocking collectives, shards(): code_pair = lax.all_gather(code_rows, 'zl', axis=0, tiled=True)  6 us
    ppermute x2, starting transfers between devices, swap(): return lax.ppermute(block, name, [(0, 1), (1, 0)])  4.68 us
  transfers between devices with their start and end apart: 6, of which 5 were waited for; matrix products, arithmetic and copies ran while one was open for 7% of the time, Pallas kernels for 1%

profile of v7, /device:TPU:2, one launch (start us, length us, event | category | flops | bytes accessed | tf_op | source)
XLA Modules:
  0.0 143.6 jit_solution(13936910914085146768)
XLA Ops:
  0.6 2.3 %shard_map.67 = (bf16[16,768]{1,0:T(8,128)(2,1)}, bf16[32,16,768]{2,1,0:T(8,128)(2,1)}) custom-call(bf16[16,16,768]{2,1,0:T(8,128)(2,1)} %code_ref.1, bf16[16,16,768]{2,1,0:T(8,128)(2,1)} %text_ref.1), custom_call_target="tpu_custom_call" | custom-call | tf_op jit(solution)/shard_map/pallas_call | solution.py:26
  2.9 6.0 %all_gather.6 = bf16[32,768]{1,0:T(8,128)(2,1)S(1)} all-gather(bf16[16,768]{1,0:T(8,128)(2,1)} %get-tuple-element.41), channel_id=1, replica_groups=mesh['x'=8,'c'=2,'zh'=4,'zl'=2,'yh'=4,'yl'=2] {'zl'}, dimensions={0}, use_global_device_ids=true | all-gather | bytes 73728 | tf_op jit(solution)/shard_map/all_gather | solution.py:174
  8.9 20.5 %all-to-all-start = ((bf16[32,16,768]{2,1,0:T(8,128)(2,1)}), bf16[32,16,768]{2,1,0:T(8,128)(2,1)S(1)}, u32[]{:S(2)}, u32[]{:S(2)}) async-start(bf16[32,16,768]{2,1,0:T(8,128)(2,1)} %get-tuple-element.44), calls=%async_computation | async-start | bytes 1572864 | tf_op jit(solution)/shard_map/all_to_all | solution.py:36
  29.4 20.5 %all_gather.7 = bf16[512,768]{1,0:T(8,128)(2,1)S(1)} all-gather(bf16[32,768]{1,0:T(8,128)(2,1)S(1)} %all_gather.6), channel_id=1, replica_groups=mesh['x'=8,'c'=2,'zh'=4,'zl'=2,'yh'=4,'yl'=2] {'yh','yl','c'}, dimensions={0}, use_global_device_ids=true | all-gather | bytes 835584 | tf_op jit(solution)/shard_map/all_gather | solution.py:177
  49.9 2.5 %convolution_convert_fusion.code_ref = bf16[512,1024]{1,0:T(8,128)(2,1)S(1)} fusion(bf16[512,768]{1,0:T(8,128)(2,1)S(1)} %all_gather.7, bf16[768,1024]{1,0:T(8,128)(2,1)} %weight_ref.3), kind=kOutput, calls=%fused_computation.1 | convolution fusion | flops 805830656 | bytes 3407872 | tf_op jit(solution)/shard_map/dot_general | solution.py:179
  52.4 1.9 %convolution_convert_fusion.1.back_ref = bf16[512,768]{1,0:T(8,128)(2,1)} fusion(bf16[512,1024]{1,0:T(8,128)(2,1)S(1)} %convolution_convert_fusion.code_ref, bf16[768,1024]{1,0:T(8,128)(2,1)S(1)} %copy-done), kind=kOutput, calls=%fused_computation.2 | convolution fusion | flops 805699584 | bytes 3407872 | tf_op jit(solution)/shard_map/dot_general | solution.py:180
  54.3 2.4 %shard_map.68 = (bf16[512,1024]{1,0:T(8,128)(2,1)S(1)}, f32[512,512]{1,0:T(8,128)S(1)}, f32[32,4,128]{2,1,0:T(4,128)}, f32[32,4,128]{2,1,0:T(4,128)S(1)}) custom-call(bf16[512,768]{1,0:T(8,128)(2,1)S(1)} %bitcast.18, bf16[768,1024]{1,0:T(8,128)(2,1)S(1)} %copy-done, bf16[512,1024]{1,0:T(8,128)(2,1)S(1)} %convolution_convert_fusion.code_ref), custom_call_target="tpu_custom_call" | custom-call | tf_op jit(solution)/shard_map/pallas_call | solution.py:75
  56.7 1.0 copy-done.2
  57.7 1.0 copy-done.4
  58.7 7.8 %all-to-all-start.1 = ((f32[32,4,128]{2,1,0:T(4,128)}), f32[32,4,128]{2,1,0:T(4,128)S(1)}, u32[]{:S(2)}, u32[]{:S(2)}) async-start(f32[32,4,128]{2,1,0:T(4,128)} %get-tuple-element.46), calls=%async_computation.1 | async-start | bytes 131072 | tf_op jit(solution)/shard_map/all_to_all | solution.py:36
  66.6 8.8 %all-to-all-done.1.row_ref = f32[32,4,128]{2,1,0:T(4,128)S(1)} async-done(((f32[32,4,128]{2,1,0:T(4,128)}), f32[32,4,128]{2,1,0:T(4,128)S(1)}, u32[]{:S(2)}, u32[]{:S(2)}) %all-to-all-start.1) | async-done | bytes 65568 | tf_op jit(solution)/shard_map/all_to_all | solution.py:36
  75.3 21.5 %all_to_all.25.col_ref = f32[32,4,128]{2,1,0:T(4,128)S(1)} all-to-all(f32[32,4,128]{2,1,0:T(4,128)S(1)} %get-tuple-element.52), channel_id=1, replica_groups=mesh['x'=8,'c'=2,'zh'=4,'zl'=2,'yh'=4,'yl'=2] {'x','zh'}, dimensions={0} | all-to-all | bytes 131072 | tf_op jit(solution)/shard_map/all_to_all | solution.py:36
  96.9 1.2 copy-done.5
  98.1 1.1 copy-done.6
  99.3 2.4 %shard_map.69 = (bf16[512,512]{1,0:T(8,128)(2,1)S(1)}, bf16[512,768]{1,0:T(8,128)(2,1)}) custom-call(s32[3]{0:T(128)S(1)} %pad_add_fusion.place_ref, f32[512,512]{1,0:T(8,128)S(1)} %copy-done.5, f32[32,4,128]{2,1,0:T(4,128)S(1)} %all-to-all-done.1.row_ref, f32[32,4,128]{2,1,0:T(4,128)S(1)} %all_to_all.25.col_ref, bf16[512,768]{1,0:T(8,128)(2,1)S(1)} %copy-done.6), custom_call_target="tpu_custom_call" | custom-call | tf_op jit(solution)/shard_map/pallas_call | solution.py:114
  101.6 5.3 %all-to-all-start.3 = ((bf16[32,16,768]{2,1,0:T(8,128)(2,1)}), bf16[32,16,768]{2,1,0:T(8,128)(2,1)}, u32[]{:S(2)}, u32[]{:S(2)}) async-start(bf16[32,16,768]{2,1,0:T(8,128)(2,1)} %bitcast.9), calls=%async_computation.3 | async-start | bytes 1572864 | tf_op jit(solution)/shard_map/all_to_all | solution.py:36
  107.0 1.2 copy-done.3
  108.2 2.0 %shard_map.70 = (bf16[256,768]{1,0:T(8,128)(2,1)S(1)}, bf16[256,768]{1,0:T(8,128)(2,1)}) custom-call(s32[1]{0:T(128)} %bitcast.3.core_ref, bf16[512,512]{1,0:T(8,128)(2,1)S(1)} %get-tuple-element.70.mixing_ref, bf16[512,1024]{1,0:T(8,128)(2,1)S(1)} %copy-done.3, bf16[768,1024]{1,0:T(8,128)(2,1)S(1)} %copy-done.1), custom_call_target="tpu_custom_call" | custom-call | flops 268435456 | bytes 1048576 | tf_op jit(solution)/shard_map/pallas_call | solution.py:151
  110.2 0.7 copy-done.7
  111.0 1.9 %collective-permute-start = (bf16[256,768]{1,0:T(8,128)(2,1)}, bf16[256,768]{1,0:T(8,128)(2,1)S(1)}, u32[]{:S(2)}, u32[]{:S(2)}) collective-permute-start(bf16[256,768]{1,0:T(8,128)(2,1)} %get-tuple-element.74), channel_id=1, source_target_pairs={{0,64},{64,0},{1,65},{65,1},{2,66},{66,2},{3,67},{67,3},{4,68},{68... | collective-permute-start | bytes 1179656 | tf_op jit(solution)/shard_map/ppermute | solution.py:127
  113.0 0.9 multiply_reduce_fusion
  113.9 0.9 collective-permute-done
  114.8 1.1 add_convert_fusion
  115.9 2.8 %collective-permute-start.1 = (bf16[4,32,768]{2,1,0:T(8,128)(2,1)S(1)}, bf16[4,32,768]{2,1,0:T(8,128)(2,1)S(1)}, u32[]{:S(2)}, u32[]{:S(2)}) collective-permute-start(bf16[4,32,768]{2,1,0:T(8,128)(2,1)S(1)} %dynamic-slice_bitcast_fusion), channel_id=1, source_target_pairs={{0,1},{1,0},{2,3},{3,2},{4,5},{5,4},{6,7},{7,6},{8,9},{9,8},{10,11... | collective-permute-start | bytes 589832 | tf_op jit(solution)/shard_map/ppermute | solution.py:127
  119.3 5.5 %collective-permute-done.1 = bf16[4,32,768]{2,1,0:T(8,128)(2,1)S(1)} collective-permute-done((bf16[4,32,768]{2,1,0:T(8,128)(2,1)S(1)}, bf16[4,32,768]{2,1,0:T(8,128)(2,1)S(1)}, u32[]{:S(2)}, u32[]{:S(2)}) %collective-permute-start.1) | collective-permute-done | bytes 196640 | tf_op jit(solution)/shard_map/ppermute | solution.py:127
  124.7 0.7 fusion
  125.4 5.0 %all-to-all-done.3 = bf16[32,16,768]{2,1,0:T(8,128)(2,1)} async-done(((bf16[32,16,768]{2,1,0:T(8,128)(2,1)}), bf16[32,16,768]{2,1,0:T(8,128)(2,1)}, u32[]{:S(2)}, u32[]{:S(2)}) %all-to-all-start.3) | async-done | bytes 786464 | tf_op jit(solution)/shard_map/all_to_all | solution.py:36
  130.4 3.4 %all-to-all-start.4 = ((bf16[8,16,768]{2,1,0:T(8,128)(2,1)}), bf16[8,16,768]{2,1,0:T(8,128)(2,1)S(1)}, u32[]{:S(2)}, u32[]{:S(2)}) async-start(bf16[8,16,768]{2,1,0:T(8,128)(2,1)} %bitcast.10), calls=%async_computation.4 | async-start | bytes 393216 | tf_op jit(solution)/shard_map/all_to_all | solution.py:36
  133.8 1.3 convert_reduce_fusion
  135.1 0.6 multiply_convert_fusion
  135.7 7.2 %all-to-all-done.4 = bf16[8,16,768]{2,1,0:T(8,128)(2,1)S(1)} async-done(((bf16[8,16,768]{2,1,0:T(8,128)(2,1)}), bf16[8,16,768]{2,1,0:T(8,128)(2,1)S(1)}, u32[]{:S(2)}, u32[]{:S(2)}) %all-to-all-start.4) | async-done | bytes 196640 | tf_op jit(solution)/shard_map/all_to_all | solution.py:36
  142.9 0.6 multiply_convert_fusion.1
  (17 shorter events, 0.8 us)
Async XLA Ops:
  8.9 45.4 %all-to-all-start = ((bf16[32,16,768]{2,1,0:T(8,128)(2,1)}), bf16[32,16,768]{2,1,0:T(8,128)(2,1)S(1)}, u32[]{:S(2)}, u32[]{:S(2)}) async-start(bf16[32,16,768]{2,1,0:T(8,128)(2,1)} %get-tuple-element.44), calls=%async_computation | async-start | bytes 1572864 | tf_op jit(solution)/shard_map/all_to_all | solution.py:36
  49.9 2.5 %copy-start = (bf16[768,1024]{1,0:T(8,128)(2,1)S(1)}, bf16[768,1024]{1,0:T(8,128)(2,1)}, u32[]{:S(2)}) copy-start(bf16[768,1024]{1,0:T(8,128)(2,1)} %weight_ref.2) | copy-start | bytes 4718596
  56.7 1.0 copy-start.2
  57.7 1.0 copy-start.4
  58.7 16.6 %all-to-all-start.1 = ((f32[32,4,128]{2,1,0:T(4,128)}), f32[32,4,128]{2,1,0:T(4,128)S(1)}, u32[]{:S(2)}, u32[]{:S(2)}) async-start(f32[32,4,128]{2,1,0:T(4,128)} %get-tuple-element.46), calls=%async_computation.1 | async-start | bytes 131072 | tf_op jit(solution)/shard_map/all_to_all | solution.py:36
  96.9 1.2 copy-start.5
  98.1 1.1 copy-start.6
  99.3 7.7 %copy-start.1 = (bf16[768,1024]{1,0:T(8,128)(2,1)S(1)}, bf16[768,1024]{1,0:T(8,128)(2,1)}, u32[]{:S(2)}) copy-start(bf16[768,1024]{1,0:T(8,128)(2,1)} %weight_ref.3) | copy-start | bytes 4718596
  101.6 28.8 %all-to-all-start.3 = ((bf16[32,16,768]{2,1,0:T(8,128)(2,1)}), bf16[32,16,768]{2,1,0:T(8,128)(2,1)}, u32[]{:S(2)}, u32[]{:S(2)}) async-start(bf16[32,16,768]{2,1,0:T(8,128)(2,1)} %bitcast.9), calls=%async_computation.3 | async-start | bytes 1572864 | tf_op jit(solution)/shard_map/all_to_all | solution.py:36
  106.9 1.2 copy-start.3
  110.2 0.7 copy-start.7
  111.0 3.8 %collective-permute-start = (bf16[256,768]{1,0:T(8,128)(2,1)}, bf16[256,768]{1,0:T(8,128)(2,1)S(1)}, u32[]{:S(2)}, u32[]{:S(2)}) collective-permute-start(bf16[256,768]{1,0:T(8,128)(2,1)} %get-tuple-element.74), channel_id=1, source_target_pairs={{0,64},{64,0},{1,65},{65,1},{2,66},{66,2},{3,67},{67,3},{4,68},{68... | collective-permute-start | bytes 1179656 | tf_op jit(solution)/shard_map/ppermute | solution.py:127
  115.9 8.8 %collective-permute-start.1 = (bf16[4,32,768]{2,1,0:T(8,128)(2,1)S(1)}, bf16[4,32,768]{2,1,0:T(8,128)(2,1)S(1)}, u32[]{:S(2)}, u32[]{:S(2)}) collective-permute-start(bf16[4,32,768]{2,1,0:T(8,128)(2,1)S(1)} %dynamic-slice_bitcast_fusion), channel_id=1, source_target_pairs={{0,1},{1,0},{2,3},{3,2},{4,5},{5,4},{6,7},{7,6},{8,9},{9,8},{10,11... | collective-permute-start | bytes 589832 | tf_op jit(solution)/shard_map/ppermute | solution.py:127
  130.4 12.5 %all-to-all-start.4 = ((bf16[8,16,768]{2,1,0:T(8,128)(2,1)}), bf16[8,16,768]{2,1,0:T(8,128)(2,1)S(1)}, u32[]{:S(2)}, u32[]{:S(2)}) async-start(bf16[8,16,768]{2,1,0:T(8,128)(2,1)} %bitcast.10), calls=%async_computation.4 | async-start | bytes 393216 | tf_op jit(solution)/shard_map/all_to_all | solution.py:36

commit v8 on v7

--- a/solution.py
+++ b/solution.py
@@ -42,10 +42,13 @@
     return exchange(lax.optimization_barrier(spread), axes)
 
 
-def score_kernel(text_ref, weight_ref, code_ref, proj_ref, exps_ref, row_ref, col_ref):
+def score_kernel(
+    text_ref, weight_ref, code_ref, proj_out, exps_out, row_ref, col_ref, proj_ref, exps_ref, sems
+):
     nt = (((1,), (1,)), ((), ()))
     lanes = row_ref.shape[2]
     step = text_ref.shape[0] // 2
+    copies = []
     row_sum = jnp.zeros((code_ref.shape[0], lanes), jnp.float32)
     for i in range(2):
         part = jnp.dot(
@@ -55,6 +58,13 @@
         scores = lax.dot_general(code_ref[...], part, nt, preferred_element_type=jnp.float32)
         exps = jnp.exp(scores * score_scale)
         exps_ref[:, i * step : (i + 1) * step] = exps
+        half = pl.ds(i * step, step)
+        copies += [
+            pltpu.make_async_copy(proj_ref.at[half, :], proj_out.at[half, :], sems.at[2 * i]),
+            pltpu.make_async_copy(exps_ref.at[:, half], exps_out.at[:, half], sems.at[2 * i + 1]),
+        ]
+        copies[-2].start()
+        copies[-1].start()
         col_sum = jnp.sum(exps, axis=0, keepdims=True)
         for j in range(step // lanes):
             row_sum += exps[:, j * lanes : (j + 1) * lanes]
@@ -65,6 +75,8 @@
     for j in range(row_ref.shape[1]):
         total = jnp.broadcast_to(row_sum[:, j * lanes : (j + 1) * lanes], (row_ref.shape[0], lanes))
         row_ref[:, j, :] = total
+    for copy in copies:
+        copy.wait()
 
 
 def score_blocks(text_group, weight, code_proj, row_copies, col_copies):
@@ -75,23 +87,45 @@
     return pl.pallas_call(
         score_kernel,
         out_shape=(
-            jax.ShapeDtypeStruct((cols, width), jnp.bfloat16),
-            jax.ShapeDtypeStruct((rows, cols), f32),
+            pltpu.HBM((cols, width), jnp.bfloat16),
+            pltpu.HBM((rows, cols), f32),
             jax.ShapeDtypeStruct((row_copies, rows // lanes, lanes), f32),
             jax.ShapeDtypeStruct((col_copies, cols // lanes, lanes), f32),
         ),
+        out_specs=(
+            pl.BlockSpec(memory_space=pltpu.HBM),
+            pl.BlockSpec(memory_space=pltpu.HBM),
+            pl.BlockSpec(memory_space=pltpu.VMEM),
+            pl.BlockSpec(memory_space=pltpu.VMEM),
+        ),
+        scratch_shapes=[
+            pltpu.VMEM((cols, width), jnp.bfloat16),
+            pltpu.VMEM((rows, cols), f32),
+            pltpu.SemaphoreType.DMA((4,)),
+        ],
         compiler_params=pltpu.CompilerParams(vmem_limit_bytes=40 << 20),
     )(text_group, weight, code_proj)
 
 
-def mix_kernel(place_ref, exps_ref, row_ref, col_ref, back_ref, mixing_ref, sum_ref):
+def in_hbm(array):
+    return pltpu.with_memory_space_constraint(array, pltpu.HBM)
+
+
+def mix_kernel(
+    place_ref, exps_in, row_ref, col_ref, back_in, mixing_ref, sum_ref, exps_ref, back_ref, sems
+):
     lanes = row_ref.shape[2]
     here = place_ref[2]
+    fetch_exps = pltpu.make_async_copy(exps_in, exps_ref, sems.at[0])
+    fetch_back = pltpu.make_async_copy(back_in, back_ref, sems.at[1])
+    fetch_exps.start()
+    fetch_back.start()
     row_scale = 0.5 / jnp.sum(row_ref[...], axis=0)
     col_scale = 0.5 / jnp.sum(col_ref[...], axis=0)
     shape = (lanes, lanes)
     apart = lax.broadcasted_iota(jnp.int32, shape, 0) - lax.broadcasted_iota(jnp.int32, shape, 1)
     down = lax.broadcasted_iota(jnp.int32, shape, 0)
+    fetch_exps.wait()
     for i in range(row_ref.shape[1]):
         rows = slice(i * lanes, (i + 1) * lanes)
         by_row = jnp.broadcast_to(row_scale[i : i + 1, :], shape).T
@@ -102,6 +136,7 @@
             part = exps_ref[rows, cols] * (by_row + col_scale[j : j + 1, :])
             paired = inside & (apart == place_ref[0] - place_ref[1] + (j - i) * lanes)
             mixing_ref[rows, cols] = (part - jnp.where(paired, 1.0, 0.0)).astype(jnp.bfloat16)
+    fetch_back.wait()
     total = lax.dot_general(
         mixing_ref[...], back_ref[...], (((0,), (0,)), ((), ())), preferred_element_type=jnp.float32
     )
@@ -110,17 +145,22 @@
 
 def mix(place, exps, row_parts, col_parts, code_back):
     rows, cols = exps.shape
-    vmem = pl.BlockSpec(memory_space=pltpu.VMEM)
+    vmem, hbm = pl.BlockSpec(memory_space=pltpu.VMEM), pl.BlockSpec(memory_space=pltpu.HBM)
     return pl.pallas_call(
         mix_kernel,
         out_shape=(
             jax.ShapeDtypeStruct((rows, cols), jnp.bfloat16),
             jax.ShapeDtypeStruct((cols, code_back.shape[1]), jnp.bfloat16),
         ),
-        in_specs=[pl.BlockSpec(memory_space=pltpu.SMEM), vmem, vmem, vmem, vmem],
-        out_specs=(vmem, vmem),
+        in_specs=[pl.BlockSpec(memory_space=pltpu.SMEM), hbm, vmem, vmem, hbm],
+        out_specs=(pl.BlockSpec(), pl.BlockSpec()),
+        scratch_shapes=[
+            pltpu.VMEM(exps.shape, exps.dtype),
+            pltpu.VMEM(code_back.shape, code_back.dtype),
+            pltpu.SemaphoreType.DMA((2,)),
+        ],
         compiler_params=pltpu.CompilerParams(vmem_limit_bytes=40 << 20),
-    )(place, exps, row_parts, col_parts, code_back)
+    )(place, in_hbm(exps), row_parts, col_parts, in_hbm(code_back))
 
 
 def swap(block, name):
@@ -146,13 +186,13 @@
 def code_sum(core, mixing, text_proj, weight):
     rows, cols = mixing.shape
     depth = weight.shape[0]
-    vmem = pl.BlockSpec(memory_space=pltpu.VMEM)
+    whole = pl.BlockSpec()
     half = jax.ShapeDtypeStruct((rows // 2, depth), jnp.bfloat16)
     return pl.pallas_call(
         code_sum_kernel,
         out_shape=(half, half),
-        in_specs=[pl.BlockSpec(memory_space=pltpu.SMEM), vmem, vmem, vmem],
-        out_specs=(vmem, vmem),
+        in_specs=[pl.BlockSpec(memory_space=pltpu.SMEM), whole, whole, whole],
+        out_specs=(whole, whole),
         scratch_shapes=[
             pltpu.VMEM((cols, depth), jnp.bfloat16),
             pltpu.VMEM((rows // 2, cols), jnp.bfloat16),

time: 144 us -> 142 us (0.986)
  local copies, waits for them, and re-layouts: 6.35 us -> 2 us
  Pallas kernels: 9.06 us -> 11.3 us
    unnamed x16 -> x8, local copies, waits for them, and re-layouts: 6.32 us -> 1.97 us
where the time goes in v8:
time: 142 us; the launch traced here: 141 us
  blocking collectives  48.1 us (34%)
  starting transfers between devices  41.6 us (29%)
  waiting for transfers between devices  27.3 us (19%)
  Pallas kernels  11.3 us (8%)
  other arithmetic  6.03 us (4%)
  matrix products  4.41 us (3%)
  local copies, waits for them, and re-layouts  2 us (1%)
    all_to_all x4, starting transfers between devices, exchange(): return lax.all_to_all(parts, axes, split_axis=0, concat_axis=0, tiled=True)  37 us
    all_to_all x1, blocking collectives, exchange(): return lax.all_to_all(parts, axes, split_axis=0, concat_axis=0, tiled=True)  21.5 us
    all_to_all x4, waiting for transfers between devices, exchange(): return lax.all_to_all(parts, axes, split_axis=0, concat_axis=0, tiled=True)  21 us
    all_gather x1, blocking collectives, shards(): code_group = lax.all_gather(code_pair, CODE[:3], axis=0, tiled=True)  20.5 us
    ppermute x2, waiting for transfers between devices, swap(): return lax.ppermute(block, name, [(0, 1), (1, 0)])  6.34 us
    all_gather x1, blocking collectives, shards(): code_pair = lax.all_gather(code_rows, 'zl', axis=0, tiled=True)  6 us
    ppermute x2, starting transfers between devices, swap(): return lax.ppermute(block, name, [(0, 1), (1, 0)])  4.68 us
    pallas_call x1, Pallas kernels, mix(): pl.pallas_call(mix_kernel, out_shape=(jax.ShapeDtypeStruct((rows, cols),...  3.58 us
  transfers between devices with their start and end apart: 6, of which 5 were waited for; matrix products, arithmetic and copies ran while one was open for 7% of the time, Pallas kernels for 1%

profile of v8, /device:TPU:2, one launch (start us, length us, event | category | flops | bytes accessed | tf_op | source)
XLA Modules:
  0.0 141.5 jit_solution(11515672541007241459)
XLA Ops:
  0.6 2.3 %shard_map.67 = (bf16[16,768]{1,0:T(8,128)(2,1)}, bf16[32,16,768]{2,1,0:T(8,128)(2,1)}) custom-call(bf16[16,16,768]{2,1,0:T(8,128)(2,1)} %code_ref.1, bf16[16,16,768]{2,1,0:T(8,128)(2,1)} %text_ref.1), custom_call_target="tpu_custom_call" | custom-call | tf_op jit(solution)/shard_map/pallas_call | solution.py:26
  2.9 6.0 %all_gather.6 = bf16[32,768]{1,0:T(8,128)(2,1)S(1)} all-gather(bf16[16,768]{1,0:T(8,128)(2,1)} %get-tuple-element.41), channel_id=1, replica_groups=mesh['x'=8,'c'=2,'zh'=4,'zl'=2,'yh'=4,'yl'=2] {'zl'}, dimensions={0}, use_global_device_ids=true | all-gather | bytes 73728 | tf_op jit(solution)/shard_map/all_gather | solution.py:214
  8.9 20.5 %all-to-all-start = ((bf16[32,16,768]{2,1,0:T(8,128)(2,1)}), bf16[32,16,768]{2,1,0:T(8,128)(2,1)S(1)}, u32[]{:S(2)}, u32[]{:S(2)}) async-start(bf16[32,16,768]{2,1,0:T(8,128)(2,1)} %get-tuple-element.44), calls=%async_computation | async-start | bytes 1572864 | tf_op jit(solution)/shard_map/all_to_all | solution.py:36
  29.4 20.5 %all_gather.7 = bf16[512,768]{1,0:T(8,128)(2,1)S(1)} all-gather(bf16[32,768]{1,0:T(8,128)(2,1)S(1)} %all_gather.6), channel_id=1, replica_groups=mesh['x'=8,'c'=2,'zh'=4,'zl'=2,'yh'=4,'yl'=2] {'yh','yl','c'}, dimensions={0}, use_global_device_ids=true | all-gather | bytes 835584 | tf_op jit(solution)/shard_map/all_gather | solution.py:217
  49.9 2.5 %convolution_convert_fusion.code_ref = bf16[512,1024]{1,0:T(8,128)(2,1)S(1)} fusion(bf16[512,768]{1,0:T(8,128)(2,1)S(1)} %all_gather.7, bf16[768,1024]{1,0:T(8,128)(2,1)} %weight_ref.3), kind=kOutput, calls=%fused_computation.1 | convolution fusion | flops 805830656 | bytes 3407872 | tf_op jit(solution)/shard_map/dot_general | solution.py:219
  52.4 0.0 copy-done
  52.5 1.9 %convolution_convert_fusion.1.back_in = bf16[512,768]{1,0:T(8,128)(2,1)} fusion(bf16[512,1024]{1,0:T(8,128)(2,1)S(1)} %convolution_convert_fusion.code_ref, bf16[768,1024]{1,0:T(8,128)(2,1)S(1)} %copy-done), kind=kOutput, calls=%fused_computation.2 | convolution fusion | flops 805699584 | bytes 3407872 | tf_op jit(solution)/shard_map/dot_general | solution.py:220
  54.4 0.0 all-to-all-done
  54.4 3.4 %shard_map.68 = (bf16[512,1024]{1,0:T(8,128)(2,1)}, f32[512,512]{1,0:T(8,128)}, f32[32,4,128]{2,1,0:T(4,128)}, f32[32,4,128]{2,1,0:T(4,128)S(1)}) custom-call(bf16[512,768]{1,0:T(8,128)(2,1)S(1)} %bitcast.18, bf16[768,1024]{1,0:T(8,128)(2,1)S(1)} %copy-done, bf16[512,1024]{1,0:T(8,128)(2,1)S(1)} %convolution_convert_fusion.code_ref), custom_call_target="tpu_custom_call" | custom-call | tf_op jit(solution)/shard_map/pallas_call | solution.py:87
  57.8 7.8 %all-to-all-start.1 = ((f32[32,4,128]{2,1,0:T(4,128)}), f32[32,4,128]{2,1,0:T(4,128)S(1)}, u32[]{:S(2)}, u32[]{:S(2)}) async-start(f32[32,4,128]{2,1,0:T(4,128)} %get-tuple-element.46), calls=%async_computation.1 | async-start | bytes 131072 | tf_op jit(solution)/shard_map/all_to_all | solution.py:36
  65.6 8.8 %all-to-all-done.1.row_ref = f32[32,4,128]{2,1,0:T(4,128)S(1)} async-done(((f32[32,4,128]{2,1,0:T(4,128)}), f32[32,4,128]{2,1,0:T(4,128)S(1)}, u32[]{:S(2)}, u32[]{:S(2)}) %all-to-all-start.1) | async-done | bytes 65568 | tf_op jit(solution)/shard_map/all_to_all | solution.py:36
  74.4 21.5 %all_to_all.25.col_ref = f32[32,4,128]{2,1,0:T(4,128)S(1)} all-to-all(f32[32,4,128]{2,1,0:T(4,128)S(1)} %get-tuple-element.52), channel_id=1, replica_groups=mesh['x'=8,'c'=2,'zh'=4,'zl'=2,'yh'=4,'yl'=2] {'x','zh'}, dimensions={0} | all-to-all | bytes 131072 | tf_op jit(solution)/shard_map/all_to_all | solution.py:36
  95.9 0.1 pad_add_fusion.place_ref
  95.9 3.6 %shard_map.69 = (bf16[512,512]{1,0:T(8,128)(2,1)S(1)}, bf16[512,768]{1,0:T(8,128)(2,1)}) custom-call(s32[3]{0:T(128)S(1)} %pad_add_fusion.place_ref, f32[512,512]{1,0:T(8,128)} %get-tuple-element.68.exps_in, f32[32,4,128]{2,1,0:T(4,128)S(1)} %all-to-all-done.1.row_ref, f32[32,4,128]{2,1,0:T(4,128)S(1)} %all_to_all.25.col_ref, ...), custom_call_target="tpu_custom_call" | custom-call | tf_op jit(solution)/shard_map/pallas_call | solution.py:149
  99.5 5.3 %all-to-all-start.3 = ((bf16[32,16,768]{2,1,0:T(8,128)(2,1)}), bf16[32,16,768]{2,1,0:T(8,128)(2,1)}, u32[]{:S(2)}, u32[]{:S(2)}) async-start(bf16[32,16,768]{2,1,0:T(8,128)(2,1)} %bitcast.9), calls=%async_computation.3 | async-start | bytes 1572864 | tf_op jit(solution)/shard_map/all_to_all | solution.py:36
  104.9 1.2 copy-done.2
  106.1 2.0 %shard_map.70 = (bf16[256,768]{1,0:T(8,128)(2,1)S(1)}, bf16[256,768]{1,0:T(8,128)(2,1)}) custom-call(s32[1]{0:T(128)} %bitcast.3.core_ref, bf16[512,512]{1,0:T(8,128)(2,1)S(1)} %get-tuple-element.70.mixing_ref, bf16[512,1024]{1,0:T(8,128)(2,1)S(1)} %copy-done.2, bf16[768,1024]{1,0:T(8,128)(2,1)S(1)} %copy-done.1), custom_call_target="tpu_custom_call" | custom-call | flops 268435456 | bytes 1048576 | tf_op jit(solution)/shard_map/pallas_call | solution.py:191
  108.1 0.7 copy-done.3
  108.9 1.9 %collective-permute-start = (bf16[256,768]{1,0:T(8,128)(2,1)}, bf16[256,768]{1,0:T(8,128)(2,1)S(1)}, u32[]{:S(2)}, u32[]{:S(2)}) collective-permute-start(bf16[256,768]{1,0:T(8,128)(2,1)} %get-tuple-element.74), channel_id=1, source_target_pairs={{0,64},{64,0},{1,65},{65,1},{2,66},{66,2},{3,67},{67,3},{4,68},{68... | collective-permute-start | bytes 1179656 | tf_op jit(solution)/shard_map/ppermute | solution.py:167
  110.9 0.9 multiply_reduce_fusion
  111.8 0.9 collective-permute-done
  112.7 1.1 add_convert_fusion
  113.8 2.8 %collective-permute-start.1 = (bf16[4,32,768]{2,1,0:T(8,128)(2,1)S(1)}, bf16[4,32,768]{2,1,0:T(8,128)(2,1)S(1)}, u32[]{:S(2)}, u32[]{:S(2)}) collective-permute-start(bf16[4,32,768]{2,1,0:T(8,128)(2,1)S(1)} %dynamic-slice_bitcast_fusion), channel_id=1, source_target_pairs={{0,1},{1,0},{2,3},{3,2},{4,5},{5,4},{6,7},{7,6},{8,9},{9,8},{10,11... | collective-permute-start | bytes 589832 | tf_op jit(solution)/shard_map/ppermute | solution.py:167
  116.6 0.6 multiply_subtract_fusion
  117.2 5.5 %collective-permute-done.1 = bf16[4,32,768]{2,1,0:T(8,128)(2,1)S(1)} collective-permute-done((bf16[4,32,768]{2,1,0:T(8,128)(2,1)S(1)}, bf16[4,32,768]{2,1,0:T(8,128)(2,1)S(1)}, u32[]{:S(2)}, u32[]{:S(2)}) %collective-permute-start.1) | collective-permute-done | bytes 196640 | tf_op jit(solution)/shard_map/ppermute | solution.py:167
  122.7 0.7 fusion
  123.4 4.9 %all-to-all-done.3 = bf16[32,16,768]{2,1,0:T(8,128)(2,1)} async-done(((bf16[32,16,768]{2,1,0:T(8,128)(2,1)}), bf16[32,16,768]{2,1,0:T(8,128)(2,1)}, u32[]{:S(2)}, u32[]{:S(2)}) %all-to-all-start.3) | async-done | bytes 786464 | tf_op jit(solution)/shard_map/all_to_all | solution.py:36
  128.3 3.4 %all-to-all-start.4 = ((bf16[8,16,768]{2,1,0:T(8,128)(2,1)}), bf16[8,16,768]{2,1,0:T(8,128)(2,1)S(1)}, u32[]{:S(2)}, u32[]{:S(2)}) async-start(bf16[8,16,768]{2,1,0:T(8,128)(2,1)} %bitcast.10), calls=%async_computation.4 | async-start | bytes 393216 | tf_op jit(solution)/shard_map/all_to_all | solution.py:36
  131.7 1.3 convert_reduce_fusion
  133.0 0.6 multiply_convert_fusion
  133.6 7.2 %all-to-all-done.4 = bf16[8,16,768]{2,1,0:T(8,128)(2,1)S(1)} async-done(((bf16[8,16,768]{2,1,0:T(8,128)(2,1)}), bf16[8,16,768]{2,1,0:T(8,128)(2,1)S(1)}, u32[]{:S(2)}, u32[]{:S(2)}) %all-to-all-start.4) | async-done | bytes 196640 | tf_op jit(solution)/shard_map/all_to_all | solution.py:36
  140.9 0.6 multiply_convert_fusion.1
  (9 shorter events, 0.2 us)
Async XLA Ops:
  8.9 45.5 %all-to-all-start = ((bf16[32,16,768]{2,1,0:T(8,128)(2,1)}), bf16[32,16,768]{2,1,0:T(8,128)(2,1)S(1)}, u32[]{:S(2)}, u32[]{:S(2)}) async-start(bf16[32,16,768]{2,1,0:T(8,128)(2,1)} %get-tuple-element.44), calls=%async_computation | async-start | bytes 1572864 | tf_op jit(solution)/shard_map/all_to_all | solution.py:36
  49.9 2.5 %copy-start = (bf16[768,1024]{1,0:T(8,128)(2,1)S(1)}, bf16[768,1024]{1,0:T(8,128)(2,1)}, u32[]{:S(2)}) copy-start(bf16[768,1024]{1,0:T(8,128)(2,1)} %weight_ref.2) | copy-start | bytes 4718596
  57.8 16.6 %all-to-all-start.1 = ((f32[32,4,128]{2,1,0:T(4,128)}), f32[32,4,128]{2,1,0:T(4,128)S(1)}, u32[]{:S(2)}, u32[]{:S(2)}) async-start(f32[32,4,128]{2,1,0:T(4,128)} %get-tuple-element.46), calls=%async_computation.1 | async-start | bytes 131072 | tf_op jit(solution)/shard_map/all_to_all | solution.py:36
  95.9 8.9 %copy-start.1 = (bf16[768,1024]{1,0:T(8,128)(2,1)S(1)}, bf16[768,1024]{1,0:T(8,128)(2,1)}, u32[]{:S(2)}) copy-start(bf16[768,1024]{1,0:T(8,128)(2,1)} %weight_ref.3) | copy-start | bytes 4718596
  99.5 28.8 %all-to-all-start.3 = ((bf16[32,16,768]{2,1,0:T(8,128)(2,1)}), bf16[32,16,768]{2,1,0:T(8,128)(2,1)}, u32[]{:S(2)}, u32[]{:S(2)}) async-start(bf16[32,16,768]{2,1,0:T(8,128)(2,1)} %bitcast.9), calls=%async_computation.3 | async-start | bytes 1572864 | tf_op jit(solution)/shard_map/all_to_all | solution.py:36
  104.9 1.2 copy-start.2
  108.1 0.7 copy-start.3
  108.9 3.8 %collective-permute-start = (bf16[256,768]{1,0:T(8,128)(2,1)}, bf16[256,768]{1,0:T(8,128)(2,1)S(1)}, u32[]{:S(2)}, u32[]{:S(2)}) collective-permute-start(bf16[256,768]{1,0:T(8,128)(2,1)} %get-tuple-element.74), channel_id=1, source_target_pairs={{0,64},{64,0},{1,65},{65,1},{2,66},{66,2},{3,67},{67,3},{4,68},{68... | collective-permute-start | bytes 1179656 | tf_op jit(solution)/shard_map/ppermute | solution.py:167
  113.8 8.8 %collective-permute-start.1 = (bf16[4,32,768]{2,1,0:T(8,128)(2,1)S(1)}, bf16[4,32,768]{2,1,0:T(8,128)(2,1)S(1)}, u32[]{:S(2)}, u32[]{:S(2)}) collective-permute-start(bf16[4,32,768]{2,1,0:T(8,128)(2,1)S(1)} %dynamic-slice_bitcast_fusion), channel_id=1, source_target_pairs={{0,1},{1,0},{2,3},{3,2},{4,5},{5,4},{6,7},{7,6},{8,9},{9,8},{10,11... | collective-permute-start | bytes 589832 | tf_op jit(solution)/shard_map/ppermute | solution.py:167
  128.3 12.5 %all-to-all-start.4 = ((bf16[8,16,768]{2,1,0:T(8,128)(2,1)}), bf16[8,16,768]{2,1,0:T(8,128)(2,1)S(1)}, u32[]{:S(2)}, u32[]{:S(2)}) async-start(bf16[8,16,768]{2,1,0:T(8,128)(2,1)} %bitcast.10), calls=%async_computation.4 | async-start | bytes 393216 | tf_op jit(solution)/shard_map/all_to_all | solution.py:36

commit v9 on v8

--- a/solution.py
+++ b/solution.py
@@ -220,11 +220,14 @@
     code_back = lax.dot_general(code_proj, text_weight, nt, preferred_element_type=f32).astype(bf16)
     code_back, text_group = lax.optimization_barrier((code_back, text_group))
     text_proj, exps, row_parts, col_parts = score_blocks(
-        text_group, text_weight, code_proj, lax.axis_size(ROWS), lax.axis_size(TEXT)
+        text_group, text_weight, code_proj, lax.axis_size(ROWS), 1
     )
     live = (exps, code_proj, code_back, text_proj, code_row, text_row, core, side)
-    row_parts, col_parts, *live = lax.optimization_barrier((exchange(row_parts, ROWS), col_parts, *live))
-    row_parts, col_parts, *live = lax.optimization_barrier((row_parts, exchange(col_parts, TEXT), *live))
+    row_parts = exchange(row_parts, ROWS)
+    col_part = lax.psum(col_parts[0], "zh")
+    row_parts, col_part, *live = lax.optimization_barrier((row_parts, col_part, *live))
+    col_parts = fan_out(col_part, "x")
+    row_parts, col_parts, *live = lax.optimization_barrier((row_parts, col_parts, *live))
     exps, code_proj, code_back, text_proj, code_row, text_row, core, side = live
     row_total = jnp.sum(row_parts, axis=0).reshape(-1)
     col_total = jnp.sum(col_parts, axis=0).reshape(-1)

time: 142 us -> 139 us (0.979)
  waiting for transfers between devices: 27.3 us -> 16.6 us
  starting transfers between devices: 41.6 us -> 46.8 us
  blocking collectives: 48.1 us -> 50.3 us
    psum x0 -> x1, blocking collectives: none -> 10.3 us  [shards(): col_part = lax.psum(col_parts[0], 'zh')]
    all_to_all x4, waiting for transfers between devices: 21 us -> 11.1 us  [exchange(): return lax.all_to_all(parts, axes, split_axis=0, concat_axis=0, tiled=True)]
    all_to_all x1, blocking collectives: 21.5 us -> 13.4 us  [exchange(): return lax.all_to_all(parts, axes, split_axis=0, concat_axis=0, tiled=True)]
    all_to_all x4, starting transfers between devices: 37 us -> 41.2 us  [exchange(): return lax.all_to_all(parts, axes, split_axis=0, concat_axis=0, tiled=True)]
  transfers between devices with their start and end apart: 6 -> 6, of which waited for: 5 -> 4; matrix products, arithmetic and copies ran while one was open for 7% -> 7% of each run, Pallas kernels for 1% -> 1%
where the time goes in v9:
time: 139 us; the launch traced here: 138 us
  blocking collectives  50.3 us (36%)
  starting transfers between devices  46.8 us (34%)
  waiting for transfers between devices  16.6 us (12%)
  Pallas kernels  11.3 us (8%)
  other arithmetic  6 us (4%)
  matrix products  4.43 us (3%)
  local copies, waits for them, and re-layouts  2 us (1%)
    all_to_all x4, starting transfers between devices, exchange(): return lax.all_to_all(parts, axes, split_axis=0, concat_axis=0, tiled=True)  41.2 us
    all_gather x1, blocking collectives, shards(): code_group = lax.all_gather(code_pair, CODE[:3], axis=0, tiled=True)  20.5 us
    all_to_all x1, blocking collectives, exchange(): return lax.all_to_all(parts, axes, split_axis=0, concat_axis=0, tiled=True)  13.4 us
    all_to_all x4, waiting for transfers between devices, exchange(): return lax.all_to_all(parts, axes, split_axis=0, concat_axis=0, tiled=True)  11.1 us
    psum x1, blocking collectives, shards(): col_part = lax.psum(col_parts[0], 'zh')  10.3 us
    all_gather x1, blocking collectives, shards(): code_pair = lax.all_gather(code_rows, 'zl', axis=0, tiled=True)  6 us
    ppermute x2, starting transfers between devices, swap(): return lax.ppermute(block, name, [(0, 1), (1, 0)])  5.61 us
    ppermute x2, waiting for transfers between devices, swap(): return lax.ppermute(block, name, [(0, 1), (1, 0)])  5.49 us
  transfers between devices with their start and end apart: 6, of which 4 were waited for; matrix products, arithmetic and copies ran while one was open for 7% of the time, Pallas kernels for 1%

profile of v9, /device:TPU:2, one launch (start us, length us, event | category | flops | bytes accessed | tf_op | source)
XLA Modules:
  0.0 138.1 jit_solution(6853500538019888443)
XLA Ops:
  0.6 2.3 %shard_map.67 = (bf16[16,768]{1,0:T(8,128)(2,1)}, bf16[32,16,768]{2,1,0:T(8,128)(2,1)}) custom-call(bf16[16,16,768]{2,1,0:T(8,128)(2,1)} %code_ref.1, bf16[16,16,768]{2,1,0:T(8,128)(2,1)} %text_ref.1), custom_call_target="tpu_custom_call" | custom-call | tf_op jit(solution)/shard_map/pallas_call | solution.py:26
  2.9 6.0 %all_gather.6 = bf16[32,768]{1,0:T(8,128)(2,1)S(1)} all-gather(bf16[16,768]{1,0:T(8,128)(2,1)} %get-tuple-element.41), channel_id=1, replica_groups=mesh['x'=8,'c'=2,'zh'=4,'zl'=2,'yh'=4,'yl'=2] {'zl'}, dimensions={0}, use_global_device_ids=true | all-gather | bytes 73728 | tf_op jit(solution)/shard_map/all_gather | solution.py:214
  8.9 20.5 %all-to-all-start = ((bf16[32,16,768]{2,1,0:T(8,128)(2,1)}), bf16[32,16,768]{2,1,0:T(8,128)(2,1)S(1)}, u32[]{:S(2)}, u32[]{:S(2)}) async-start(bf16[32,16,768]{2,1,0:T(8,128)(2,1)} %get-tuple-element.44), calls=%async_computation | async-start | bytes 1572864 | tf_op jit(solution)/shard_map/all_to_all | solution.py:36
  29.4 20.5 %all_gather.7 = bf16[512,768]{1,0:T(8,128)(2,1)S(1)} all-gather(bf16[32,768]{1,0:T(8,128)(2,1)S(1)} %all_gather.6), channel_id=1, replica_groups=mesh['x'=8,'c'=2,'zh'=4,'zl'=2,'yh'=4,'yl'=2] {'yh','yl','c'}, dimensions={0}, use_global_device_ids=true | all-gather | bytes 835584 | tf_op jit(solution)/shard_map/all_gather | solution.py:217
  49.9 2.5 %convolution_convert_fusion.code_ref = bf16[512,1024]{1,0:T(8,128)(2,1)S(1)} fusion(bf16[512,768]{1,0:T(8,128)(2,1)S(1)} %all_gather.7, bf16[768,1024]{1,0:T(8,128)(2,1)} %weight_ref.3), kind=kOutput, calls=%fused_computation.1 | convolution fusion | flops 805830656 | bytes 3407872 | tf_op jit(solution)/shard_map/dot_general | solution.py:219
  52.5 1.9 %convolution_convert_fusion.1.back_in = bf16[512,768]{1,0:T(8,128)(2,1)} fusion(bf16[512,1024]{1,0:T(8,128)(2,1)S(1)} %convolution_convert_fusion.code_ref, bf16[768,1024]{1,0:T(8,128)(2,1)S(1)} %copy-done), kind=kOutput, calls=%fused_computation.2 | convolution fusion | flops 805699584 | bytes 3407872 | tf_op jit(solution)/shard_map/dot_general | solution.py:220
  54.4 0.0 all-to-all-done
  54.4 3.4 %shard_map.68 = (bf16[512,1024]{1,0:T(8,128)(2,1)}, f32[512,512]{1,0:T(8,128)}, f32[32,4,128]{2,1,0:T(4,128)}, f32[1,4,128]{2,1,0:T(4,128)S(1)}) custom-call(bf16[512,768]{1,0:T(8,128)(2,1)S(1)} %bitcast.19, bf16[768,1024]{1,0:T(8,128)(2,1)S(1)} %copy-done, bf16[512,1024]{1,0:T(8,128)(2,1)S(1)} %convolution_convert_fusion.code_ref), custom_call_target="tpu_custom_call" | custom-call | tf_op jit(solution)/shard_map/pallas_call | solution.py:87
  57.8 7.8 %all-to-all-start.1 = ((f32[32,4,128]{2,1,0:T(4,128)}), f32[32,4,128]{2,1,0:T(4,128)S(1)}, u32[]{:S(2)}, u32[]{:S(2)}) async-start(f32[32,4,128]{2,1,0:T(4,128)} %get-tuple-element.46), calls=%async_computation.1 | async-start | bytes 131072 | tf_op jit(solution)/shard_map/all_to_all | solution.py:36
  65.6 10.3 %psum.7 = f32[4,128]{1,0:T(4,128)S(1)} all-reduce(f32[4,128]{1,0:T(4,128)S(1)} %bitcast.20), channel_id=1, replica_groups=mesh['x'=8,'c'=2,'zh'=4,'zl'=2,'yh'=4,'yl'=2] {'zh'}, use_global_device_ids=true, to_apply=%region_0.0 | all-reduce | flops 512 | bytes 4096 | tf_op jit(solution)/shard_map/psum | solution.py:227
  75.9 0.0 all-to-all-done.1.row_ref
  75.9 13.4 %all_to_all.25.col_ref = f32[8,4,128]{2,1,0:T(4,128)S(1)} all-to-all(f32[8,4,128]{2,1,0:T(4,128)S(1)} %broadcast_in_dim.2), channel_id=1, replica_groups=mesh['x'=8,'c'=2,'zh'=4,'zl'=2,'yh'=4,'yl'=2] {'x'}, dimensions={0} | all-to-all | bytes 32768 | tf_op jit(solution)/shard_map/all_to_all | solution.py:36
  89.3 0.1 pad_add_fusion.place_ref
  89.4 3.6 %shard_map.69 = (bf16[512,512]{1,0:T(8,128)(2,1)S(1)}, bf16[512,768]{1,0:T(8,128)(2,1)}) custom-call(s32[3]{0:T(128)S(1)} %pad_add_fusion.place_ref, f32[512,512]{1,0:T(8,128)} %get-tuple-element.68.exps_in, f32[32,4,128]{2,1,0:T(4,128)S(1)} %all-to-all-done.1.row_ref, f32[8,4,128]{2,1,0:T(4,128)S(1)} %all_to_all.25.col_ref, ...), custom_call_target="tpu_custom_call" | custom-call | tf_op jit(solution)/shard_map/pallas_call | solution.py:149
  93.0 5.7 %all-to-all-start.3 = ((bf16[32,16,768]{2,1,0:T(8,128)(2,1)}), bf16[32,16,768]{2,1,0:T(8,128)(2,1)}, u32[]{:S(2)}, u32[]{:S(2)}) async-start(bf16[32,16,768]{2,1,0:T(8,128)(2,1)} %bitcast.10), calls=%async_computation.3 | async-start | bytes 1572864 | tf_op jit(solution)/shard_map/all_to_all | solution.py:36
  98.7 1.2 copy-done.2
  99.9 2.0 %shard_map.70 = (bf16[256,768]{1,0:T(8,128)(2,1)S(1)}, bf16[256,768]{1,0:T(8,128)(2,1)}) custom-call(s32[1]{0:T(128)} %bitcast.4.core_ref, bf16[512,512]{1,0:T(8,128)(2,1)S(1)} %get-tuple-element.70.mixing_ref, bf16[512,1024]{1,0:T(8,128)(2,1)S(1)} %copy-done.2, bf16[768,1024]{1,0:T(8,128)(2,1)S(1)} %copy-done.1), custom_call_target="tpu_custom_call" | custom-call | flops 268435456 | bytes 1048576 | tf_op jit(solution)/shard_map/pallas_call | solution.py:191
  101.9 0.7 copy-done.3
  102.7 1.9 %collective-permute-start = (bf16[256,768]{1,0:T(8,128)(2,1)}, bf16[256,768]{1,0:T(8,128)(2,1)S(1)}, u32[]{:S(2)}, u32[]{:S(2)}) collective-permute-start(bf16[256,768]{1,0:T(8,128)(2,1)} %get-tuple-element.74), channel_id=1, source_target_pairs={{0,64},{64,0},{1,65},{65,1},{2,66},{66,2},{3,67},{67,3},{4,68},{68... | collective-permute-start | bytes 1179656 | tf_op jit(solution)/shard_map/ppermute | solution.py:167
  104.7 0.9 multiply_reduce_fusion
  105.6 0.9 collective-permute-done
  106.5 1.1 add_convert_fusion
  107.6 3.7 %collective-permute-start.1 = (bf16[4,32,768]{2,1,0:T(8,128)(2,1)S(1)}, bf16[4,32,768]{2,1,0:T(8,128)(2,1)S(1)}, u32[]{:S(2)}, u32[]{:S(2)}) collective-permute-start(bf16[4,32,768]{2,1,0:T(8,128)(2,1)S(1)} %dynamic-slice_bitcast_fusion), channel_id=1, source_target_pairs={{0,1},{1,0},{2,3},{3,2},{4,5},{5,4},{6,7},{7,6},{8,9},{9,8},{10,11... | collective-permute-start | bytes 589832 | tf_op jit(solution)/shard_map/ppermute | solution.py:167
  111.3 0.6 multiply_subtract_fusion
  111.9 4.6 %collective-permute-done.1 = bf16[4,32,768]{2,1,0:T(8,128)(2,1)S(1)} collective-permute-done((bf16[4,32,768]{2,1,0:T(8,128)(2,1)S(1)}, bf16[4,32,768]{2,1,0:T(8,128)(2,1)S(1)}, u32[]{:S(2)}, u32[]{:S(2)}) %collective-permute-start.1) | collective-permute-done | bytes 196640 | tf_op jit(solution)/shard_map/ppermute | solution.py:167
  116.5 0.7 fusion
  117.2 4.1 %all-to-all-done.3 = bf16[32,16,768]{2,1,0:T(8,128)(2,1)} async-done(((bf16[32,16,768]{2,1,0:T(8,128)(2,1)}), bf16[32,16,768]{2,1,0:T(8,128)(2,1)}, u32[]{:S(2)}, u32[]{:S(2)}) %all-to-all-start.3) | async-done | bytes 786464 | tf_op jit(solution)/shard_map/all_to_all | solution.py:36
  121.3 7.3 %all-to-all-start.4 = ((bf16[8,16,768]{2,1,0:T(8,128)(2,1)}), bf16[8,16,768]{2,1,0:T(8,128)(2,1)S(1)}, u32[]{:S(2)}, u32[]{:S(2)}) async-start(bf16[8,16,768]{2,1,0:T(8,128)(2,1)} %bitcast.11), calls=%async_computation.4 | async-start | bytes 393216 | tf_op jit(solution)/shard_map/all_to_all | solution.py:36
  128.6 1.3 convert_reduce_fusion
  129.8 0.6 multiply_convert_fusion
  130.4 7.0 %all-to-all-done.4 = bf16[8,16,768]{2,1,0:T(8,128)(2,1)S(1)} async-done(((bf16[8,16,768]{2,1,0:T(8,128)(2,1)}), bf16[8,16,768]{2,1,0:T(8,128)(2,1)S(1)}, u32[]{:S(2)}, u32[]{:S(2)}) %all-to-all-start.4) | async-done | bytes 196640 | tf_op jit(solution)/shard_map/all_to_all | solution.py:36
  137.5 0.6 multiply_convert_fusion.1
  (11 shorter events, 0.1 us)
Async XLA Ops:
  8.9 45.5 %all-to-all-start = ((bf16[32,16,768]{2,1,0:T(8,128)(2,1)}), bf16[32,16,768]{2,1,0:T(8,128)(2,1)S(1)}, u32[]{:S(2)}, u32[]{:S(2)}) async-start(bf16[32,16,768]{2,1,0:T(8,128)(2,1)} %get-tuple-element.44), calls=%async_computation | async-start | bytes 1572864 | tf_op jit(solution)/shard_map/all_to_all | solution.py:36
  49.9 2.5 %copy-start = (bf16[768,1024]{1,0:T(8,128)(2,1)S(1)}, bf16[768,1024]{1,0:T(8,128)(2,1)}, u32[]{:S(2)}) copy-start(bf16[768,1024]{1,0:T(8,128)(2,1)} %weight_ref.2) | copy-start | bytes 4718596
  57.8 18.1 %all-to-all-start.1 = ((f32[32,4,128]{2,1,0:T(4,128)}), f32[32,4,128]{2,1,0:T(4,128)S(1)}, u32[]{:S(2)}, u32[]{:S(2)}) async-start(f32[32,4,128]{2,1,0:T(4,128)} %get-tuple-element.46), calls=%async_computation.1 | async-start | bytes 131072 | tf_op jit(solution)/shard_map/all_to_all | solution.py:36
  89.4 9.3 %copy-start.1 = (bf16[768,1024]{1,0:T(8,128)(2,1)S(1)}, bf16[768,1024]{1,0:T(8,128)(2,1)}, u32[]{:S(2)}) copy-start(bf16[768,1024]{1,0:T(8,128)(2,1)} %weight_ref.3) | copy-start | bytes 4718596
  93.0 28.3 %all-to-all-start.3 = ((bf16[32,16,768]{2,1,0:T(8,128)(2,1)}), bf16[32,16,768]{2,1,0:T(8,128)(2,1)}, u32[]{:S(2)}, u32[]{:S(2)}) async-start(bf16[32,16,768]{2,1,0:T(8,128)(2,1)} %bitcast.10), calls=%async_computation.3 | async-start | bytes 1572864 | tf_op jit(solution)/shard_map/all_to_all | solution.py:36
  98.7 1.2 copy-start.2
  101.9 0.7 copy-start.3
  102.7 3.8 %collective-permute-start = (bf16[256,768]{1,0:T(8,128)(2,1)}, bf16[256,768]{1,0:T(8,128)(2,1)S(1)}, u32[]{:S(2)}, u32[]{:S(2)}) collective-permute-start(bf16[256,768]{1,0:T(8,128)(2,1)} %get-tuple-element.74), channel_id=1, source_target_pairs={{0,64},{64,0},{1,65},{65,1},{2,66},{66,2},{3,67},{67,3},{4,68},{68... | collective-permute-start | bytes 1179656 | tf_op jit(solution)/shard_map/ppermute | solution.py:167
  107.6 8.9 %collective-permute-start.1 = (bf16[4,32,768]{2,1,0:T(8,128)(2,1)S(1)}, bf16[4,32,768]{2,1,0:T(8,128)(2,1)S(1)}, u32[]{:S(2)}, u32[]{:S(2)}) collective-permute-start(bf16[4,32,768]{2,1,0:T(8,128)(2,1)S(1)} %dynamic-slice_bitcast_fusion), channel_id=1, source_target_pairs={{0,1},{1,0},{2,3},{3,2},{4,5},{5,4},{6,7},{7,6},{8,9},{9,8},{10,11... | collective-permute-start | bytes 589832 | tf_op jit(solution)/shard_map/ppermute | solution.py:167
  121.3 16.1 %all-to-all-start.4 = ((bf16[8,16,768]{2,1,0:T(8,128)(2,1)}), bf16[8,16,768]{2,1,0:T(8,128)(2,1)S(1)}, u32[]{:S(2)}, u32[]{:S(2)}) async-start(bf16[8,16,768]{2,1,0:T(8,128)(2,1)} %bitcast.11), calls=%async_computation.4 | async-start | bytes 393216 | tf_op jit(solution)/shard_map/all_to_all | solution.py:36
